TPU v7x, 256 devices: a whole 4x4x8 slice. The times are simulated.
256 devices in a mesh: prow: 8 (over x, core), pcol: 32 (over z, y).
Axes of the slice: x: 4, y: 4, z: 8, core: 2. Of those that a mesh axis runs over, the one named last changes fastest.
Arguments:
- rhs: float32 [64, 65536], P(None, 'pcol'), may hold values from -6 to 6
- pivots: int32 [65536], P('pcol'), may hold values from 0 to 65535, as said below
- tile_of: int32 [256], replicated, may hold values from 0 to 255, as said below
- upper_rows: bfloat16 [3, 2048, 65536], P(None, 'prow', 'pcol'), may hold values from -0.125 to 0.125
- upper_inv: bfloat16 [3, 2048, 2048], P(None, 'pcol', 'prow'), may hold values from -0.125 to 0.125
- lower_rows: bfloat16 [3, 2048, 65536], P(None, 'prow', 'pcol'), may hold values from -0.125 to 0.125
- lower_inv: bfloat16 [3, 2048, 2048], P(None, 'prow', 'pcol'), may hold values from -0.125 to 0.125
- solved: float32 [64, 65536], P(None, 'pcol'), may hold values from -6 to 6
Outputs:
- forward: float32 [64, 65536], P(None, 'pcol')
- backward: float32 [64, 65536], P(None, 'pcol')
Inputs may be any that keep to these rules, and one draw needn't show every extreme that they name: pivots[p] lies in the same tile of 256 storage columns as p, and each column of a tile appears once. `tile_of`: storage tile d * 256 / 32 + l holds global tile l * 32 + c(d), c a permutation of the process columns.
All inputs are finite; a program needn't handle non-finite values.
Results may differ from a plain program's by a relative error of at most 0.015.
Values may be sent and summed in bfloat16 or wider, within the bound.
No kernel may reach another device: no remote copies, remote signals or barrier semaphores. Data moves between devices by JAX's collectives and lax.ppermute only.
A program may use at most 64 MiB of HBM per device.

v0:
```python
import jax
import jax.numpy as jnp
from jax import lax
from jax.sharding import PartitionSpec as P

NB = 2048
TILE = 256
STEPS = 3


def body(rhs, pivots, tile_of, upper_rows, upper_inv, lower_rows, lower_inv, solved):
    pcol_index = lax.axis_index("pcol")
    prow_index = lax.axis_index("prow")
    width_here = rhs.shape[1]
    tiles_here = width_here // TILE
    tiles_block = NB // TILE
    prow_rows = upper_rows.shape[1]
    count = rhs.shape[0]
    my_tiles = lax.dynamic_slice_in_dim(tile_of, pcol_index * tiles_here, tiles_here)
    my_blocks = my_tiles // tiles_block
    cell_blocks = jnp.repeat(my_blocks, TILE)

    def locate(step):
        match = my_blocks == step
        holds = jnp.any(match)
        tile_slot = jnp.argmax(match)
        block_place = my_tiles[tile_slot] % tiles_block
        return (holds, tile_slot, block_place)

    def write_block(field, block_full, step):
        holds, tile_slot, block_place = locate(step)
        piece = lax.dynamic_slice_in_dim(block_full, block_place * TILE, TILE, 1).astype(
            jnp.float32
        )
        written = lax.dynamic_update_slice_in_dim(field, piece, tile_slot * TILE, 1)
        return jnp.where(holds, written, field)

    state = jnp.take(rhs, pivots - pcol_index * width_here, axis=1)
    finished = []
    for step in range(STEPS):
        holds, tile_slot, block_place = locate(step)
        piece = lax.dynamic_slice_in_dim(state, tile_slot * TILE, TILE, 1)
        piece = jnp.where(holds, piece, 0.0)
        buffer = jnp.zeros((count, NB), jnp.float32)
        buffer = lax.dynamic_update_slice_in_dim(buffer, piece, block_place * TILE, 1)
        block_part = lax.psum_scatter(
            buffer.astype(jnp.bfloat16), "pcol", scatter_dimension=1, tiled=True
        )
        inverse_part = jnp.dot(block_part, upper_inv[step], preferred_element_type=jnp.float32)
        block_rows = lax.psum(inverse_part, "pcol").astype(jnp.bfloat16)
        block_full = lax.all_gather(block_rows, "prow", axis=1, tiled=True)
        update = jnp.dot(block_rows, upper_rows[step], preferred_element_type=jnp.float32)
        total = lax.psum(update, "prow")
        state = state - jnp.where(cell_blocks > step, total, 0.0)
        state = write_block(state, block_full, step)
        finished.append(block_full)
    solution = solved
    for step in reversed(range(STEPS)):
        known = jnp.where(cell_blocks > step, solution, 0.0).astype(jnp.bfloat16)
        partial_value = lax.dot_general(
            known, lower_rows[step], (((1,), (1,)), ((), ())), preferred_element_type=jnp.float32
        )
        sums = lax.psum(partial_value, "pcol")
        own_rows = lax.dynamic_slice_in_dim(
            finished[step], prow_index * prow_rows, prow_rows, 1
        ).astype(jnp.float32)
        resid = (own_rows - sums).astype(jnp.bfloat16)
        inverse_part = jnp.dot(resid, lower_inv[step], preferred_element_type=jnp.float32)
        new_cols = lax.psum(inverse_part, "prow").astype(jnp.bfloat16)
        new_block = lax.all_gather(new_cols, "pcol", axis=1, tiled=True)
        solution = write_block(solution, new_block, step)
    return (state, solution)


def solution(mesh):
    return jax.shard_map(
        body,
        mesh=mesh,
        in_specs=(
            P(None, "pcol"),
            P("pcol"),
            P(),
            P(None, "prow", "pcol"),
            P(None, "pcol", "prow"),
            P(None, "prow", "pcol"),
            P(None, "prow", "pcol"),
            P(None, "pcol"),
        ),
        out_specs=(P(None, "pcol"), P(None, "pcol")),
        check_vma=False,
    )
```

profile of v0, /device:TPU:1, one launch (start us, length us, event | category | flops | bytes accessed | tf_op | source)
XLA Modules:
  0.0 1748.7 jit_solution(12627563569382211011)
XLA Ops:
  24.7 5.5 gather_fusion
  32.3 211.6 %reduce-scatter.10.cloned.1.call-done = bf16[64,64]{1,0:T(8,128)(2,1)} async-done(((bf16[2048,64]{1,0:T(8,128)(2,1)}), bf16[64,64]{1,0:T(8,128)(2,1)}) %reduce-scatter.10.cloned.1.call-update) | async-done | bytes 8208
  244.8 112.4 %psum.84 = bf16[64,256]{1,0:T(8,128)(2,1)S(1)} all-reduce(f32[64,256]{1,0:T(8,128)S(1)} %fusion.34), channel_id=1, replica_groups=mesh['prow'=8,'pcol'=32] {'pcol'}, use_global_device_ids=true, to_apply=%region_3.4 | all-reduce | flops 16384 | bytes 98304 | tf_op jit(solution)/shard_map/psum | solution.py:50
  357.2 2.3 fusion.10
  362.2 46.7 %all_gather.18 = bf16[64,2048]{1,0:T(8,128)(2,1)S(1)} all-gather(bf16[64,256]{1,0:T(8,128)(2,1)S(1)} %psum.84), channel_id=1, replica_groups=mesh['prow'=8,'pcol'=32] {'prow'}, dimensions={1}, use_global_device_ids=true | all-gather | bytes 294912 | tf_op jit(solution)/shard_map/all_gather | solution.py:51
  408.9 45.0 %all-reduce.7.cloned.1.call-done = f32[64,2048]{1,0:T(8,128)} async-done(((f32[64,2048]{1,0:T(8,128)}), f32[64,2048]{1,0:T(8,128)}) %all-reduce.7.cloned.1.call-update) | async-done | bytes 524304 | tf_op jit(solution)/shard_map/psum | solution.py:53
  457.6 209.8 %reduce-scatter.12.cloned.1.call-done = bf16[64,64]{1,0:T(8,128)(2,1)} async-done(((bf16[2048,64]{1,0:T(8,128)(2,1)}), bf16[64,64]{1,0:T(8,128)(2,1)}) %reduce-scatter.12.cloned.1.call-update) | async-done | bytes 8208
  668.3 112.4 %psum.86 = bf16[64,256]{1,0:T(8,128)(2,1)S(1)} all-reduce(f32[64,256]{1,0:T(8,128)S(1)} %fusion.32), channel_id=1, replica_groups=mesh['prow'=8,'pcol'=32] {'pcol'}, use_global_device_ids=true, to_apply=%region_8.9 | all-reduce | flops 16384 | bytes 98304 | tf_op jit(solution)/shard_map/psum | solution.py:50
  780.7 2.3 fusion.8
  785.6 46.7 %all_gather.19 = bf16[64,2048]{1,0:T(8,128)(2,1)S(1)} all-gather(bf16[64,256]{1,0:T(8,128)(2,1)S(1)} %psum.86), channel_id=1, replica_groups=mesh['prow'=8,'pcol'=32] {'prow'}, dimensions={1}, use_global_device_ids=true | all-gather | bytes 294912 | tf_op jit(solution)/shard_map/all_gather | solution.py:51
  832.3 45.2 %all-reduce.9.cloned.1.call-done = f32[64,2048]{1,0:T(8,128)} async-done(((f32[64,2048]{1,0:T(8,128)}), f32[64,2048]{1,0:T(8,128)}) %all-reduce.9.cloned.1.call-update) | async-done | bytes 524304 | tf_op jit(solution)/shard_map/psum | solution.py:53
  883.5 207.2 %reduce-scatter.14.cloned.1.call-done = bf16[64,64]{1,0:T(8,128)(2,1)} async-done(((bf16[2048,64]{1,0:T(8,128)(2,1)}), bf16[64,64]{1,0:T(8,128)(2,1)}) %reduce-scatter.14.cloned.1.call-update) | async-done | bytes 8208
  1091.6 112.6 %psum.88 = bf16[64,256]{1,0:T(8,128)(2,1)S(1)} all-reduce(f32[64,256]{1,0:T(8,128)S(1)} %fusion.30), channel_id=1, replica_groups=mesh['prow'=8,'pcol'=32] {'pcol'}, use_global_device_ids=true, to_apply=%region_13.14 | all-reduce | flops 16384 | bytes 98304 | tf_op jit(solution)/shard_map/psum | solution.py:50
  1204.2 46.7 %all_gather.20 = bf16[64,2048]{1,0:T(8,128)(2,1)S(1)} all-gather(bf16[64,256]{1,0:T(8,128)(2,1)S(1)} %psum.88), channel_id=1, replica_groups=mesh['prow'=8,'pcol'=32] {'prow'}, dimensions={1}, use_global_device_ids=true | all-gather | bytes 294912 | tf_op jit(solution)/shard_map/all_gather | solution.py:51
  1251.9 22.4 %psum.91 = bf16[64,64]{1,0:T(8,128)(2,1)S(1)} all-reduce(f32[64,64]{1,0:T(8,128)S(1)} %fusion.24), channel_id=1, replica_groups=mesh['prow'=8,'pcol'=32] {'prow'}, use_global_device_ids=true, to_apply=%region_16.17 | all-reduce | flops 4096 | bytes 24576 | tf_op jit(solution)/shard_map/psum | solution.py:69
  1274.4 34.9 %all_gather.21 = bf16[64,2048]{0,1:T(8,128)(2,1)S(1)} all-gather(bf16[64,64]{0,1:T(8,128)(2,1)S(1)} %copy.14), channel_id=1, replica_groups=mesh['prow'=8,'pcol'=32] {'pcol'}, dimensions={1}, use_global_device_ids=true | all-gather | bytes 270336 | tf_op jit(solution)/shard_map/all_gather | solution.py:70
  1312.4 146.9 %all-reduce.15.cloned.1.call-done = f32[64,256]{1,0:T(8,128)} async-done(((f32[64,256]{1,0:T(8,128)}), f32[64,256]{1,0:T(8,128)}) %all-reduce.15.cloned.1.call-update) | async-done | bytes 65552 | tf_op jit(solution)/shard_map/psum | solution.py:63
  1460.3 24.8 %psum.93 = bf16[64,64]{1,0:T(8,128)(2,1)S(1)} all-reduce(f32[64,64]{1,0:T(8,128)S(1)} %fusion.25), channel_id=1, replica_groups=mesh['prow'=8,'pcol'=32] {'prow'}, use_global_device_ids=true, to_apply=%region_18.19 | all-reduce | flops 4096 | bytes 24576 | tf_op jit(solution)/shard_map/psum | solution.py:69
  1485.1 36.3 %all_gather.22 = bf16[64,2048]{0,1:T(8,128)(2,1)S(1)} all-gather(bf16[64,64]{0,1:T(8,128)(2,1)S(1)} %copy.16), channel_id=1, replica_groups=mesh['prow'=8,'pcol'=32] {'pcol'}, dimensions={1}, use_global_device_ids=true | all-gather | bytes 270336 | tf_op jit(solution)/shard_map/all_gather | solution.py:70
  1524.6 2.3 fusion.6
  1526.9 143.5 %all-reduce.17.cloned.1.call-done = f32[64,256]{1,0:T(8,128)} async-done(((f32[64,256]{1,0:T(8,128)}), f32[64,256]{1,0:T(8,128)}) %all-reduce.17.cloned.1.call-update) | async-done | bytes 65552 | tf_op jit(solution)/shard_map/psum | solution.py:63
  1671.4 24.8 %psum.95 = bf16[64,64]{1,0:T(8,128)(2,1)S(1)} all-reduce(f32[64,64]{1,0:T(8,128)S(1)} %fusion.26), channel_id=1, replica_groups=mesh['prow'=8,'pcol'=32] {'prow'}, use_global_device_ids=true, to_apply=%region_20.21 | all-reduce | flops 4096 | bytes 24576 | tf_op jit(solution)/shard_map/psum | solution.py:69
  1696.2 37.7 %all_gather.23 = bf16[64,2048]{0,1:T(8,128)(2,1)S(1)} all-gather(bf16[64,64]{0,1:T(8,128)(2,1)S(1)} %copy.18), channel_id=1, replica_groups=mesh['prow'=8,'pcol'=32] {'pcol'}, dimensions={1}, use_global_device_ids=true | all-gather | bytes 270336 | tf_op jit(solution)/shard_map/all_gather | solution.py:70
  1734.8 4.8 all-reduce.11.cloned.1.call-done
  (81 shorter events, 36.1 us)
Async XLA Ops:
  7.2 236.8 %reduce-scatter.10.cloned.1.call-start = ((), (), s32[]{:S(2)}) async-start(), calls=%async_computation.9 | async-start | bytes 540672
  30.1 213.8 %copy-start.2 = (bf16[3,64,256]{2,1,0:T(8,128)(2,1)S(1)}, bf16[3,64,256]{2,1,0:T(8,128)(2,1)}, u32[]{:S(2)}) copy-start(bf16[3,64,256]{2,1,0:T(8,128)(2,1)} %param.12) | copy-start | bytes 294916
  32.3 421.7 %all-reduce.7.cloned.1.call-start = ((), (), s32[]{:S(2)}) async-start(), calls=%async_computation.3 | async-start | bytes 1048576 | tf_op jit(solution)/shard_map/psum | solution.py:53
  359.6 307.8 %reduce-scatter.12.cloned.1.call-start = ((), (), s32[]{:S(2)}) async-start(), calls=%async_computation.10 | async-start | bytes 540672
  457.6 419.9 %all-reduce.9.cloned.1.call-start = ((), (), s32[]{:S(2)}) async-start(), calls=%async_computation.4 | async-start | bytes 1048576 | tf_op jit(solution)/shard_map/psum | solution.py:53
  783.0 467.9 %copy-start.3 = (bf16[3,256,64]{1,2,0:T(8,128)(2,1)S(1)}, bf16[3,256,64]{1,2,0:T(8,128)(2,1)}, u32[]{:S(2)}) copy-start(bf16[3,256,64]{1,2,0:T(8,128)(2,1)} %param.14) | copy-start | bytes 294916
  783.0 307.6 %reduce-scatter.14.cloned.1.call-start = ((), (), s32[]{:S(2)}) async-start(), calls=%async_computation.11 | async-start | bytes 540672
  880.9 370.0 %all-reduce.13.cloned.1.call-start = ((), (), s32[]{:S(2)}) async-start(), calls=%async_computation.6 | async-start | bytes 131072 | tf_op jit(solution)/shard_map/psum | solution.py:63
  883.4 575.9 %all-reduce.15.cloned.1.call-start = ((), (), s32[]{:S(2)}) async-start(), calls=%async_computation.7 | async-start | bytes 131072 | tf_op jit(solution)/shard_map/psum | solution.py:63
  1312.4 358.0 %all-reduce.17.cloned.1.call-start = ((), (), s32[]{:S(2)}) async-start(), calls=%async_computation.8 | async-start | bytes 131072 | tf_op jit(solution)/shard_map/psum | solution.py:63
  1524.5 215.1 %all-reduce.11.cloned.1.call-start = ((), (), s32[]{:S(2)}) async-start(), calls=%async_computation.5 | async-start | bytes 1048576 | tf_op jit(solution)/shard_map/psum | solution.py:53
  1734.8 6.5 copy-start
  1741.3 0.8 copy-start.1
Sparse Core Ops, SparseCore 0:
  32.4 211.4 reduce-scatter.9
  359.7 94.2 all-reduce.6
  458.4 209.0 reduce-scatter.11
  783.2 94.2 all-reduce.8
  881.7 208.9 reduce-scatter.13
  1095.0 138.6 all-reduce.12
  1312.5 146.7 all-reduce.14
  1524.7 145.7 all-reduce.16
  1673.4 66.1 all-reduce.10
where the time goes:
time: 1760 us; the launch traced here: 1750 us
  waiting for transfers between devices  1010 us (57%)
  blocking collectives  658 us (37%)
  between operations  27.5 us (2%)
  matrix products  19.4 us (1%)
    unnamed x12, waiting for transfers between devices  629 us
    psum x3, blocking collectives, body(): block_rows = lax.psum(inverse_part, 'pcol').astype(jnp.bfloat16)  337 us
    psum x3, waiting for transfers between devices, body(): sums = lax.psum(partial_value, 'pcol')  290 us
    all_gather x3, blocking collectives, body(): block_full = lax.all_gather(block_rows, 'prow', axis=1, tiled=True)  140 us
    all_gather x3, blocking collectives, body(): new_block = lax.all_gather(new_cols, 'pcol', axis=1, tiled=True)  109 us
    psum x3, waiting for transfers between devices, body(): total = lax.psum(update, 'prow')  95.1 us
    psum x3, blocking collectives, body(): new_cols = lax.psum(inverse_part, 'prow').astype(jnp.bfloat16)  71.9 us
  transfers between devices with their start and end apart: 9, of which 8 were waited for; matrix products, arithmetic and copies ran while one was open for 0% of the time, Pallas kernels for 0%

commit v1 on v0

v1 whole, which is shorter than its diff:
```python
import jax
import jax.numpy as jnp
from jax import lax
from jax.sharding import PartitionSpec as P

NB = 2048
TILE = 256
STEPS = 3
NY = 4
NZ = 8
NP = 8
NC = 32
PER = NB // TILE
Y_GROUPS = [[z * NY + y for y in range(NY)] for z in range(NZ)]
Z_GROUPS = [[z * NY + y for z in range(NZ)] for y in range(NY)]
BF = jnp.bfloat16
F32 = jnp.float32


def swap_y(x):
    return lax.all_to_all(x, "pcol", 0, 0, axis_index_groups=Y_GROUPS, tiled=True)


def swap_z(x):
    return lax.all_to_all(x, "pcol", 0, 0, axis_index_groups=Z_GROUPS, tiled=True)


def swap_pcol(x):
    return lax.all_to_all(x, "pcol", 0, 0, tiled=True)


def swap_prow(x):
    return lax.all_to_all(x, "prow", 0, 0, tiled=True)


def to_all(x, count):
    return jnp.broadcast_to(x[None], (count,) + x.shape)


def total(x):
    return jnp.sum(x.astype(F32), axis=0)


def choose(values, index):
    where = (index[:, None] == jnp.arange(values.shape[0])[None, :]).astype(BF)
    flat = jnp.dot(where, values.reshape(values.shape[0], -1), preferred_element_type=F32)
    return flat.astype(BF).reshape((index.shape[0],) + values.shape[1:])


def body(rhs, pivots, tile_of, upper_rows, upper_inv, lower_rows, lower_inv, solved):
    col = lax.axis_index("pcol")
    row = lax.axis_index("prow")
    z = col // NY
    count, width = rhs.shape
    slots = width // TILE
    rows_z = count // NY
    rows_own = count // NC
    first_tiles = tile_of.reshape(NC, slots)[:, 0]
    my_tile = first_tiles[col]
    my_block = my_tile // PER
    my_place = my_tile % PER
    plane_tiles = lax.dynamic_slice_in_dim(first_tiles, z * NY, NY)
    plane_blocks = plane_tiles // PER

    lower_pack = jnp.concatenate(
        [
            jnp.swapaxes(lower_inv, 1, 2).reshape(STEPS * (NB // NC), TILE),
            lower_rows[: STEPS - 1, :, :TILE].reshape((STEPS - 1) * TILE, TILE),
        ],
        axis=0,
    )
    lower_all = lax.all_gather(lower_pack, "pcol", axis=0)

    local_pivots = pivots - col * width
    own = jnp.take(rhs[:, :TILE], local_pivots[:TILE], axis=1)
    state0 = jnp.take(rhs, local_pivots, axis=1)

    own = own.reshape(NZ, NY, rows_own, TILE).transpose(1, 0, 2, 3).reshape(NY, rows_z, TILE)
    own_high = own.astype(BF)
    own_low = (own - own_high.astype(F32)).astype(BF)
    upper_pack = jnp.concatenate(
        [
            upper_inv.reshape(STEPS * (NB // NC), TILE),
            upper_rows[: STEPS - 1, :, :TILE].reshape((STEPS - 1) * TILE, TILE),
        ],
        axis=0,
    )
    got = swap_y(jnp.concatenate([own_high, own_low, to_all(upper_pack, NY)], axis=1))
    tiles = got[:, :rows_z].astype(F32) + got[:, rows_z : 2 * rows_z].astype(F32)
    at = 2 * rows_z
    inverse = []
    for step in range(STEPS):
        inverse.append(got[:, at : at + NB // NC].reshape(TILE, TILE))
        at += NB // NC
    upper_tiles = []
    for step in range(STEPS - 1):
        upper_tiles.append(got[:, at : at + TILE])
        at += TILE

    slot_known = jnp.where(my_block >= STEPS, solved[:, :TILE], 0.0)
    known = jnp.concatenate([slot_known, solved[:, TILE:]], axis=1).astype(BF)
    outer = lax.dot_general(
        known, lower_rows, (((1,), (2,)), ((), ())), preferred_element_type=F32
    )
    outer = outer.astype(BF).reshape(NZ, NY * rows_own * STEPS, TILE)

    finished = []
    for step in range(STEPS):
        block = tiles.astype(BF)
        pick = plane_tiles[None, :] == step * PER + jnp.arange(NZ)[:, None]
        routed = jnp.sum(jnp.where(pick[:, :, None, None], block[None], 0), axis=1)
        mine = jnp.sum(swap_z(routed), axis=0)
        part = jnp.dot(mine, inverse[step], preferred_element_type=F32).astype(BF)
        message = to_all(part, NZ)
        if step == 1:
            message = jnp.concatenate([message, outer], axis=1)
        back = total(swap_z(message))
        solved_rows = back[:rows_z].astype(BF)
        if step == 1:
            outer_sum = back[rows_z:]
        finished.append(solved_rows)
        if step < STEPS - 1:
            update = lax.dot_general(
                solved_rows,
                upper_tiles[step],
                (((1,), (1,)), ((), ())),
                preferred_element_type=F32,
            )
            update = total(swap_prow(to_all(update.astype(BF), NP)))
            update = update.transpose(1, 0, 2)
            tiles = tiles - jnp.where((plane_blocks > step)[:, None, None], update, 0.0)

    stacked = jnp.concatenate(finished, axis=0)
    outer_send = outer_sum.astype(BF).reshape(NY, rows_own * STEPS, TILE)
    got = swap_y(jnp.concatenate([outer_send, to_all(stacked, NY)], axis=1))
    outer_rows = total(got[:, : rows_own * STEPS]).reshape(rows_own, STEPS, TILE)
    every = got[:, rows_own * STEPS :].reshape(NY, STEPS, NZ, rows_own, TILE)
    every = every.transpose(1, 2, 0, 3, 4).reshape(STEPS, count, TILE)

    bulk = jnp.dot(
        jnp.concatenate(list(every), axis=1),
        upper_rows.reshape(STEPS * TILE, width),
        preferred_element_type=F32,
    )
    window_value = jnp.where(
        my_place == row, lax.dynamic_index_in_dim(every, jnp.minimum(my_block, STEPS - 1), 0, False), 0
    ).astype(F32)
    slot_bulk = jnp.where(my_block < STEPS, window_value, bulk[:, :TILE])
    bulk = jnp.concatenate([slot_bulk, bulk[:, TILE:]], axis=1).astype(BF)
    bulk = bulk.reshape(NP, count // NP, width)

    inverse_rows = STEPS * (NB // NC)
    found = [None] * STEPS
    later = [outer_rows[:, step] for step in range(STEPS)]
    for step in reversed(range(STEPS)):
        own_rows = lax.dynamic_slice_in_dim(finished[step], z * rows_own, rows_own, 0)
        resid = (own_rows.astype(F32) - later[step]).astype(BF)
        weights = lower_all[:, step * (NB // NC) : (step + 1) * (NB // NC)].reshape(NB, TILE)
        part = lax.dot_general(
            resid, weights, (((1,), (1,)), ((), ())), preferred_element_type=F32
        ).astype(BF)
        message = to_all(part, NP)
        if step == 1:
            message = jnp.concatenate([message, bulk], axis=1)
        if step == 0:
            message = jnp.concatenate([message, to_all(bulk_sum, NP)], axis=1)
        back = swap_prow(message)
        if step == 1:
            bulk_sum = total(back[:, rows_own:]).astype(BF)
        if step == 0:
            bulk_all = back[:, rows_own:].reshape(count, width).astype(F32)
        value = total(back[:, :rows_own]).astype(BF)
        value = value.reshape(rows_own, PER, TILE).transpose(1, 0, 2)
        found[step] = value
        for earlier in range(step):
            spread = choose(value, first_tiles - step * PER)
            start = inverse_rows + earlier * TILE
            piece = lax.dot_general(
                spread,
                lower_all[:, start : start + TILE],
                (((2,), (2,)), ((0,), (0,))),
                preferred_element_type=F32,
            )
            later[earlier] = later[earlier] + jnp.sum(piece, axis=0)

    window = jnp.concatenate(found, axis=0)
    window = swap_pcol(choose(window, first_tiles)).reshape(count, TILE).astype(F32)
    slot_solution = jnp.where(my_block < STEPS, window, solved[:, :TILE])
    backward = jnp.concatenate([slot_solution, solved[:, TILE:]], axis=1)
    slot_forward = jnp.where(
        my_block < STEPS, bulk_all[:, :TILE], state0[:, :TILE] - bulk_all[:, :TILE]
    )
    forward = jnp.concatenate([slot_forward, state0[:, TILE:] - bulk_all[:, TILE:]], axis=1)
    return (forward, backward)


def solution(mesh):
    return jax.shard_map(
        body,
        mesh=mesh,
        in_specs=(
            P(None, "pcol"),
            P("pcol"),
            P(),
            P(None, "prow", "pcol"),
            P(None, "pcol", "prow"),
            P(None, "prow", "pcol"),
            P(None, "prow", "pcol"),
            P(None, "pcol"),
        ),
        out_specs=(P(None, "pcol"), P(None, "pcol")),
        check_vma=False,
    )
```

time: 1760 us -> 249 us (0.14)
  waiting for transfers between devices: 1010 us -> 72.7 us
  blocking collectives: 658 us -> 36.2 us
  starting transfers between devices: 0.37 us -> 59.4 us
    unnamed x12 -> x1, waiting for transfers between devices: 629 us -> 0.02 us
    psum x6 -> x0, blocking collectives: 409 us -> none  [the longest x3 337 us: body(): block_rows = lax.psum(inverse_part, 'pcol').astype(jnp.bfloat16)]
    psum x6 -> x0, waiting for transfers between devices: 385 us -> none  [the longest x3 290 us: body(): sums = lax.psum(partial_value, 'pcol')]
    all_gather x6 -> x0, blocking collectives: 249 us -> none  [the longest x3 140 us: body(): block_full = lax.all_gather(block_rows, 'prow', axis=1, tiled=True)]
    all_to_all x0 -> x11, waiting for transfers between devices: none -> 72.6 us  [the longest x4 24.3 us: swap_z(): lax.all_to_all(x, 'pcol', 0, 0, axis_index_groups=Z_GROUPS, tiled=True)]
    all_to_all x0 -> x11, starting transfers between devices: none -> 59.3 us  [the longest x4 24.4 us: swap_prow(): return lax.all_to_all(x, 'prow', 0, 0, tiled=True)]
    all_to_all x0 -> x3, blocking collectives: none -> 36.2 us  [the longest x2 22.7 us: swap_z(): lax.all_to_all(x, 'pcol', 0, 0, axis_index_groups=Z_GROUPS, tiled=True)]
  transfers between devices with their start and end apart: 9 -> 12, of which waited for: 8 -> 10; matrix products, arithmetic and copies ran while one was open for 0% -> 17% of each run, Pallas kernels for 0% -> 0%
where the time goes in v1:
time: 249 us; the launch traced here: 247 us
  waiting for transfers between devices  72.7 us (29%)
  starting transfers between devices  59.4 us (24%)
  blocking collectives  36.2 us (15%)
  local copies, waits for them, and re-layouts  22 us (9%)
  other arithmetic  20.2 us (8%)
  matrix products  19.3 us (8%)
  between operations  17.3 us (7%)
    all_to_all x4, starting transfers between devices, swap_prow(): return lax.all_to_all(x, 'prow', 0, 0, tiled=True)  24.4 us
    all_to_all x4, waiting for transfers between devices, swap_z(): lax.all_to_all(x, 'pcol', 0, 0, axis_index_groups=Z_GROUPS, tiled=True)  24.3 us
    all_to_all x2, blocking collectives, swap_z(): lax.all_to_all(x, 'pcol', 0, 0, axis_index_groups=Z_GROUPS, tiled=True)  22.7 us
    all_to_all x4, starting transfers between devices, swap_z(): lax.all_to_all(x, 'pcol', 0, 0, axis_index_groups=Z_GROUPS, tiled=True)  21.6 us
    all_to_all x2, waiting for transfers between devices, swap_y(): lax.all_to_all(x, 'pcol', 0, 0, axis_index_groups=Y_GROUPS, tiled=True)  20.6 us
    all_to_all x4, waiting for transfers between devices, swap_prow(): return lax.all_to_all(x, 'prow', 0, 0, tiled=True)  19.9 us
    all_to_all x1, blocking collectives, swap_prow(): return lax.all_to_all(x, 'prow', 0, 0, tiled=True)  13.4 us
    dot_general x3, matrix products, body(): lax.dot_general(resid, weights, (((1,), (1,)), ((), ())), preferred_eleme...  8.84 us
  transfers between devices with their start and end apart: 12, of which 10 were waited for; matrix products, arithmetic and copies ran while one was open for 17% of the time, Pallas kernels for 0%

profile of v1, /device:TPU:1, one launch (start us, length us, event | category | flops | bytes accessed | tf_op | source)
XLA Modules:
  0.0 247.0 jit_solution(5384892492573945297)
XLA Ops:
  15.3 5.1 %all-to-all-start = ((bf16[4,736,256]{2,1,0:T(8,128)(2,1)}), bf16[4,736,256]{2,1,0:T(8,128)(2,1)S(1)}, u32[]{:S(2)}, u32[]{:S(2)}) async-start(bf16[4,736,256]{2,1,0:T(8,128)(2,1)} %pad_maximum_fusion), calls=%async_computation | async-start | bytes 3014656 | tf_op jit(solution)/shard_map/all_to_all | solution.py:21
  22.0 20.6 %all-to-all-done = bf16[4,736,256]{2,1,0:T(8,128)(2,1)S(1)} async-done(((bf16[4,736,256]{2,1,0:T(8,128)(2,1)}), bf16[4,736,256]{2,1,0:T(8,128)(2,1)S(1)}, u32[]{:S(2)}, u32[]{:S(2)}) %all-to-all-start) | async-done | bytes 1507360 | tf_op jit(solution)/shard_map/all_to_all | solution.py:21
  43.4 10.9 %all-to-all-start.1 = ((bf16[8,16,256]{2,1,0:T(8,128)(2,1)}), bf16[8,16,256]{2,1,0:T(8,128)(2,1)S(1)}, u32[]{:S(2)}, u32[]{:S(2)}) async-start(bf16[8,16,256]{2,1,0:T(8,128)(2,1)} %select_reduce_fusion.2), calls=%async_computation.1 | async-start | bytes 131072 | tf_op jit(solution)/shard_map/all_to_all | solution.py:25
  54.9 6.6 %all-to-all-done.1 = bf16[8,16,256]{2,1,0:T(8,128)(2,1)S(1)} async-done(((bf16[8,16,256]{2,1,0:T(8,128)(2,1)}), bf16[8,16,256]{2,1,0:T(8,128)(2,1)S(1)}, u32[]{:S(2)}, u32[]{:S(2)}) %all-to-all-start.1) | async-done | bytes 65568 | tf_op jit(solution)/shard_map/all_to_all | solution.py:25
  66.3 6.7 %all-to-all-done.2 = bf16[8,16,256]{2,1,0:T(8,128)(2,1)S(1)} async-done(((bf16[8,16,256]{2,1,0:T(8,128)(2,1)}), bf16[8,16,256]{2,1,0:T(8,128)(2,1)S(1)}, u32[]{:S(2)}, u32[]{:S(2)}) %all-to-all-start.2) | async-done | bytes 65568 | tf_op jit(solution)/shard_map/all_to_all | solution.py:25
  73.9 9.3 %all-to-all-start.3 = ((bf16[8,16,4,256]{3,1,2,0:T(8,128)(2,1)}), bf16[8,16,4,256]{3,1,2,0:T(8,128)(2,1)S(1)}, u32[]{:S(2)}, u32[]{:S(2)}) async-start(bf16[8,16,4,256]{3,1,2,0:T(8,128)(2,1)} %broadcast_in_dim.189), calls=%async_computation.3 | async-start | bytes 524288 | tf_op jit(solution)/shard_map/all_to_all | solution.py:33
  92.0 4.0 %all-to-all-start.4 = ((bf16[8,16,256]{2,1,0:T(8,128)(2,1)}), bf16[8,16,256]{2,1,0:T(8,128)(2,1)}, u32[]{:S(2)}, u32[]{:S(2)}) async-start(bf16[8,16,256]{2,1,0:T(8,128)(2,1)} %select_reduce_fusion.1), calls=%async_computation.4 | async-start | bytes 131072 | tf_op jit(solution)/shard_map/all_to_all | solution.py:25
  100.0 3.9 %all-to-all-done.4 = bf16[8,16,256]{2,1,0:T(8,128)(2,1)} async-done(((bf16[8,16,256]{2,1,0:T(8,128)(2,1)}), bf16[8,16,256]{2,1,0:T(8,128)(2,1)}, u32[]{:S(2)}, u32[]{:S(2)}) %all-to-all-start.4) | async-done | bytes 65568 | tf_op jit(solution)/shard_map/all_to_all | solution.py:25
  105.8 13.1 %all_to_all.70 = bf16[8,40,256]{2,1,0:T(8,128)(2,1)S(1)} all-to-all(bf16[8,40,256]{2,1,0:T(8,128)(2,1)S(1)} %pad_maximum_fusion.6), channel_id=1, replica_groups={{0,4,8,12,16,20,24,28},{1,5,9,13,17,21,25,29},{2,6,10,14,18,22,26,30},{..., dimensions={0} | all-to-all | bytes 327680 | tf_op jit(solution)/shard_map/all_to_all | solution.py:25
  119.2 13.4 %all_to_all.71 = bf16[8,16,4,256]{3,1,2,0:T(8,128)(2,1)S(1)} all-to-all(bf16[8,16,4,256]{3,1,2,0:T(8,128)(2,1)S(1)} %broadcast_in_dim.196), channel_id=1, replica_groups=mesh['prow'=8,'pcol'=32] {'prow'}, dimensions={0} | all-to-all | bytes 524288 | tf_op jit(solution)/shard_map/all_to_all | solution.py:33
  134.2 9.6 %all_to_all.72 = bf16[8,16,256]{2,1,0:T(8,128)(2,1)S(1)} all-to-all(bf16[8,16,256]{2,1,0:T(8,128)(2,1)S(1)} %select_reduce_fusion), channel_id=1, replica_groups={{0,4,8,12,16,20,24,28},{1,5,9,13,17,21,25,29},{2,6,10,14,18,22,26,30},{..., dimensions={0} | all-to-all | bytes 131072 | tf_op jit(solution)/shard_map/all_to_all | solution.py:25
  148.0 7.1 %all-to-all-done.8 = bf16[8,16,256]{2,1,0:T(8,128)(2,1)S(1)} async-done(((bf16[8,16,256]{2,1,0:T(8,128)(2,1)}), bf16[8,16,256]{2,1,0:T(8,128)(2,1)S(1)}, u32[]{:S(2)}, u32[]{:S(2)}) %all-to-all-start.8) | async-done | bytes 65568 | tf_op jit(solution)/shard_map/all_to_all | solution.py:25
  159.2 5.5 %gather_fusion.1 = f32[2048,64]{1,0:T(8,128)S(1)} fusion(f32[64,2048]{0,1:T(8,128)S(1)} %copy.73, s32[2048]{0:T(1024)S(1)} %fusion.61), kind=kCustom, calls=%fused_computation.1 | custom fusion | bytes 1056768 | tf_op jit(solution)/shard_map/jit(_take)/gather | solution.py:76
  172.7 6.5 %all-to-all-start.10 = ((bf16[8,2,2048]{2,1,0:T(2,128)(2,1)}), bf16[8,2,2048]{2,1,0:T(2,128)(2,1)S(1)}, u32[]{:S(2)}, u32[]{:S(2)}) async-start(bf16[8,2,2048]{2,1,0:T(2,128)(2,1)} %broadcast_in_dim.200), calls=%async_computation.10 | async-start | bytes 131072 | tf_op jit(solution)/shard_map/all_to_all | solution.py:33
  180.0 4.1 %all-to-all-done.10 = bf16[8,2,2048]{2,1,0:T(2,128)(2,1)S(1)} async-done(((bf16[8,2,2048]{2,1,0:T(2,128)(2,1)}), bf16[8,2,2048]{2,1,0:T(2,128)(2,1)S(1)}, u32[]{:S(2)}, u32[]{:S(2)}) %all-to-all-start.10) | async-done | bytes 65568 | tf_op jit(solution)/shard_map/all_to_all | solution.py:33
  184.4 4.2 %convolution_convert_fusion.1 = bf16[2,2048]{1,0:T(2,128)(2,1)S(1)} fusion(bf16[2048,256]{1,0:T(8,128)(2,1)S(1)} %bitcast.132, bf16[32,2,256]{2,1,0:T(2,128)(2,1)S(1)} %reshape.282, bf16[32,704,256]{2,1,0:T(8,128)(2,1)} %bitcast.127, f32[2,1,256]{2,1,0:T(1,128)S(1)} %get-tuple-element.23, bf16[16,256]{1,0:T(8,128)(2,1)S(1)} %slice.167, s32[]{:T(128)S(6)} %select_n.124), kind=kOutput, calls=%fused_computation.9 | convolution fusion | flops 10491904 | bytes 5286916 | tf_op jit(solution)/shard_map/dot_general | solution.py:159
  189.6 4.2 %all-to-all-start.11 = ((bf16[8,10,2048]{2,1,0:T(8,128)(2,1)}), bf16[8,10,2048]{2,1,0:T(8,128)(2,1)S(1)}, u32[]{:S(2)}, u32[]{:S(2)}) async-start(bf16[8,10,2048]{2,1,0:T(8,128)(2,1)} %maximum_maximum_fusion), calls=%async_computation.11 | async-start | bytes 1048576 | tf_op jit(solution)/shard_map/all_to_all | solution.py:33
  193.8 3.4 %fusion.33 = f32[2,256]{1,0:T(2,128)S(1)} fusion(bf16[32,2,256]{2,1,0:T(2,128)(2,1)S(1)} %reshape.282, bf16[32,704,256]{2,1,0:T(8,128)(2,1)} %bitcast.128, f32[2,1,256]{2,1,0:T(1,128)S(1)} %get-tuple-element.21), kind=kOutput, calls=%fused_computation.30 | convolution fusion | flops 8389120 | bytes 4231168 | tf_op jit(solution)/shard_map/dot_general | solution.py:178
  197.2 6.1 %all-to-all-done.11 = bf16[8,10,2048]{2,1,0:T(8,128)(2,1)S(1)} async-done(((bf16[8,10,2048]{2,1,0:T(8,128)(2,1)}), bf16[8,10,2048]{2,1,0:T(8,128)(2,1)S(1)}, u32[]{:S(2)}, u32[]{:S(2)}) %all-to-all-start.11) | async-done | bytes 327712 | tf_op jit(solution)/shard_map/all_to_all | solution.py:33
  203.6 4.2 %convolution_convert_fusion = bf16[2,2048]{1,0:T(2,128)(2,1)S(1)} fusion(bf16[2048,256]{1,0:T(8,128)(2,1)S(1)} %bitcast.131, f32[2,256]{1,0:T(2,128)S(1)} %fusion.33, bf16[32,2,256]{2,1,0:T(2,128)(2,1)S(1)} %reshape.289, bf16[32,704,256]{2,1,0:T(8,128)(2,1)} %bitcast.129, bf16[16,256]{1,0:T(8,128)(2,1)S(1)} %reduce_sum.194, s32[]{:T(128)S(6)} %select_n.124), kind=kOutput, calls=%fused_computation.8 | convolution fusion | flops 10491904 | bytes 5286916 | tf_op jit(solution)/shard_map/dot_general | solution.py:159
  209.0 4.4 %all-to-all-start.12 = ((bf16[8,10,2048]{2,1,0:T(8,128)(2,1)}), bf16[8,10,2048]{2,1,0:T(8,128)(2,1)S(1)}, u32[]{:S(2)}, u32[]{:S(2)}) async-start(bf16[8,10,2048]{2,1,0:T(8,128)(2,1)} %pad_maximum_fusion.1), calls=%async_computation.12 | async-start | bytes 1048576 | tf_op jit(solution)/shard_map/all_to_all | solution.py:33
  213.5 9.4 %all-to-all-done.12 = bf16[8,10,2048]{2,1,0:T(8,128)(2,1)S(1)} async-done(((bf16[8,10,2048]{2,1,0:T(8,128)(2,1)}), bf16[8,10,2048]{2,1,0:T(8,128)(2,1)S(1)}, u32[]{:S(2)}, u32[]{:S(2)}) %all-to-all-start.12) | async-done | bytes 327712 | tf_op jit(solution)/shard_map/all_to_all | solution.py:33
  225.7 4.8 %all-to-all-start.13 = ((bf16[32,2,256]{2,1,0:T(2,128)(2,1)}), bf16[32,2,256]{2,1,0:T(2,128)(2,1)S(1)}, u32[]{:S(2)}, u32[]{:S(2)}) async-start(bf16[32,2,256]{2,1,0:T(2,128)(2,1)} %reshape.293), calls=%async_computation.13 | async-start | bytes 65536 | tf_op jit(solution)/shard_map/all_to_all | solution.py:29
  231.4 7.9 %all-to-all-done.13 = bf16[32,2,256]{2,1,0:T(2,128)(2,1)S(1)} async-done(((bf16[32,2,256]{2,1,0:T(2,128)(2,1)}), bf16[32,2,256]{2,1,0:T(2,128)(2,1)S(1)}, u32[]{:S(2)}, u32[]{:S(2)}) %all-to-all-start.13) | async-done | bytes 32800 | tf_op jit(solution)/shard_map/all_to_all | solution.py:29
  (147 shorter events, 54.5 us)
Async XLA Ops:
  7.2 4.1 %copy-start.7 = (s32[2048]{0:T(1024)S(1)}, s32[2048]{0:T(1024)}, u32[]{:S(2)}) copy-start(s32[2048]{0:T(1024)} %param.9) | copy-start | bytes 24580
  7.2 6.7 %copy-start.4 = (bf16[3,64,256]{2,1,0:T(8,128)(2,1)S(1)}, bf16[3,64,256]{2,1,0:T(8,128)(2,1)}, u32[]{:S(2)}) copy-start(bf16[3,64,256]{2,1,0:T(8,128)(2,1)} %param.12) | copy-start | bytes 294916
  7.2 162.2 %all-gather.3.cloned.1.call-start = ((), (), s32[]{:S(2)}) async-start(), calls=%async_computation.14 | async-start | bytes 11894784 | tf_op jit(solution)/shard_map/all_gather | solution.py:72
  14.0 6.4 %copy-start.8 = (s32[256]{0:T(256)S(1)}, s32[256]{0:T(256)}, u32[]{:S(2)}) copy-start(s32[256]{0:T(256)} %param.10) | copy-start | bytes 3076
  15.3 72.9 %copy-start = (f32[64,2048]{1,0:T(8,128)S(1)}, f32[64,2048]{1,0:T(8,128)}, u32[]{:S(2)}) copy-start(f32[64,2048]{1,0:T(8,128)} %param.15) | copy-start | bytes 1572868
  15.3 27.3 %all-to-all-start = ((bf16[4,736,256]{2,1,0:T(8,128)(2,1)}), bf16[4,736,256]{2,1,0:T(8,128)(2,1)S(1)}, u32[]{:S(2)}, u32[]{:S(2)}) async-start(bf16[4,736,256]{2,1,0:T(8,128)(2,1)} %pad_maximum_fusion), calls=%async_computation | async-start | bytes 3014656 | tf_op jit(solution)/shard_map/all_to_all | solution.py:21
  43.4 18.2 %all-to-all-start.1 = ((bf16[8,16,256]{2,1,0:T(8,128)(2,1)}), bf16[8,16,256]{2,1,0:T(8,128)(2,1)S(1)}, u32[]{:S(2)}, u32[]{:S(2)}) async-start(bf16[8,16,256]{2,1,0:T(8,128)(2,1)} %select_reduce_fusion.2), calls=%async_computation.1 | async-start | bytes 131072 | tf_op jit(solution)/shard_map/all_to_all | solution.py:25
  62.3 10.6 %all-to-all-start.2 = ((bf16[8,16,256]{2,1,0:T(8,128)(2,1)}), bf16[8,16,256]{2,1,0:T(8,128)(2,1)S(1)}, u32[]{:S(2)}, u32[]{:S(2)}) async-start(bf16[8,16,256]{2,1,0:T(8,128)(2,1)} %broadcast_in_dim.186), calls=%async_computation.2 | async-start | bytes 131072 | tf_op jit(solution)/shard_map/all_to_all | solution.py:25
  73.9 15.9 %all-to-all-start.3 = ((bf16[8,16,4,256]{3,1,2,0:T(8,128)(2,1)}), bf16[8,16,4,256]{3,1,2,0:T(8,128)(2,1)S(1)}, u32[]{:S(2)}, u32[]{:S(2)}) async-start(bf16[8,16,4,256]{3,1,2,0:T(8,128)(2,1)} %broadcast_in_dim.189), calls=%async_computation.3 | async-start | bytes 524288 | tf_op jit(solution)/shard_map/all_to_all | solution.py:33
  89.8 15.0 %copy-start.3 = (bf16[4,64,256]{2,1,0:T(8,128)(2,1)S(1)}, bf16[4,64,256]{2,1,0:T(8,128)(2,1)}, u32[]{:S(2)}) copy-start(bf16[4,64,256]{2,1,0:T(8,128)(2,1)} %get-tuple-element.15) | copy-start | bytes 393220
  92.0 11.9 %all-to-all-start.4 = ((bf16[8,16,256]{2,1,0:T(8,128)(2,1)}), bf16[8,16,256]{2,1,0:T(8,128)(2,1)}, u32[]{:S(2)}, u32[]{:S(2)}) async-start(bf16[8,16,256]{2,1,0:T(8,128)(2,1)} %select_reduce_fusion.1), calls=%async_computation.4 | async-start | bytes 131072 | tf_op jit(solution)/shard_map/all_to_all | solution.py:25
  144.6 10.5 %all-to-all-start.8 = ((bf16[8,16,256]{2,1,0:T(8,128)(2,1)}), bf16[8,16,256]{2,1,0:T(8,128)(2,1)S(1)}, u32[]{:S(2)}, u32[]{:S(2)}) async-start(bf16[8,16,256]{2,1,0:T(8,128)(2,1)} %broadcast_in_dim.198), calls=%async_computation.8 | async-start | bytes 131072 | tf_op jit(solution)/shard_map/all_to_all | solution.py:25
  155.8 9.2 %all-to-all-start.9 = ((bf16[4,54,256]{2,1,0:T(8,128)(2,1)}), bf16[4,54,256]{2,1,0:T(8,128)(2,1)S(1)}, u32[]{:S(2)}, u32[]{:S(2)}) async-start(bf16[4,54,256]{2,1,0:T(8,128)(2,1)} %pad_maximum_fusion.7), calls=%async_computation.9 | async-start | bytes 229376 | tf_op jit(solution)/shard_map/all_to_all | solution.py:21
  169.4 14.7 %copy-start.11 = (s32[32]{0:T(128)S(1)}, s32[32]{0:T(128)}, u32[]{:S(2)}) copy-start(s32[32]{0:T(128)} %get-tuple-element.3) | copy-start | bytes 388
  172.7 11.4 %all-to-all-start.10 = ((bf16[8,2,2048]{2,1,0:T(2,128)(2,1)}), bf16[8,2,2048]{2,1,0:T(2,128)(2,1)S(1)}, u32[]{:S(2)}, u32[]{:S(2)}) async-start(bf16[8,2,2048]{2,1,0:T(2,128)(2,1)} %broadcast_in_dim.200), calls=%async_computation.10 | async-start | bytes 131072 | tf_op jit(solution)/shard_map/all_to_all | solution.py:33
  180.0 8.7 %copy-start.2 = (bf16[8,8,1792]{2,1,0:T(8,128)(2,1)S(1)}, bf16[8,8,1792]{2,1,0:T(8,128)(2,1)}, u32[]{:S(2)}) copy-start(bf16[8,8,1792]{2,1,0:T(8,128)(2,1)} %fusion.45) | copy-start | bytes 688132
  188.6 14.8 %copy-start.10 = (s32[32]{0:T(128)S(1)}, s32[32]{0:T(128)}, u32[]{:S(2)}) copy-start(s32[32]{0:T(128)} %get-tuple-element.4) | copy-start | bytes 388
  189.6 13.7 %all-to-all-start.11 = ((bf16[8,10,2048]{2,1,0:T(8,128)(2,1)}), bf16[8,10,2048]{2,1,0:T(8,128)(2,1)S(1)}, u32[]{:S(2)}, u32[]{:S(2)}) async-start(bf16[8,10,2048]{2,1,0:T(8,128)(2,1)} %maximum_maximum_fusion), calls=%async_computation.11 | async-start | bytes 1048576 | tf_op jit(solution)/shard_map/all_to_all | solution.py:33
  203.6 9.8 %copy-start.6 = (pred[2048]{0:T(1024)(128)(4,1)S(1)}, pred[2048]{0:T(1024)(128)(4,1)}, u32[]{:S(2)}) copy-start(pred[2048]{0:T(1024)(128)(4,1)} %get-tuple-element.5) | copy-start | bytes 6148
  207.9 17.0 %copy-start.9 = (s32[32]{0:T(128)S(1)}, s32[32]{0:T(128)}, u32[]{:S(2)}) copy-start(s32[32]{0:T(128)} %get-tuple-element.2) | copy-start | bytes 388
  209.0 30.3 %slice-start = ((f32[64,2048]{1,0:T(8,128)}), f32[64,1792]{1,0:T(8,128)S(1)}, s32[]{:S(2)}) async-start(f32[64,2048]{1,0:T(8,128)} %param.15), calls=%async_computation.15 | async-start | bytes 917504 | tf_op jit(solution)/shard_map/slice | solution.py:101
  209.0 13.9 %all-to-all-start.12 = ((bf16[8,10,2048]{2,1,0:T(8,128)(2,1)}), bf16[8,10,2048]{2,1,0:T(8,128)(2,1)S(1)}, u32[]{:S(2)}, u32[]{:S(2)}) async-start(bf16[8,10,2048]{2,1,0:T(8,128)(2,1)} %pad_maximum_fusion.1), calls=%async_computation.12 | async-start | bytes 1048576 | tf_op jit(solution)/shard_map/all_to_all | solution.py:33
  222.9 0.8 copy-start.1
  225.7 13.5 %all-to-all-start.13 = ((bf16[32,2,256]{2,1,0:T(2,128)(2,1)}), bf16[32,2,256]{2,1,0:T(2,128)(2,1)S(1)}, u32[]{:S(2)}, u32[]{:S(2)}) async-start(bf16[32,2,256]{2,1,0:T(2,128)(2,1)} %reshape.293), calls=%async_computation.13 | async-start | bytes 65536 | tf_op jit(solution)/shard_map/all_to_all | solution.py:29
  (1 other events, 0.8 us)
Sparse Core Ops, SparseCore 0:
  11.2 122.6 all-gather.2

commit v2 on v1

v2 whole, which is shorter than its diff:
```python
import jax
import jax.numpy as jnp
from jax import lax
from jax.experimental import pallas as pl
from jax.experimental.pallas import tpu as pltpu
from jax.sharding import PartitionSpec as P

NB = 2048
TILE = 256
STEPS = 3
NY = 4
NZ = 8
NP = 8
NC = 32
PER = NB // TILE
PIECE = NB // NC
Y_GROUPS = [[z * NY + y for y in range(NY)] for z in range(NZ)]
Z_GROUPS = [[z * NY + y for z in range(NZ)] for y in range(NY)]
BF = jnp.bfloat16
F32 = jnp.float32
UPPER_AT = STEPS * PIECE
LOWER_AT = UPPER_AT + PIECE
PACK = LOWER_AT + (STEPS - 1) * TILE
ROWS = 16


def swap_y(x):
    return lax.all_to_all(x, "pcol", 0, 0, axis_index_groups=Y_GROUPS, tiled=True)


def swap_z(x):
    return lax.all_to_all(x, "pcol", 0, 0, axis_index_groups=Z_GROUPS, tiled=True)


def swap_pcol(x):
    return lax.all_to_all(x, "pcol", 0, 0, tiled=True)


def swap_prow(x):
    return lax.all_to_all(x, "prow", 0, 0, tiled=True)


def to_all(x, count):
    return jnp.broadcast_to(x[None], (count,) + x.shape)


def total(x):
    return jnp.sum(x.astype(F32), axis=0)


def choose(values, index):
    where = (index[:, None] == jnp.arange(values.shape[0])[None, :]).astype(BF)
    flat = jnp.dot(where, values.reshape(values.shape[0], -1), preferred_element_type=F32)
    return flat.astype(BF).reshape((index.shape[0],) + values.shape[1:])


def dot_nt(a, b):
    return lax.dot_general(a, b, (((1,), (1,)), ((), ())), preferred_element_type=F32)


def dot_nn(a, b):
    return jnp.dot(a, b, preferred_element_type=F32)


def place_mask(place):
    return lax.broadcasted_iota(jnp.int32, (ROWS, TILE), 0) % PER == place


def lower_part(resid, inverse):
    part = jnp.zeros((ROWS, TILE), F32)
    for place in range(PER):
        weights = inverse[4 * place : 4 * place + 4].reshape(TILE, TILE)
        part = jnp.where(place_mask(place), dot_nt(resid, weights), part)
    return part.astype(BF)


def last_kernel(pos, got, pick_own, outer, pack, solved_out, message_out, upper, inverse, sems):
    copies = [
        pltpu.make_async_copy(pack.at[:, pl.ds(UPPER_AT, PIECE), :], upper, sems.at[0]),
        pltpu.make_async_copy(
            pack.at[:, pl.ds((STEPS - 1) * PIECE, PIECE), :], inverse, sems.at[1]
        ),
    ]
    for copy in copies:
        copy.start()
    copies[0].wait()
    value = jnp.zeros((ROWS, TILE), F32)
    for place in range(PER):
        weights = upper[4 * place : 4 * place + 4].reshape(TILE, TILE)
        value = value + dot_nn(got[pos[(STEPS - 1) * PER + place]], weights)
    value = value.astype(BF)
    solved_out[...] = value
    resid = (dot_nn(pick_own[...], value) - outer[...]).astype(BF)
    copies[1].wait()
    part = lower_part(resid, inverse)
    for index in range(NP):
        message_out[index] = part


def last_call(pos, got, pick_own, outer, pack):
    vmem = pl.BlockSpec(memory_space=pltpu.VMEM)
    return pl.pallas_call(
        last_kernel,
        out_shape=(
            jax.ShapeDtypeStruct((ROWS, TILE), BF),
            jax.ShapeDtypeStruct((NP, ROWS, TILE), BF),
        ),
        in_specs=[
            pl.BlockSpec(memory_space=pltpu.SMEM),
            vmem,
            vmem,
            vmem,
            pl.BlockSpec(memory_space=pl.ANY),
        ],
        out_specs=(vmem, vmem),
        scratch_shapes=[
            pltpu.VMEM((NC, PIECE, TILE), BF),
            pltpu.VMEM((NC, PIECE, TILE), BF),
            pltpu.SemaphoreType.DMA((2,)),
        ],
        compiler_params=pltpu.CompilerParams(vmem_limit_bytes=24 << 20),
        name="last_block",
    )(pos, got, pick_own, outer, pack)


def lower_kernel(step, pos, back, base, *rest):
    known = rest[: STEPS - 2 - step]
    pack, value_out, message_out, tiles, inverse, sems = rest[STEPS - 2 - step :]
    later = list(range(step + 1, STEPS))
    first = pltpu.make_async_copy(
        pack.at[:, pl.ds(step * PIECE, PIECE), :], inverse, sems.at[len(later) * PER]
    )
    copies = []
    for at, block in enumerate(later):
        for place in range(PER):
            slot = at * PER + place
            copy = pltpu.make_async_copy(
                pack.at[pos[block * PER + place], pl.ds(LOWER_AT + step * TILE, TILE), :],
                tiles.at[slot],
                sems.at[slot],
            )
            copy.start()
            copies.append(copy)
    first.start()
    value = jnp.sum(back[...].astype(F32), axis=0).astype(BF)
    value_out[...] = value
    sums = jnp.zeros((ROWS, TILE), F32)
    for at in reversed(range(len(later))):
        solved = value if at == 0 else known[at - 1][...]
        for place in range(PER):
            slot = at * PER + place
            copies[slot].wait()
            product = dot_nt(solved, tiles[slot])
            sums = sums + jnp.where(place_mask(place), product, 0.0)
    sums = jnp.sum(sums.reshape(ROWS // PER, PER, TILE), axis=1, keepdims=True)
    sums = jnp.broadcast_to(sums, (ROWS // PER, PER, TILE)).reshape(ROWS, TILE)
    resid = (base[...] - sums).astype(BF)
    first.wait()
    part = lower_part(resid, inverse)
    for index in range(NP):
        message_out[index] = part


def lower_call(step, pos, back, base, known, pack):
    vmem = pl.BlockSpec(memory_space=pltpu.VMEM)
    count = (STEPS - 1 - step) * PER
    return pl.pallas_call(
        lambda *refs: lower_kernel(step, *refs),
        out_shape=(
            jax.ShapeDtypeStruct((ROWS, TILE), BF),
            jax.ShapeDtypeStruct((NP, ROWS, TILE), BF),
        ),
        in_specs=[pl.BlockSpec(memory_space=pltpu.SMEM), vmem, vmem]
        + [vmem] * len(known)
        + [pl.BlockSpec(memory_space=pl.ANY)],
        out_specs=(vmem, vmem),
        scratch_shapes=[
            pltpu.VMEM((count, TILE, TILE), BF),
            pltpu.VMEM((NC, PIECE, TILE), BF),
            pltpu.SemaphoreType.DMA((count + 1,)),
        ],
        compiler_params=pltpu.CompilerParams(vmem_limit_bytes=24 << 20),
        name=f"lower_block_{step}",
    )(pos, back, base, *known, pack)


def body(rhs, pivots, tile_of, upper_rows, upper_inv, lower_rows, lower_inv, solved):
    col = lax.axis_index("pcol")
    row = lax.axis_index("prow")
    z = col // NY
    count, width = rhs.shape
    slots = width // TILE
    rows_z = count // NY
    rows_own = count // NC
    first_tiles = tile_of.reshape(NC, slots)[:, 0]
    my_tile = first_tiles[col]
    my_block = my_tile // PER
    my_place = my_tile % PER
    plane_tiles = lax.dynamic_slice_in_dim(first_tiles, z * NY, NY)
    plane_blocks = plane_tiles // PER
    pos = jnp.sum(
        jnp.where(
            first_tiles[None, :] == jnp.arange(STEPS * PER)[:, None],
            jnp.arange(NC, dtype=jnp.int32)[None, :],
            0,
        ),
        axis=1,
        dtype=jnp.int32,
    )

    pack = jnp.concatenate(
        [
            jnp.swapaxes(lower_inv, 1, 2).reshape(STEPS * PIECE, TILE),
            upper_inv[STEPS - 1],
            lower_rows[: STEPS - 1, :, :TILE].reshape((STEPS - 1) * TILE, TILE),
        ],
        axis=0,
    )
    pack_all = lax.all_gather(pack, "pcol", axis=0)

    local_pivots = pivots - col * width
    own = jnp.take(rhs[:, :TILE], local_pivots[:TILE], axis=1)
    own = own.reshape(NZ, NY, rows_own, TILE).transpose(1, 0, 2, 3).reshape(NY, rows_z, TILE)
    own_high = own.astype(BF)
    own_low = (own - own_high.astype(F32)).astype(BF)
    got = swap_y(jnp.concatenate([own_high, own_low, to_all(upper_inv[0], NY)], axis=1))
    tiles = got[:, :rows_z].astype(F32) + got[:, rows_z : 2 * rows_z].astype(F32)
    inverse = [got[:, 2 * rows_z :].reshape(TILE, TILE)]

    slot_known = jnp.where(my_block >= STEPS, solved[:, :TILE], 0.0)
    known = jnp.concatenate([slot_known, solved[:, TILE:]], axis=1).astype(BF)
    outer = lax.dot_general(
        known, lower_rows, (((1,), (2,)), ((), ())), preferred_element_type=F32
    )
    outer = outer.astype(BF).reshape(NZ, NY, rows_own, STEPS, TILE).transpose(1, 0, 2, 3, 4)
    outer = outer.reshape(NY, NZ * rows_own * STEPS, TILE)
    upper_pack = jnp.concatenate(
        [upper_rows[: STEPS - 1, :, :TILE].reshape((STEPS - 1) * TILE, TILE), upper_inv[1]], axis=0
    )
    got = swap_y(jnp.concatenate([to_all(upper_pack, NY), outer], axis=1))
    upper_tiles = [got[:, step * TILE : (step + 1) * TILE] for step in range(STEPS - 1)]
    at = (STEPS - 1) * TILE
    inverse.append(got[:, at : at + PIECE].reshape(TILE, TILE))
    outer = total(got[:, at + PIECE :]).astype(BF).reshape(NZ, rows_own * STEPS, TILE)

    finished = []
    for step in range(STEPS - 1):
        block = tiles.astype(BF)
        pick = plane_tiles[None, :] == step * PER + jnp.arange(NZ)[:, None]
        routed = jnp.sum(jnp.where(pick[:, :, None, None], block[None], 0), axis=1)
        mine = jnp.sum(swap_z(routed), axis=0)
        part = jnp.dot(mine, inverse[step], preferred_element_type=F32).astype(BF)
        message = to_all(part, NZ)
        if step == 1:
            message = jnp.concatenate([message, outer], axis=1)
        back = total(swap_z(message))
        solved_rows = back[:rows_z].astype(BF)
        if step == 1:
            outer = back[rows_z:].reshape(rows_own, STEPS, TILE)
        finished.append(solved_rows)
        update = lax.dot_general(
            solved_rows, upper_tiles[step], (((1,), (1,)), ((), ())), preferred_element_type=F32
        )
        update = total(swap_prow(to_all(update.astype(BF), NP)))
        update = update.transpose(1, 0, 2)
        tiles = tiles - jnp.where((plane_blocks > step)[:, None, None], update, 0.0)

    got = swap_z(to_all(tiles.astype(BF), NZ).reshape(NZ * NY, rows_z, TILE))
    order = jnp.arange(ROWS)
    pick_own = (
        (order[None, :] // rows_own == z) & (order[None, :] % rows_own == order[:, None] // PER)
    ).astype(BF)
    outer = jnp.repeat(outer.transpose(1, 0, 2), PER, axis=1)
    last, message = last_call(pos, got, pick_own, outer[STEPS - 1], pack_all)
    finished.append(last)
    bases = [
        jnp.dot(pick_own, finished[step], preferred_element_type=F32) - outer[step]
        for step in range(STEPS - 1)
    ]

    stacked, message = lax.optimization_barrier((jnp.concatenate(finished, axis=0), message))
    every = swap_y(to_all(stacked, NY)).reshape(NY, STEPS, NZ, rows_own, TILE)
    every = every.transpose(1, 2, 0, 3, 4).reshape(STEPS, count, TILE)
    bulk = jnp.dot(
        jnp.concatenate(list(every), axis=1),
        upper_rows.reshape(STEPS * TILE, width),
        preferred_element_type=F32,
    )
    window_value = jnp.where(
        my_place == row, lax.dynamic_index_in_dim(every, jnp.minimum(my_block, STEPS - 1), 0, False), 0
    ).astype(F32)
    slot_bulk = jnp.where(my_block < STEPS, window_value, bulk[:, :TILE])
    bulk = jnp.concatenate([slot_bulk, bulk[:, TILE:]], axis=1).astype(BF)
    bulk = bulk.reshape(NP, count // NP * slots, TILE)

    back = swap_prow(message)
    last, message = lower_call(1, pos, back, bases[1], [], pack_all)
    back = swap_prow(jnp.concatenate([message, bulk], axis=1))
    bulk = total(back[:, ROWS:]).astype(BF)
    middle, message = lower_call(0, pos, back[:, :ROWS], bases[0], [last], pack_all)
    back = swap_prow(jnp.concatenate([message, to_all(bulk, NP)], axis=1))
    bulk = back[:, ROWS:].reshape(count, width).astype(F32)
    first = total(back[:, :ROWS]).astype(BF)

    window = jnp.concatenate([first, middle, last], axis=0)
    window = window.reshape(STEPS, rows_own, PER, TILE).transpose(0, 2, 1, 3)
    window = swap_pcol(choose(window.reshape(STEPS * PER, rows_own, TILE), first_tiles))
    window = window.reshape(count, TILE).astype(F32)
    slot_solution = jnp.where(my_block < STEPS, window, solved[:, :TILE])
    backward = jnp.concatenate([slot_solution, solved[:, TILE:]], axis=1)
    state0 = jnp.take(rhs, local_pivots, axis=1)
    slot_forward = jnp.where(my_block < STEPS, bulk[:, :TILE], state0[:, :TILE] - bulk[:, :TILE])
    forward = jnp.concatenate([slot_forward, state0[:, TILE:] - bulk[:, TILE:]], axis=1)
    return (forward, backward)


def solution(mesh):
    return jax.shard_map(
        body,
        mesh=mesh,
        in_specs=(
            P(None, "pcol"),
            P("pcol"),
            P(),
            P(None, "prow", "pcol"),
            P(None, "pcol", "prow"),
            P(None, "prow", "pcol"),
            P(None, "prow", "pcol"),
            P(None, "pcol"),
        ),
        out_specs=(P(None, "pcol"), P(None, "pcol")),
        check_vma=False,
    )
```

time: 249 us -> 245 us (0.984)
  blocking collectives: 36.2 us -> 0 us
  starting transfers between devices: 59.4 us -> 79.3 us
  waiting for transfers between devices: 72.7 us -> 87.1 us
  Pallas kernels: 0 us -> 13.3 us
  matrix products: 19.3 us -> 6.72 us
  other arithmetic: 20.2 us -> 9.91 us
  local copies, waits for them, and re-layouts: 22 us -> 30.4 us
    all_to_all x3 -> x0, blocking collectives: 36.2 us -> none  [the longest x2 22.7 us: swap_z(): lax.all_to_all(x, 'pcol', 0, 0, axis_index_groups=Z_GROUPS, tiled=True)]
    all_to_all x4 -> x5, starting transfers between devices: 24.4 us -> 40.7 us  [swap_prow(): return lax.all_to_all(x, 'prow', 0, 0, tiled=True)]
    all_to_all x4 -> x5, waiting for transfers between devices: 24.3 us -> 40.2 us  [swap_z(): lax.all_to_all(x, 'pcol', 0, 0, axis_index_groups=Z_GROUPS, tiled=True)]
    pallas_call x0 -> x3, Pallas kernels: none -> 13.3 us  [the longest x2 10.9 us: lower_call(): pl.pallas_call(lambda *refs: lower_kernel(step, *refs), out_shape=(jax.Sh...]
    unnamed x28 -> x16, local copies, waits for them, and re-layouts: 2.16 us -> 15.2 us
    dot_general x4 -> x2, matrix products: 12.2 us -> 0.38 us  [body(): jnp.dot(pick_own, finished[step], preferred_element_type=F32) - outer[step]]
    all_to_all x2 -> x3, waiting for transfers between devices: 20.6 us -> 12.9 us  [swap_y(): lax.all_to_all(x, 'pcol', 0, 0, axis_index_groups=Y_GROUPS, tiled=True)]
    all_to_all x4 -> x5, waiting for transfers between devices: 19.9 us -> 26.1 us  [swap_prow(): return lax.all_to_all(x, 'prow', 0, 0, tiled=True)]
  transfers between devices with their start and end apart: 12 -> 15, of which waited for: 10 -> 12; matrix products, arithmetic and copies ran while one was open for 17% -> 9% of each run, Pallas kernels for 0% -> 2%
where the time goes in v2:
time: 245 us; the launch traced here: 244 us
  waiting for transfers between devices  87.1 us (36%)
  starting transfers between devices  79.3 us (32%)
  local copies, waits for them, and re-layouts  30.4 us (12%)
  between operations  16.9 us (7%)
  Pallas kernels  13.3 us (5%)
  other arithmetic  9.91 us (4%)
  matrix products  6.72 us (3%)
    all_to_all x5, starting transfers between devices, swap_prow(): return lax.all_to_all(x, 'prow', 0, 0, tiled=True)  40.7 us
    all_to_all x5, waiting for transfers between devices, swap_z(): lax.all_to_all(x, 'pcol', 0, 0, axis_index_groups=Z_GROUPS, tiled=True)  40.2 us
    all_to_all x5, waiting for transfers between devices, swap_prow(): return lax.all_to_all(x, 'prow', 0, 0, tiled=True)  26.1 us
    all_to_all x5, starting transfers between devices, swap_z(): lax.all_to_all(x, 'pcol', 0, 0, axis_index_groups=Z_GROUPS, tiled=True)  21.7 us
    unnamed x16, local copies, waits for them, and re-layouts  15.2 us
    all_to_all x3, waiting for transfers between devices, swap_y(): lax.all_to_all(x, 'pcol', 0, 0, axis_index_groups=Y_GROUPS, tiled=True)  12.9 us
    all_to_all x3, starting transfers between devices, swap_y(): lax.all_to_all(x, 'pcol', 0, 0, axis_index_groups=Y_GROUPS, tiled=True)  12 us
    pallas_call x2, Pallas kernels, lower_call(): pl.pallas_call(lambda *refs: lower_kernel(step, *refs), out_shape=(jax.Sh...  10.9 us
  transfers between devices with their start and end apart: 15, of which 12 were waited for; matrix products, arithmetic and copies ran while one was open for 9% of the time, Pallas kernels for 2%

profile of v2, /device:TPU:1, one launch (start us, length us, event | category | flops | bytes accessed | tf_op | source)
XLA Modules:
  0.0 243.6 jit_solution(2067941201983566578)
XLA Ops:
  13.9 5.0 %all-to-all-start = ((bf16[4,96,256]{2,1,0:T(8,128)(2,1)}), bf16[4,96,256]{2,1,0:T(8,128)(2,1)S(1)}, u32[]{:S(2)}, u32[]{:S(2)}) async-start(bf16[4,96,256]{2,1,0:T(8,128)(2,1)} %pad_maximum_fusion.8), calls=%async_computation | async-start | bytes 393216 | tf_op jit(solution)/shard_map/all_to_all | solution.py:28
  26.9 8.2 %all-to-all-start.1 = ((bf16[8,16,256]{2,1,0:T(8,128)(2,1)}), bf16[8,16,256]{2,1,0:T(8,128)(2,1)S(1)}, u32[]{:S(2)}, u32[]{:S(2)}) async-start(bf16[8,16,256]{2,1,0:T(8,128)(2,1)} %select_reduce_fusion.1), calls=%async_computation.1 | async-start | bytes 131072 | tf_op jit(solution)/shard_map/all_to_all | solution.py:32
  35.2 7.6 %all-to-all-done.1 = bf16[8,16,256]{2,1,0:T(8,128)(2,1)S(1)} async-done(((bf16[8,16,256]{2,1,0:T(8,128)(2,1)}), bf16[8,16,256]{2,1,0:T(8,128)(2,1)S(1)}, u32[]{:S(2)}, u32[]{:S(2)}) %all-to-all-start.1) | async-done | bytes 65568 | tf_op jit(solution)/shard_map/all_to_all | solution.py:32
  48.2 6.3 %all-to-all-done.2 = bf16[8,16,256]{2,1,0:T(8,128)(2,1)S(1)} async-done(((bf16[8,16,256]{2,1,0:T(8,128)(2,1)}), bf16[8,16,256]{2,1,0:T(8,128)(2,1)S(1)}, u32[]{:S(2)}, u32[]{:S(2)}) %all-to-all-start.2) | async-done | bytes 65568 | tf_op jit(solution)/shard_map/all_to_all | solution.py:32
  58.3 12.9 %all-to-all-done.3 = bf16[4,624,256]{2,1,0:T(8,128)(2,1)S(1)} async-done(((bf16[4,624,256]{2,1,0:T(8,128)(2,1)}), bf16[4,624,256]{2,1,0:T(8,128)(2,1)S(1)}, u32[]{:S(2)}, u32[]{:S(2)}) %all-to-all-start.3) | async-done | bytes 1277984 | tf_op jit(solution)/shard_map/all_to_all | solution.py:28
  72.1 19.6 %all-to-all-start.4 = ((bf16[8,16,4,256]{3,1,2,0:T(8,128)(2,1)}), bf16[8,16,4,256]{3,1,2,0:T(8,128)(2,1)S(1)}, u32[]{:S(2)}, u32[]{:S(2)}) async-start(bf16[8,16,4,256]{3,1,2,0:T(8,128)(2,1)} %broadcast_in_dim.192), calls=%async_computation.4 | async-start | bytes 524288 | tf_op jit(solution)/shard_map/all_to_all | solution.py:40
  91.8 6.5 %all-to-all-done.4 = bf16[8,16,4,256]{3,1,2,0:T(8,128)(2,1)S(1)} async-done(((bf16[8,16,4,256]{3,1,2,0:T(8,128)(2,1)}), bf16[8,16,4,256]{3,1,2,0:T(8,128)(2,1)S(1)}, u32[]{:S(2)}, u32[]{:S(2)}) %all-to-all-start.4) | async-done | bytes 262176 | tf_op jit(solution)/shard_map/all_to_all | solution.py:40
  102.6 7.8 %all-to-all-done.5 = bf16[8,16,256]{2,1,0:T(8,128)(2,1)S(1)} async-done(((bf16[8,16,256]{2,1,0:T(8,128)(2,1)}), bf16[8,16,256]{2,1,0:T(8,128)(2,1)S(1)}, u32[]{:S(2)}, u32[]{:S(2)}) %all-to-all-start.5) | async-done | bytes 65568 | tf_op jit(solution)/shard_map/all_to_all | solution.py:32
  114.5 8.5 %all-to-all-done.6 = bf16[8,22,256]{2,1,0:T(8,128)(2,1)S(1)} async-done(((bf16[8,22,256]{2,1,0:T(8,128)(2,1)}), bf16[8,22,256]{2,1,0:T(8,128)(2,1)S(1)}, u32[]{:S(2)}, u32[]{:S(2)}) %all-to-all-start.6) | async-done | bytes 90144 | tf_op jit(solution)/shard_map/all_to_all | solution.py:32
  124.0 6.6 %all-to-all-start.7 = ((bf16[8,16,4,256]{3,1,2,0:T(8,128)(2,1)}), bf16[8,16,4,256]{3,1,2,0:T(8,128)(2,1)S(1)}, u32[]{:S(2)}, u32[]{:S(2)}) async-start(bf16[8,16,4,256]{3,1,2,0:T(8,128)(2,1)} %broadcast_in_dim.197), calls=%async_computation.7 | async-start | bytes 524288 | tf_op jit(solution)/shard_map/all_to_all | solution.py:40
  130.8 6.5 %all-to-all-done.7 = bf16[8,16,4,256]{3,1,2,0:T(8,128)(2,1)S(1)} async-done(((bf16[8,16,4,256]{3,1,2,0:T(8,128)(2,1)}), bf16[8,16,4,256]{3,1,2,0:T(8,128)(2,1)S(1)}, u32[]{:S(2)}, u32[]{:S(2)}) %all-to-all-start.7) | async-done | bytes 262176 | tf_op jit(solution)/shard_map/all_to_all | solution.py:40
  141.7 10.0 %all-to-all-done.8.got = bf16[32,16,256]{2,1,0:T(8,128)(2,1)S(1)} async-done(((bf16[32,16,256]{2,1,0:T(8,128)(2,1)}), bf16[32,16,256]{2,1,0:T(8,128)(2,1)S(1)}, u32[]{:S(2)}, u32[]{:S(2)}) %all-to-all-start.8) | async-done | bytes 262176 | tf_op jit(solution)/shard_map/all_to_all | solution.py:32
  151.7 4.6 %copy-done = bf16[24576,256]{1,0:T(8,128)(2,1)S(1)} copy-done((bf16[24576,256]{1,0:T(8,128)(2,1)S(1)}, bf16[24576,256]{1,0:T(8,128)(2,1)}, u32[]{:S(2)}) %copy-start) | copy-done | bytes 12582936
  158.6 5.8 %all-to-all-start.9 = ((bf16[8,16,256]{2,1,0:T(8,128)(2,1)}), bf16[8,16,256]{2,1,0:T(8,128)(2,1)S(1)}, u32[]{:S(2)}, u32[]{:S(2)}) async-start(bf16[8,16,256]{2,1,0:T(8,128)(2,1)} %get-tuple-element.12), calls=%async_computation.9 | async-start | bytes 131072 | tf_op jit(solution)/shard_map/all_to_all | solution.py:40
  164.5 4.9 %all-to-all-done.9.refs_1_ = bf16[8,16,256]{2,1,0:T(8,128)(2,1)S(1)} async-done(((bf16[8,16,256]{2,1,0:T(8,128)(2,1)}), bf16[8,16,256]{2,1,0:T(8,128)(2,1)S(1)}, u32[]{:S(2)}, u32[]{:S(2)}) %all-to-all-start.9) | async-done | bytes 65568 | tf_op jit(solution)/shard_map/all_to_all | solution.py:40
  173.5 4.6 %copy-done.1 = bf16[24576,256]{1,0:T(8,128)(2,1)S(1)} copy-done((bf16[24576,256]{1,0:T(8,128)(2,1)S(1)}, bf16[24576,256]{1,0:T(8,128)(2,1)}, u32[]{:S(2)}) %copy-start.1) | copy-done | bytes 12582936
  186.0 4.1 %all-to-all-start.11 = ((bf16[8,80,256]{2,1,0:T(8,128)(2,1)}), bf16[8,80,256]{2,1,0:T(8,128)(2,1)S(1)}, u32[]{:S(2)}, u32[]{:S(2)}) async-start(bf16[8,80,256]{2,1,0:T(8,128)(2,1)} %pad_maximum_fusion.4), calls=%async_computation.11 | async-start | bytes 655360 | tf_op jit(solution)/shard_map/all_to_all | solution.py:40
  190.1 5.5 %gather_fusion.1 = f32[2048,64]{1,0:T(8,128)S(1)} fusion(f32[64,2048]{0,1:T(8,128)S(1)} %copy.89, s32[2048]{0:T(1024)S(1)} %fusion.17), kind=kCustom, calls=%fused_computation.1 | custom fusion | bytes 1056768 | tf_op jit(solution)/shard_map/jit(_take)/gather | solution.py:311
  197.3 4.6 %copy-done.2 = bf16[24576,256]{1,0:T(8,128)(2,1)S(1)} copy-done((bf16[24576,256]{1,0:T(8,128)(2,1)S(1)}, bf16[24576,256]{1,0:T(8,128)(2,1)}, u32[]{:S(2)}) %copy-start.2) | copy-done | bytes 12582936
  201.8 6.9 %lower_block_0.1 = (bf16[16,256]{1,0:T(8,128)(2,1)S(1)}, bf16[8,16,256]{2,1,0:T(8,128)(2,1)S(1)}) custom-call(s32[24]{0:T(128)S(1)} %select_reduce_fusion.2.pos.refs_0_, bf16[8,16,256]{2,1,0:T(8,128)(2,1)S(1)} %slice.171.refs_1_, f32[16,256]{1,0:T(8,128)S(1)} %convolution_subtract_fusion.refs_2_, bf16[16,256]{1,0:T(8,128)(2,1)S(1)} %get-tuple-element.15.refs_3_, ...), custom_call_target="tpu_custom_call" | custom-call | tf_op jit(solution)/shard_map/lower_block_0/pallas_call | solution.py:167
  209.6 4.5 %all-to-all-start.12 = ((bf16[8,80,256]{2,1,0:T(8,128)(2,1)}), bf16[8,80,256]{2,1,0:T(8,128)(2,1)S(1)}, u32[]{:S(2)}, u32[]{:S(2)}) async-start(bf16[8,80,256]{2,1,0:T(8,128)(2,1)} %pad_maximum_fusion.5), calls=%async_computation.12 | async-start | bytes 655360 | tf_op jit(solution)/shard_map/all_to_all | solution.py:40
  214.1 7.1 %all-to-all-done.12 = bf16[8,80,256]{2,1,0:T(8,128)(2,1)S(1)} async-done(((bf16[8,80,256]{2,1,0:T(8,128)(2,1)}), bf16[8,80,256]{2,1,0:T(8,128)(2,1)S(1)}, u32[]{:S(2)}, u32[]{:S(2)}) %all-to-all-start.12) | async-done | bytes 327712 | tf_op jit(solution)/shard_map/all_to_all | solution.py:40
  222.3 4.9 %all-to-all-start.13 = ((bf16[32,2,256]{2,1,0:T(2,128)(2,1)}), bf16[32,2,256]{2,1,0:T(2,128)(2,1)S(1)}, u32[]{:S(2)}, u32[]{:S(2)}) async-start(bf16[32,2,256]{2,1,0:T(2,128)(2,1)} %reshape.318), calls=%async_computation.13 | async-start | bytes 65536 | tf_op jit(solution)/shard_map/all_to_all | solution.py:36
  228.0 7.9 %all-to-all-done.13 = bf16[32,2,256]{2,1,0:T(2,128)(2,1)S(1)} async-done(((bf16[32,2,256]{2,1,0:T(2,128)(2,1)}), bf16[32,2,256]{2,1,0:T(2,128)(2,1)S(1)}, u32[]{:S(2)}, u32[]{:S(2)}) %all-to-all-start.13) | async-done | bytes 32800 | tf_op jit(solution)/shard_map/all_to_all | solution.py:36
  (137 shorter events, 55.9 us)
Async XLA Ops:
  7.2 5.0 %copy-start.4 = (s32[2048]{0:T(1024)S(1)}, s32[2048]{0:T(1024)}, u32[]{:S(2)}) copy-start(s32[2048]{0:T(1024)} %param.9) | copy-start | bytes 24580
  7.2 144.5 %all-gather.3.cloned.1.call-start = ((), (), s32[]{:S(2)}) async-start(), calls=%async_computation.14 | async-start | bytes 12976128 | tf_op jit(solution)/shard_map/all_gather | solution.py:219
  9.0 9.9 %copy-start.5 = (s32[256]{0:T(256)S(1)}, s32[256]{0:T(256)}, u32[]{:S(2)}) copy-start(s32[256]{0:T(256)} %param.10) | copy-start | bytes 3076
  10.7 11.3 %copy-start.3 = (f32[64,2048]{1,0:T(8,128)S(1)}, f32[64,2048]{1,0:T(8,128)}, u32[]{:S(2)}) copy-start(f32[64,2048]{1,0:T(8,128)} %param.15) | copy-start | bytes 1572868
  13.9 12.3 %all-to-all-start = ((bf16[4,96,256]{2,1,0:T(8,128)(2,1)}), bf16[4,96,256]{2,1,0:T(8,128)(2,1)S(1)}, u32[]{:S(2)}, u32[]{:S(2)}) async-start(bf16[4,96,256]{2,1,0:T(8,128)(2,1)} %pad_maximum_fusion.8), calls=%async_computation | async-start | bytes 393216 | tf_op jit(solution)/shard_map/all_to_all | solution.py:28
  26.9 15.8 %all-to-all-start.1 = ((bf16[8,16,256]{2,1,0:T(8,128)(2,1)}), bf16[8,16,256]{2,1,0:T(8,128)(2,1)S(1)}, u32[]{:S(2)}, u32[]{:S(2)}) async-start(bf16[8,16,256]{2,1,0:T(8,128)(2,1)} %select_reduce_fusion.1), calls=%async_computation.1 | async-start | bytes 131072 | tf_op jit(solution)/shard_map/all_to_all | solution.py:32
  43.6 11.0 %all-to-all-start.2 = ((bf16[8,16,256]{2,1,0:T(8,128)(2,1)}), bf16[8,16,256]{2,1,0:T(8,128)(2,1)S(1)}, u32[]{:S(2)}, u32[]{:S(2)}) async-start(bf16[8,16,256]{2,1,0:T(8,128)(2,1)} %broadcast_in_dim.187), calls=%async_computation.2 | async-start | bytes 131072 | tf_op jit(solution)/shard_map/all_to_all | solution.py:32
  54.5 16.7 %all-to-all-start.3 = ((bf16[4,624,256]{2,1,0:T(8,128)(2,1)}), bf16[4,624,256]{2,1,0:T(8,128)(2,1)S(1)}, u32[]{:S(2)}, u32[]{:S(2)}) async-start(bf16[4,624,256]{2,1,0:T(8,128)(2,1)} %pad_maximum_fusion), calls=%async_computation.3 | async-start | bytes 2555904 | tf_op jit(solution)/shard_map/all_to_all | solution.py:28
  72.1 26.2 %all-to-all-start.4 = ((bf16[8,16,4,256]{3,1,2,0:T(8,128)(2,1)}), bf16[8,16,4,256]{3,1,2,0:T(8,128)(2,1)S(1)}, u32[]{:S(2)}, u32[]{:S(2)}) async-start(bf16[8,16,4,256]{3,1,2,0:T(8,128)(2,1)} %broadcast_in_dim.192), calls=%async_computation.4 | async-start | bytes 524288 | tf_op jit(solution)/shard_map/all_to_all | solution.py:40
  99.2 11.2 %all-to-all-start.5 = ((bf16[8,16,256]{2,1,0:T(8,128)(2,1)}), bf16[8,16,256]{2,1,0:T(8,128)(2,1)S(1)}, u32[]{:S(2)}, u32[]{:S(2)}) async-start(bf16[8,16,256]{2,1,0:T(8,128)(2,1)} %select_reduce_fusion), calls=%async_computation.5 | async-start | bytes 131072 | tf_op jit(solution)/shard_map/all_to_all | solution.py:32
  111.2 11.9 %all-to-all-start.6 = ((bf16[8,22,256]{2,1,0:T(8,128)(2,1)}), bf16[8,22,256]{2,1,0:T(8,128)(2,1)S(1)}, u32[]{:S(2)}, u32[]{:S(2)}) async-start(bf16[8,22,256]{2,1,0:T(8,128)(2,1)} %pad_maximum_fusion.9), calls=%async_computation.6 | async-start | bytes 196608 | tf_op jit(solution)/shard_map/all_to_all | solution.py:32
  124.0 13.2 %all-to-all-start.7 = ((bf16[8,16,4,256]{3,1,2,0:T(8,128)(2,1)}), bf16[8,16,4,256]{3,1,2,0:T(8,128)(2,1)S(1)}, u32[]{:S(2)}, u32[]{:S(2)}) async-start(bf16[8,16,4,256]{3,1,2,0:T(8,128)(2,1)} %broadcast_in_dim.197), calls=%async_computation.7 | async-start | bytes 524288 | tf_op jit(solution)/shard_map/all_to_all | solution.py:40
  138.1 13.6 %all-to-all-start.8 = ((bf16[32,16,256]{2,1,0:T(8,128)(2,1)}), bf16[32,16,256]{2,1,0:T(8,128)(2,1)S(1)}, u32[]{:S(2)}, u32[]{:S(2)}) async-start(bf16[32,16,256]{2,1,0:T(8,128)(2,1)} %bitcast.16), calls=%async_computation.8 | async-start | bytes 524288 | tf_op jit(solution)/shard_map/all_to_all | solution.py:32
  151.7 4.6 %copy-start = (bf16[24576,256]{1,0:T(8,128)(2,1)S(1)}, bf16[24576,256]{1,0:T(8,128)(2,1)}, u32[]{:S(2)}) copy-start(bf16[24576,256]{1,0:T(8,128)(2,1)} %all-gather.3.cloned.1.call-done) | copy-start | bytes 37748740
  158.6 10.7 %all-to-all-start.9 = ((bf16[8,16,256]{2,1,0:T(8,128)(2,1)}), bf16[8,16,256]{2,1,0:T(8,128)(2,1)S(1)}, u32[]{:S(2)}, u32[]{:S(2)}) async-start(bf16[8,16,256]{2,1,0:T(8,128)(2,1)} %get-tuple-element.12), calls=%async_computation.9 | async-start | bytes 131072 | tf_op jit(solution)/shard_map/all_to_all | solution.py:40
  170.0 12.1 %all-to-all-start.10 = ((bf16[4,48,256]{2,1,0:T(8,128)(2,1)}), bf16[4,48,256]{2,1,0:T(8,128)(2,1)S(1)}, u32[]{:S(2)}, u32[]{:S(2)}) async-start(bf16[4,48,256]{2,1,0:T(8,128)(2,1)} %broadcast_in_dim.203), calls=%async_computation.10 | async-start | bytes 196608 | tf_op jit(solution)/shard_map/all_to_all | solution.py:28
  173.5 4.6 %copy-start.1 = (bf16[24576,256]{1,0:T(8,128)(2,1)S(1)}, bf16[24576,256]{1,0:T(8,128)(2,1)}, u32[]{:S(2)}) copy-start(bf16[24576,256]{1,0:T(8,128)(2,1)} %all-gather.3.cloned.1.call-done) | copy-start | bytes 37748740
  186.0 11.2 %all-to-all-start.11 = ((bf16[8,80,256]{2,1,0:T(8,128)(2,1)}), bf16[8,80,256]{2,1,0:T(8,128)(2,1)S(1)}, u32[]{:S(2)}, u32[]{:S(2)}) async-start(bf16[8,80,256]{2,1,0:T(8,128)(2,1)} %pad_maximum_fusion.4), calls=%async_computation.11 | async-start | bytes 655360 | tf_op jit(solution)/shard_map/all_to_all | solution.py:40
  197.3 4.6 %copy-start.2 = (bf16[24576,256]{1,0:T(8,128)(2,1)S(1)}, bf16[24576,256]{1,0:T(8,128)(2,1)}, u32[]{:S(2)}) copy-start(bf16[24576,256]{1,0:T(8,128)(2,1)} %all-gather.3.cloned.1.call-done) | copy-start | bytes 37748740
  209.6 11.6 %all-to-all-start.12 = ((bf16[8,80,256]{2,1,0:T(8,128)(2,1)}), bf16[8,80,256]{2,1,0:T(8,128)(2,1)S(1)}, u32[]{:S(2)}, u32[]{:S(2)}) async-start(bf16[8,80,256]{2,1,0:T(8,128)(2,1)} %pad_maximum_fusion.5), calls=%async_computation.12 | async-start | bytes 655360 | tf_op jit(solution)/shard_map/all_to_all | solution.py:40
  214.1 21.8 %slice-start = ((f32[64,2048]{1,0:T(8,128)}), f32[64,1792]{1,0:T(8,128)S(1)}, s32[]{:S(2)}) async-start(f32[64,2048]{1,0:T(8,128)} %param.15), calls=%async_computation.15 | async-start | bytes 917504 | tf_op jit(solution)/shard_map/slice | solution.py:231
  222.3 13.6 %all-to-all-start.13 = ((bf16[32,2,256]{2,1,0:T(2,128)(2,1)}), bf16[32,2,256]{2,1,0:T(2,128)(2,1)S(1)}, u32[]{:S(2)}, u32[]{:S(2)}) async-start(bf16[32,2,256]{2,1,0:T(2,128)(2,1)} %reshape.318), calls=%async_computation.13 | async-start | bytes 65536 | tf_op jit(solution)/shard_map/all_to_all | solution.py:36
Sparse Core Ops, SparseCore 0:
  11.2 130.1 all-gather.2

commit v3 on v2

--- a/solution.py
+++ b/solution.py
@@ -28,6 +28,10 @@
     return lax.all_to_all(x, "pcol", 0, 0, axis_index_groups=Y_GROUPS, tiled=True)
 
 
+def pass_y(x, step):
+    return lax.ppermute(x, "pcol", [(at, at ^ step) for at in range(NC)])
+
+
 def swap_z(x):
     return lax.all_to_all(x, "pcol", 0, 0, axis_index_groups=Z_GROUPS, tiled=True)
 
@@ -67,10 +71,10 @@
 
 
 def lower_part(resid, inverse):
-    part = jnp.zeros((ROWS, TILE), F32)
-    for place in range(PER):
-        weights = inverse[4 * place : 4 * place + 4].reshape(TILE, TILE)
-        part = jnp.where(place_mask(place), dot_nt(resid, weights), part)
+    full = dot_nt(resid, inverse[...].reshape(NB, TILE))
+    part = full[:, :TILE]
+    for place in range(1, PER):
+        part = jnp.where(place_mask(place), full[:, place * TILE : (place + 1) * TILE], part)
     return part.astype(BF)
 
 
@@ -84,11 +88,8 @@
     for copy in copies:
         copy.start()
     copies[0].wait()
-    value = jnp.zeros((ROWS, TILE), F32)
-    for place in range(PER):
-        weights = upper[4 * place : 4 * place + 4].reshape(TILE, TILE)
-        value = value + dot_nn(got[pos[(STEPS - 1) * PER + place]], weights)
-    value = value.astype(BF)
+    block = jnp.concatenate([got[pos[place]] for place in range(PER)], axis=1)
+    value = dot_nn(block, upper[...].reshape(NB, TILE)).astype(BF)
     solved_out[...] = value
     resid = (dot_nn(pick_own[...], value) - outer[...]).astype(BF)
     copies[1].wait()
@@ -110,7 +111,7 @@
             vmem,
             vmem,
             vmem,
-            pl.BlockSpec(memory_space=pl.ANY),
+            pl.BlockSpec(memory_space=pltpu.HBM),
         ],
         out_specs=(vmem, vmem),
         scratch_shapes=[
@@ -136,7 +137,7 @@
             slot = at * PER + place
             copy = pltpu.make_async_copy(
                 pack.at[pos[block * PER + place], pl.ds(LOWER_AT + step * TILE, TILE), :],
-                tiles.at[slot],
+                tiles.at[at, :, pl.ds(place * TILE, TILE)],
                 sems.at[slot],
             )
             copy.start()
@@ -147,11 +148,13 @@
     sums = jnp.zeros((ROWS, TILE), F32)
     for at in reversed(range(len(later))):
         solved = value if at == 0 else known[at - 1][...]
+        wide = jnp.concatenate(
+            [jnp.where(place_mask(place), solved, jnp.zeros_like(solved)) for place in range(PER)],
+            axis=1,
+        )
         for place in range(PER):
-            slot = at * PER + place
-            copies[slot].wait()
-            product = dot_nt(solved, tiles[slot])
-            sums = sums + jnp.where(place_mask(place), product, 0.0)
+            copies[at * PER + place].wait()
+        sums = sums + dot_nt(wide, tiles[at])
     sums = jnp.sum(sums.reshape(ROWS // PER, PER, TILE), axis=1, keepdims=True)
     sums = jnp.broadcast_to(sums, (ROWS // PER, PER, TILE)).reshape(ROWS, TILE)
     resid = (base[...] - sums).astype(BF)
@@ -163,7 +166,8 @@
 
 def lower_call(step, pos, back, base, known, pack):
     vmem = pl.BlockSpec(memory_space=pltpu.VMEM)
-    count = (STEPS - 1 - step) * PER
+    later = STEPS - 1 - step
+    count = later * PER
     return pl.pallas_call(
         lambda *refs: lower_kernel(step, *refs),
         out_shape=(
@@ -172,10 +176,10 @@
         ),
         in_specs=[pl.BlockSpec(memory_space=pltpu.SMEM), vmem, vmem]
         + [vmem] * len(known)
-        + [pl.BlockSpec(memory_space=pl.ANY)],
+        + [pl.BlockSpec(memory_space=pltpu.HBM)],
         out_specs=(vmem, vmem),
         scratch_shapes=[
-            pltpu.VMEM((count, TILE, TILE), BF),
+            pltpu.VMEM((later, TILE, NB), BF),
             pltpu.VMEM((NC, PIECE, TILE), BF),
             pltpu.SemaphoreType.DMA((count + 1,)),
         ],
@@ -188,6 +192,7 @@
     col = lax.axis_index("pcol")
     row = lax.axis_index("prow")
     z = col // NY
+    y = col % NY
     count, width = rhs.shape
     slots = width // TILE
     rows_z = count // NY
@@ -196,7 +201,7 @@
     my_tile = first_tiles[col]
     my_block = my_tile // PER
     my_place = my_tile % PER
-    plane_tiles = lax.dynamic_slice_in_dim(first_tiles, z * NY, NY)
+    plane_tiles = jnp.stack([first_tiles[z * NY + (y ^ step)] for step in range(NY)])
     plane_blocks = plane_tiles // PER
     pos = jnp.sum(
         jnp.where(
@@ -223,9 +228,16 @@
     own = own.reshape(NZ, NY, rows_own, TILE).transpose(1, 0, 2, 3).reshape(NY, rows_z, TILE)
     own_high = own.astype(BF)
     own_low = (own - own_high.astype(F32)).astype(BF)
-    got = swap_y(jnp.concatenate([own_high, own_low, to_all(upper_inv[0], NY)], axis=1))
+    first_inverses = upper_inv[: STEPS - 1].reshape((STEPS - 1) * PIECE, TILE)
+    got = swap_y(jnp.concatenate([own_high, own_low, to_all(first_inverses, NY)], axis=1))
     tiles = got[:, :rows_z].astype(F32) + got[:, rows_z : 2 * rows_z].astype(F32)
-    inverse = [got[:, 2 * rows_z :].reshape(TILE, TILE)]
+    tiles = jnp.stack(
+        [lax.dynamic_index_in_dim(tiles, y ^ step, 0, False) for step in range(NY)]
+    )
+    inverse = []
+    for step in range(STEPS - 1):
+        start = 2 * rows_z + step * PIECE
+        inverse.append(got[:, start : start + PIECE].reshape(TILE, TILE))
 
     slot_known = jnp.where(my_block >= STEPS, solved[:, :TILE], 0.0)
     known = jnp.concatenate([slot_known, solved[:, TILE:]], axis=1).astype(BF)
@@ -234,14 +246,19 @@
     )
     outer = outer.astype(BF).reshape(NZ, NY, rows_own, STEPS, TILE).transpose(1, 0, 2, 3, 4)
     outer = outer.reshape(NY, NZ * rows_own * STEPS, TILE)
-    upper_pack = jnp.concatenate(
-        [upper_rows[: STEPS - 1, :, :TILE].reshape((STEPS - 1) * TILE, TILE), upper_inv[1]], axis=0
-    )
-    got = swap_y(jnp.concatenate([to_all(upper_pack, NY), outer], axis=1))
-    upper_tiles = [got[:, step * TILE : (step + 1) * TILE] for step in range(STEPS - 1)]
-    at = (STEPS - 1) * TILE
-    inverse.append(got[:, at : at + PIECE].reshape(TILE, TILE))
-    outer = total(got[:, at + PIECE :]).astype(BF).reshape(NZ, rows_own * STEPS, TILE)
+    upper_pack = upper_rows[: STEPS - 1, :, :TILE].reshape((STEPS - 1) * TILE, TILE)
+    near = [upper_pack]
+    outer_sum = lax.dynamic_index_in_dim(outer, y, 0, False).astype(F32)
+    for step in range(1, NY):
+        theirs = lax.dynamic_index_in_dim(outer, y ^ step, 0, False)
+        got = pass_y(jnp.concatenate([upper_pack, theirs], axis=0), step)
+        near.append(got[: (STEPS - 1) * TILE])
+        outer_sum = outer_sum + got[(STEPS - 1) * TILE :].astype(F32)
+    upper_tiles = [
+        jnp.stack([part[step * TILE : (step + 1) * TILE] for part in near])
+        for step in range(STEPS - 1)
+    ]
+    outer = outer_sum.astype(BF).reshape(NZ, rows_own * STEPS, TILE)
 
     finished = []
     for step in range(STEPS - 1):
@@ -271,7 +288,9 @@
         (order[None, :] // rows_own == z) & (order[None, :] % rows_own == order[:, None] // PER)
     ).astype(BF)
     outer = jnp.repeat(outer.transpose(1, 0, 2), PER, axis=1)
-    last, message = last_call(pos, got, pick_own, outer[STEPS - 1], pack_all)
+    last_pos = pos[(STEPS - 1) * PER :]
+    last_pos = last_pos - last_pos % NY + ((last_pos % NY) ^ y)
+    last, message = last_call(last_pos, got, pick_own, outer[STEPS - 1], pack_all)
     finished.append(last)
     bases = [
         jnp.dot(pick_own, finished[step], preferred_element_type=F32) - outer[step]

time: 245 us -> 234 us (0.955)
  starting transfers between devices: 79.3 us -> 72.3 us
  Pallas kernels: 13.3 us -> 7.34 us
  waiting for transfers between devices: 87.1 us -> 81.2 us
  local copies, waits for them, and re-layouts: 30.4 us -> 34.1 us
    all_to_all x5, starting transfers between devices: 40.7 us -> 27.6 us  [swap_prow(): return lax.all_to_all(x, 'prow', 0, 0, tiled=True)]
    all_to_all x3 -> x2, waiting for transfers between devices: 12.9 us -> 0.01 us  [swap_y(): lax.all_to_all(x, 'pcol', 0, 0, axis_index_groups=Y_GROUPS, tiled=True)]
    pallas_call x2, Pallas kernels: 10.9 us -> 4.98 us  [lower_call(): pl.pallas_call(lambda *refs: lower_kernel(step, *refs), out_shape=(jax.Sh...]
    ppermute x0 -> x3, waiting for transfers between devices: none -> 5.56 us  [pass_y(): return lax.ppermute(x, 'pcol', [(at, at ^ step) for at in range(NC)])]
    all_gather x1, waiting for transfers between devices: 0.01 us -> 4.95 us  [body(): pack_all = lax.all_gather(pack, 'pcol', axis=0)]
    ppermute x0 -> x3, starting transfers between devices: none -> 4.04 us  [pass_y(): return lax.ppermute(x, 'pcol', [(at, at ^ step) for at in range(NC)])]
    all_to_all x3 -> x2, starting transfers between devices: 12 us -> 8.32 us  [swap_y(): lax.all_to_all(x, 'pcol', 0, 0, axis_index_groups=Y_GROUPS, tiled=True)]
    all_to_all x5, waiting for transfers between devices: 40.2 us -> 36.7 us  [swap_z(): lax.all_to_all(x, 'pcol', 0, 0, axis_index_groups=Z_GROUPS, tiled=True)]
  transfers between devices with their start and end apart: 15 -> 17, of which waited for: 12 -> 13; matrix products, arithmetic and copies ran while one was open for 9% -> 13% of each run, Pallas kernels for 2% -> 1%
where the time goes in v3:
time: 234 us; the launch traced here: 232 us
  waiting for transfers between devices  81.2 us (35%)
  starting transfers between devices  72.3 us (31%)
  local copies, waits for them, and re-layouts  34.1 us (15%)
  between operations  17 us (7%)
  other arithmetic  12.1 us (5%)
  matrix products  7.64 us (3%)
  Pallas kernels  7.34 us (3%)
    all_to_all x5, waiting for transfers between devices, swap_z(): lax.all_to_all(x, 'pcol', 0, 0, axis_index_groups=Z_GROUPS, tiled=True)  36.7 us
    all_to_all x5, starting transfers between devices, swap_prow(): return lax.all_to_all(x, 'prow', 0, 0, tiled=True)  27.6 us
    all_to_all x5, waiting for transfers between devices, swap_prow(): return lax.all_to_all(x, 'prow', 0, 0, tiled=True)  26.1 us
    all_to_all x5, starting transfers between devices, swap_z(): lax.all_to_all(x, 'pcol', 0, 0, axis_index_groups=Z_GROUPS, tiled=True)  24.9 us
    unnamed x20, local copies, waits for them, and re-layouts  15.1 us
    all_to_all x2, starting transfers between devices, swap_y(): lax.all_to_all(x, 'pcol', 0, 0, axis_index_groups=Y_GROUPS, tiled=True)  8.32 us
    all_to_all x1, waiting for transfers between devices, swap_pcol(): return lax.all_to_all(x, 'pcol', 0, 0, tiled=True)  7.87 us
    all_to_all x1, starting transfers between devices, swap_pcol(): return lax.all_to_all(x, 'pcol', 0, 0, tiled=True)  7.43 us
  transfers between devices with their start and end apart: 17, of which 13 were waited for; matrix products, arithmetic and copies ran while one was open for 13% of the time, Pallas kernels for 1%

profile of v3, /device:TPU:1, one launch (start us, length us, event | category | flops | bytes accessed | tf_op | source)
XLA Modules:
  0.0 231.7 jit_solution(5165699886734385717)
XLA Ops:
  13.9 5.0 %all-to-all-start = ((bf16[4,160,256]{2,1,0:T(8,128)(2,1)}), bf16[4,160,256]{2,1,0:T(8,128)(2,1)S(1)}, u32[]{:S(2)}, u32[]{:S(2)}) async-start(bf16[4,160,256]{2,1,0:T(8,128)(2,1)} %pad_maximum_fusion.3), calls=%async_computation | async-start | bytes 655360 | tf_op jit(solution)/shard_map/all_to_all | solution.py:28
  35.5 8.2 %all-to-all-start.1 = ((bf16[8,16,256]{2,1,0:T(8,128)(2,1)}), bf16[8,16,256]{2,1,0:T(8,128)(2,1)S(1)}, u32[]{:S(2)}, u32[]{:S(2)}) async-start(bf16[8,16,256]{2,1,0:T(8,128)(2,1)} %select_reduce_fusion.1), calls=%async_computation.1 | async-start | bytes 131072 | tf_op jit(solution)/shard_map/all_to_all | solution.py:36
  43.7 5.6 %collective-permute-done.1 = bf16[560,256]{1,0:T(8,128)(2,1)} collective-permute-done((bf16[560,256]{1,0:T(8,128)(2,1)S(1)}, bf16[560,256]{1,0:T(8,128)(2,1)}, u32[]{:S(2)}, u32[]{:S(2)}) %collective-permute-start.1) | collective-permute-done | bytes 286752 | tf_op jit(solution)/shard_map/ppermute | solution.py:32
  52.2 6.6 %all-to-all-start.2 = ((bf16[8,16,256]{2,1,0:T(8,128)(2,1)}), bf16[8,16,256]{2,1,0:T(8,128)(2,1)S(1)}, u32[]{:S(2)}, u32[]{:S(2)}) async-start(bf16[8,16,256]{2,1,0:T(8,128)(2,1)} %broadcast_in_dim.181), calls=%async_computation.2 | async-start | bytes 131072 | tf_op jit(solution)/shard_map/all_to_all | solution.py:36
  59.7 6.2 %all-to-all-done.2 = bf16[8,16,256]{2,1,0:T(8,128)(2,1)S(1)} async-done(((bf16[8,16,256]{2,1,0:T(8,128)(2,1)}), bf16[8,16,256]{2,1,0:T(8,128)(2,1)S(1)}, u32[]{:S(2)}, u32[]{:S(2)}) %all-to-all-start.2) | async-done | bytes 65568 | tf_op jit(solution)/shard_map/all_to_all | solution.py:36
  67.8 6.8 %all-to-all-start.3 = ((bf16[8,16,4,256]{3,1,2,0:T(8,128)(2,1)}), bf16[8,16,4,256]{3,1,2,0:T(8,128)(2,1)S(1)}, u32[]{:S(2)}, u32[]{:S(2)}) async-start(bf16[8,16,4,256]{3,1,2,0:T(8,128)(2,1)} %broadcast_in_dim.185), calls=%async_computation.3 | async-start | bytes 524288 | tf_op jit(solution)/shard_map/all_to_all | solution.py:44
  74.6 6.5 %all-to-all-done.3 = bf16[8,16,4,256]{3,1,2,0:T(8,128)(2,1)S(1)} async-done(((bf16[8,16,4,256]{3,1,2,0:T(8,128)(2,1)}), bf16[8,16,4,256]{3,1,2,0:T(8,128)(2,1)S(1)}, u32[]{:S(2)}, u32[]{:S(2)}) %all-to-all-start.3) | async-done | bytes 262176 | tf_op jit(solution)/shard_map/all_to_all | solution.py:44
  86.2 6.6 %all-to-all-done.4 = bf16[8,16,256]{2,1,0:T(8,128)(2,1)S(1)} async-done(((bf16[8,16,256]{2,1,0:T(8,128)(2,1)}), bf16[8,16,256]{2,1,0:T(8,128)(2,1)S(1)}, u32[]{:S(2)}, u32[]{:S(2)}) %all-to-all-start.4) | async-done | bytes 65568 | tf_op jit(solution)/shard_map/all_to_all | solution.py:36
  97.1 8.4 %all-to-all-done.5 = bf16[8,22,256]{2,1,0:T(8,128)(2,1)S(1)} async-done(((bf16[8,22,256]{2,1,0:T(8,128)(2,1)}), bf16[8,22,256]{2,1,0:T(8,128)(2,1)S(1)}, u32[]{:S(2)}, u32[]{:S(2)}) %all-to-all-start.5) | async-done | bytes 90144 | tf_op jit(solution)/shard_map/all_to_all | solution.py:36
  106.5 6.8 %all-to-all-start.6 = ((bf16[8,16,4,256]{3,1,2,0:T(8,128)(2,1)}), bf16[8,16,4,256]{3,1,2,0:T(8,128)(2,1)S(1)}, u32[]{:S(2)}, u32[]{:S(2)}) async-start(bf16[8,16,4,256]{3,1,2,0:T(8,128)(2,1)} %broadcast_in_dim.190), calls=%async_computation.6 | async-start | bytes 524288 | tf_op jit(solution)/shard_map/all_to_all | solution.py:44
  113.4 6.5 %all-to-all-done.6 = bf16[8,16,4,256]{3,1,2,0:T(8,128)(2,1)S(1)} async-done(((bf16[8,16,4,256]{3,1,2,0:T(8,128)(2,1)}), bf16[8,16,4,256]{3,1,2,0:T(8,128)(2,1)S(1)}, u32[]{:S(2)}, u32[]{:S(2)}) %all-to-all-start.6) | async-done | bytes 262176 | tf_op jit(solution)/shard_map/all_to_all | solution.py:44
  124.3 14.4 %all-to-all-done.7.got = bf16[32,16,256]{2,1,0:T(8,128)(2,1)S(1)} async-done(((bf16[32,16,256]{2,1,0:T(8,128)(2,1)}), bf16[32,16,256]{2,1,0:T(8,128)(2,1)S(1)}, u32[]{:S(2)}, u32[]{:S(2)}) %all-to-all-start.7) | async-done | bytes 262176 | tf_op jit(solution)/shard_map/all_to_all | solution.py:36
  138.6 4.9 %all-gather.3.cloned.1.call-done = bf16[24576,256]{1,0:T(8,128)(2,1)} async-done(((bf16[768,256]{1,0:T(8,128)(2,1)}), bf16[24576,256]{1,0:T(8,128)(2,1)}) %all-gather.3.cloned.1.call-update) | async-done | bytes 12582928 | tf_op jit(solution)/shard_map/all_gather | solution.py:224
  143.6 4.6 %copy-done = bf16[24576,256]{1,0:T(8,128)(2,1)S(1)} copy-done((bf16[24576,256]{1,0:T(8,128)(2,1)S(1)}, bf16[24576,256]{1,0:T(8,128)(2,1)}, u32[]{:S(2)}) %copy-start) | copy-done | bytes 12582936
  150.5 5.4 %all-to-all-start.8 = ((bf16[8,16,256]{2,1,0:T(8,128)(2,1)}), bf16[8,16,256]{2,1,0:T(8,128)(2,1)S(1)}, u32[]{:S(2)}, u32[]{:S(2)}) async-start(bf16[8,16,256]{2,1,0:T(8,128)(2,1)} %get-tuple-element.12), calls=%async_computation.8 | async-start | bytes 131072 | tf_op jit(solution)/shard_map/all_to_all | solution.py:44
  156.0 4.8 %all-to-all-done.8.refs_1_ = bf16[8,16,256]{2,1,0:T(8,128)(2,1)S(1)} async-done(((bf16[8,16,256]{2,1,0:T(8,128)(2,1)}), bf16[8,16,256]{2,1,0:T(8,128)(2,1)S(1)}, u32[]{:S(2)}, u32[]{:S(2)}) %all-to-all-start.8) | async-done | bytes 65568 | tf_op jit(solution)/shard_map/all_to_all | solution.py:44
  165.0 4.6 %copy-done.1 = bf16[24576,256]{1,0:T(8,128)(2,1)S(1)} copy-done((bf16[24576,256]{1,0:T(8,128)(2,1)S(1)}, bf16[24576,256]{1,0:T(8,128)(2,1)}, u32[]{:S(2)}) %copy-start.1) | copy-done | bytes 12582936
  175.7 4.1 %all-to-all-start.10 = ((bf16[8,80,256]{2,1,0:T(8,128)(2,1)}), bf16[8,80,256]{2,1,0:T(8,128)(2,1)S(1)}, u32[]{:S(2)}, u32[]{:S(2)}) async-start(bf16[8,80,256]{2,1,0:T(8,128)(2,1)} %pad_maximum_fusion.4), calls=%async_computation.10 | async-start | bytes 655360 | tf_op jit(solution)/shard_map/all_to_all | solution.py:44
  179.8 5.5 %gather_fusion.1 = f32[2048,64]{1,0:T(8,128)S(1)} fusion(f32[64,2048]{0,1:T(8,128)S(1)} %copy.89, s32[2048]{0:T(1024)S(1)} %fusion.32), kind=kCustom, calls=%fused_computation.1 | custom fusion | bytes 1056768 | tf_op jit(solution)/shard_map/jit(_take)/gather | solution.py:330
  187.0 4.6 %copy-done.2 = bf16[24576,256]{1,0:T(8,128)(2,1)S(1)} copy-done((bf16[24576,256]{1,0:T(8,128)(2,1)S(1)}, bf16[24576,256]{1,0:T(8,128)(2,1)}, u32[]{:S(2)}) %copy-start.2) | copy-done | bytes 12582936
  195.2 4.5 %all-to-all-start.11 = ((bf16[8,80,256]{2,1,0:T(8,128)(2,1)}), bf16[8,80,256]{2,1,0:T(8,128)(2,1)S(1)}, u32[]{:S(2)}, u32[]{:S(2)}) async-start(bf16[8,80,256]{2,1,0:T(8,128)(2,1)} %pad_maximum_fusion.5), calls=%async_computation.11 | async-start | bytes 655360 | tf_op jit(solution)/shard_map/all_to_all | solution.py:44
  199.7 7.1 %all-to-all-done.11 = bf16[8,80,256]{2,1,0:T(8,128)(2,1)S(1)} async-done(((bf16[8,80,256]{2,1,0:T(8,128)(2,1)}), bf16[8,80,256]{2,1,0:T(8,128)(2,1)S(1)}, u32[]{:S(2)}, u32[]{:S(2)}) %all-to-all-start.11) | async-done | bytes 327712 | tf_op jit(solution)/shard_map/all_to_all | solution.py:44
  207.8 7.4 %all-to-all-start.12 = ((bf16[32,2,256]{2,1,0:T(2,128)(2,1)}), bf16[32,2,256]{2,1,0:T(2,128)(2,1)S(1)}, u32[]{:S(2)}, u32[]{:S(2)}) async-start(bf16[32,2,256]{2,1,0:T(2,128)(2,1)} %reshape.503), calls=%async_computation.12 | async-start | bytes 65536 | tf_op jit(solution)/shard_map/all_to_all | solution.py:40
  216.1 7.9 %all-to-all-done.12 = bf16[32,2,256]{2,1,0:T(2,128)(2,1)S(1)} async-done(((bf16[32,2,256]{2,1,0:T(2,128)(2,1)}), bf16[32,2,256]{2,1,0:T(2,128)(2,1)S(1)}, u32[]{:S(2)}, u32[]{:S(2)}) %all-to-all-start.12) | async-done | bytes 32800 | tf_op jit(solution)/shard_map/all_to_all | solution.py:40
  (150 shorter events, 61.8 us)
Async XLA Ops:
  7.2 6.0 %slice-start.1 = ((bf16[3,64,256]{2,1,0:T(8,128)(2,1)}), bf16[2,64,256]{2,1,0:T(8,128)(2,1)S(1)}, s32[]{:S(2)}) async-start(bf16[3,64,256]{2,1,0:T(8,128)(2,1)} %param.12), calls=%async_computation.15 | async-start | bytes 131072 | tf_op jit(solution)/shard_map/slice | solution.py:231
  7.2 5.0 %copy-start.5 = (s32[2048]{0:T(1024)S(1)}, s32[2048]{0:T(1024)}, u32[]{:S(2)}) copy-start(s32[2048]{0:T(1024)} %param.9) | copy-start | bytes 24580
  7.2 136.4 %all-gather.3.cloned.1.call-start = ((), (), s32[]{:S(2)}) async-start(), calls=%async_computation.13 | async-start | bytes 12976128 | tf_op jit(solution)/shard_map/all_gather | solution.py:224
  9.0 10.0 %copy-start.6 = (s32[256]{0:T(256)S(1)}, s32[256]{0:T(256)}, u32[]{:S(2)}) copy-start(s32[256]{0:T(256)} %param.10) | copy-start | bytes 3076
  9.0 13.0 %copy-start.3 = (f32[64,2048]{1,0:T(8,128)S(1)}, f32[64,2048]{1,0:T(8,128)}, u32[]{:S(2)}) copy-start(f32[64,2048]{1,0:T(8,128)} %param.15) | copy-start | bytes 1572868
  13.9 20.7 %all-to-all-start = ((bf16[4,160,256]{2,1,0:T(8,128)(2,1)}), bf16[4,160,256]{2,1,0:T(8,128)(2,1)S(1)}, u32[]{:S(2)}, u32[]{:S(2)}) async-start(bf16[4,160,256]{2,1,0:T(8,128)(2,1)} %pad_maximum_fusion.3), calls=%async_computation | async-start | bytes 655360 | tf_op jit(solution)/shard_map/all_to_all | solution.py:28
  26.4 17.3 %collective-permute-start = (bf16[560,256]{1,0:T(8,128)(2,1)S(1)}, bf16[560,256]{1,0:T(8,128)(2,1)S(1)}, u32[]{:S(2)}, u32[]{:S(2)}) collective-permute-start(bf16[560,256]{1,0:T(8,128)(2,1)S(1)} %get-tuple-element.33), channel_id=1, source_target_pairs={{0,1},{1,0},{2,3},{3,2},{4,5},{5,4},{6,7},{7,6},{8,9},{9,8},{10,11... | collective-permute-start | bytes 860168 | tf_op jit(solution)/shard_map/ppermute | solution.py:32
  28.0 21.3 %collective-permute-start.1 = (bf16[560,256]{1,0:T(8,128)(2,1)S(1)}, bf16[560,256]{1,0:T(8,128)(2,1)}, u32[]{:S(2)}, u32[]{:S(2)}) collective-permute-start(bf16[560,256]{1,0:T(8,128)(2,1)S(1)} %get-tuple-element.34), channel_id=1, source_target_pairs={{0,2},{1,3},{2,0},{3,1},{4,6},{5,7},{6,4},{7,5},{8,10},{9,11},{10,... | collective-permute-start | bytes 860168 | tf_op jit(solution)/shard_map/ppermute | solution.py:32
  30.4 28.4 %collective-permute-start.2 = (bf16[560,256]{1,0:T(8,128)(2,1)S(1)}, bf16[560,256]{1,0:T(8,128)(2,1)}, u32[]{:S(2)}, u32[]{:S(2)}) collective-permute-start(bf16[560,256]{1,0:T(8,128)(2,1)S(1)} %get-tuple-element.35), channel_id=1, source_target_pairs={{0,3},{1,2},{2,1},{3,0},{4,7},{5,6},{6,5},{7,4},{8,11},{9,10},{10,... | collective-permute-start | bytes 860168 | tf_op jit(solution)/shard_map/ppermute | solution.py:32
  35.5 15.9 %all-to-all-start.1 = ((bf16[8,16,256]{2,1,0:T(8,128)(2,1)}), bf16[8,16,256]{2,1,0:T(8,128)(2,1)S(1)}, u32[]{:S(2)}, u32[]{:S(2)}) async-start(bf16[8,16,256]{2,1,0:T(8,128)(2,1)} %select_reduce_fusion.1), calls=%async_computation.1 | async-start | bytes 131072 | tf_op jit(solution)/shard_map/all_to_all | solution.py:36
  43.7 61.9 %copy-start.4 = (bf16[1,256,256]{2,1,0:T(8,128)(2,1)S(1)}, bf16[1,256,256]{2,1,0:T(8,128)(2,1)}, u32[]{:S(2)}) copy-start(bf16[1,256,256]{2,1,0:T(8,128)(2,1)} %get-tuple-element.24) | copy-start | bytes 393220
  52.2 13.8 %all-to-all-start.2 = ((bf16[8,16,256]{2,1,0:T(8,128)(2,1)}), bf16[8,16,256]{2,1,0:T(8,128)(2,1)S(1)}, u32[]{:S(2)}, u32[]{:S(2)}) async-start(bf16[8,16,256]{2,1,0:T(8,128)(2,1)} %broadcast_in_dim.181), calls=%async_computation.2 | async-start | bytes 131072 | tf_op jit(solution)/shard_map/all_to_all | solution.py:36
  67.8 13.3 %all-to-all-start.3 = ((bf16[8,16,4,256]{3,1,2,0:T(8,128)(2,1)}), bf16[8,16,4,256]{3,1,2,0:T(8,128)(2,1)S(1)}, u32[]{:S(2)}, u32[]{:S(2)}) async-start(bf16[8,16,4,256]{3,1,2,0:T(8,128)(2,1)} %broadcast_in_dim.185), calls=%async_computation.3 | async-start | bytes 524288 | tf_op jit(solution)/shard_map/all_to_all | solution.py:44
  82.0 10.8 %all-to-all-start.4 = ((bf16[8,16,256]{2,1,0:T(8,128)(2,1)}), bf16[8,16,256]{2,1,0:T(8,128)(2,1)S(1)}, u32[]{:S(2)}, u32[]{:S(2)}) async-start(bf16[8,16,256]{2,1,0:T(8,128)(2,1)} %select_reduce_fusion), calls=%async_computation.4 | async-start | bytes 131072 | tf_op jit(solution)/shard_map/all_to_all | solution.py:36
  93.6 11.9 %all-to-all-start.5 = ((bf16[8,22,256]{2,1,0:T(8,128)(2,1)}), bf16[8,22,256]{2,1,0:T(8,128)(2,1)S(1)}, u32[]{:S(2)}, u32[]{:S(2)}) async-start(bf16[8,22,256]{2,1,0:T(8,128)(2,1)} %pad_maximum_fusion.10), calls=%async_computation.5 | async-start | bytes 196608 | tf_op jit(solution)/shard_map/all_to_all | solution.py:36
  106.5 13.3 %all-to-all-start.6 = ((bf16[8,16,4,256]{3,1,2,0:T(8,128)(2,1)}), bf16[8,16,4,256]{3,1,2,0:T(8,128)(2,1)S(1)}, u32[]{:S(2)}, u32[]{:S(2)}) async-start(bf16[8,16,4,256]{3,1,2,0:T(8,128)(2,1)} %broadcast_in_dim.190), calls=%async_computation.6 | async-start | bytes 524288 | tf_op jit(solution)/shard_map/all_to_all | solution.py:44
  120.7 17.9 %all-to-all-start.7 = ((bf16[32,16,256]{2,1,0:T(8,128)(2,1)}), bf16[32,16,256]{2,1,0:T(8,128)(2,1)S(1)}, u32[]{:S(2)}, u32[]{:S(2)}) async-start(bf16[32,16,256]{2,1,0:T(8,128)(2,1)} %bitcast.27), calls=%async_computation.7 | async-start | bytes 524288 | tf_op jit(solution)/shard_map/all_to_all | solution.py:36
  150.5 10.3 %all-to-all-start.8 = ((bf16[8,16,256]{2,1,0:T(8,128)(2,1)}), bf16[8,16,256]{2,1,0:T(8,128)(2,1)S(1)}, u32[]{:S(2)}, u32[]{:S(2)}) async-start(bf16[8,16,256]{2,1,0:T(8,128)(2,1)} %get-tuple-element.12), calls=%async_computation.8 | async-start | bytes 131072 | tf_op jit(solution)/shard_map/all_to_all | solution.py:44
  161.5 10.3 %all-to-all-start.9 = ((bf16[4,48,256]{2,1,0:T(8,128)(2,1)}), bf16[4,48,256]{2,1,0:T(8,128)(2,1)S(1)}, u32[]{:S(2)}, u32[]{:S(2)}) async-start(bf16[4,48,256]{2,1,0:T(8,128)(2,1)} %broadcast_in_dim.196), calls=%async_computation.9 | async-start | bytes 196608 | tf_op jit(solution)/shard_map/all_to_all | solution.py:28
  165.0 4.6 %copy-start.1 = (bf16[24576,256]{1,0:T(8,128)(2,1)S(1)}, bf16[24576,256]{1,0:T(8,128)(2,1)}, u32[]{:S(2)}) copy-start(bf16[24576,256]{1,0:T(8,128)(2,1)} %all-gather.3.cloned.1.call-done) | copy-start | bytes 37748740
  175.7 11.3 %all-to-all-start.10 = ((bf16[8,80,256]{2,1,0:T(8,128)(2,1)}), bf16[8,80,256]{2,1,0:T(8,128)(2,1)S(1)}, u32[]{:S(2)}, u32[]{:S(2)}) async-start(bf16[8,80,256]{2,1,0:T(8,128)(2,1)} %pad_maximum_fusion.4), calls=%async_computation.10 | async-start | bytes 655360 | tf_op jit(solution)/shard_map/all_to_all | solution.py:44
  195.2 11.6 %all-to-all-start.11 = ((bf16[8,80,256]{2,1,0:T(8,128)(2,1)}), bf16[8,80,256]{2,1,0:T(8,128)(2,1)S(1)}, u32[]{:S(2)}, u32[]{:S(2)}) async-start(bf16[8,80,256]{2,1,0:T(8,128)(2,1)} %pad_maximum_fusion.5), calls=%async_computation.11 | async-start | bytes 655360 | tf_op jit(solution)/shard_map/all_to_all | solution.py:44
  199.6 24.4 %slice-start = ((f32[64,2048]{1,0:T(8,128)}), f32[64,1792]{1,0:T(8,128)S(1)}, s32[]{:S(2)}) async-start(f32[64,2048]{1,0:T(8,128)} %param.15), calls=%async_computation.14 | async-start | bytes 917504 | tf_op jit(solution)/shard_map/slice | solution.py:243
  207.8 16.1 %all-to-all-start.12 = ((bf16[32,2,256]{2,1,0:T(2,128)(2,1)}), bf16[32,2,256]{2,1,0:T(2,128)(2,1)S(1)}, u32[]{:S(2)}, u32[]{:S(2)}) async-start(bf16[32,2,256]{2,1,0:T(2,128)(2,1)} %reshape.503), calls=%async_computation.12 | async-start | bytes 65536 | tf_op jit(solution)/shard_map/all_to_all | solution.py:40
  (2 other events, 9.2 us)
Sparse Core Ops, SparseCore 0:
  11.2 132.3 all-gather.2

commit v4 on v3

--- a/solution.py
+++ b/solution.py
@@ -32,6 +32,17 @@
     return lax.ppermute(x, "pcol", [(at, at ^ step) for at in range(NC)])
 
 
+def pass_prow(x, step):
+    return lax.ppermute(x, "prow", [(at, at ^ step) for at in range(NP)])
+
+
+def by_place(parts, index, count):
+    parts = jnp.stack(parts)
+    return jnp.stack(
+        [lax.dynamic_index_in_dim(parts, index ^ place, 0, False) for place in range(count)]
+    )
+
+
 def swap_z(x):
     return lax.all_to_all(x, "pcol", 0, 0, axis_index_groups=Z_GROUPS, tiled=True)
 
@@ -119,7 +130,7 @@
             pltpu.VMEM((NC, PIECE, TILE), BF),
             pltpu.SemaphoreType.DMA((2,)),
         ],
-        compiler_params=pltpu.CompilerParams(vmem_limit_bytes=24 << 20),
+        compiler_params=pltpu.CompilerParams(vmem_limit_bytes=50 << 20),
         name="last_block",
     )(pos, got, pick_own, outer, pack)
 
@@ -183,7 +194,7 @@
             pltpu.VMEM((NC, PIECE, TILE), BF),
             pltpu.SemaphoreType.DMA((count + 1,)),
         ],
-        compiler_params=pltpu.CompilerParams(vmem_limit_bytes=24 << 20),
+        compiler_params=pltpu.CompilerParams(vmem_limit_bytes=50 << 20),
         name=f"lower_block_{step}",
     )(pos, back, base, *known, pack)
 
@@ -239,35 +250,39 @@
         start = 2 * rows_z + step * PIECE
         inverse.append(got[:, start : start + PIECE].reshape(TILE, TILE))
 
-    slot_known = jnp.where(my_block >= STEPS, solved[:, :TILE], 0.0)
-    known = jnp.concatenate([slot_known, solved[:, TILE:]], axis=1).astype(BF)
-    outer = lax.dot_general(
-        known, lower_rows, (((1,), (2,)), ((), ())), preferred_element_type=F32
-    )
-    outer = outer.astype(BF).reshape(NZ, NY, rows_own, STEPS, TILE).transpose(1, 0, 2, 3, 4)
-    outer = outer.reshape(NY, NZ * rows_own * STEPS, TILE)
     upper_pack = upper_rows[: STEPS - 1, :, :TILE].reshape((STEPS - 1) * TILE, TILE)
-    near = [upper_pack]
-    outer_sum = lax.dynamic_index_in_dim(outer, y, 0, False).astype(F32)
-    for step in range(1, NY):
-        theirs = lax.dynamic_index_in_dim(outer, y ^ step, 0, False)
-        got = pass_y(jnp.concatenate([upper_pack, theirs], axis=0), step)
-        near.append(got[: (STEPS - 1) * TILE])
-        outer_sum = outer_sum + got[(STEPS - 1) * TILE :].astype(F32)
+    near = [upper_pack] + [pass_y(upper_pack, step) for step in range(1, NY)]
     upper_tiles = [
         jnp.stack([part[step * TILE : (step + 1) * TILE] for part in near])
         for step in range(STEPS - 1)
     ]
-    outer = outer_sum.astype(BF).reshape(NZ, rows_own * STEPS, TILE)
 
     finished = []
     for step in range(STEPS - 1):
         block = tiles.astype(BF)
         pick = plane_tiles[None, :] == step * PER + jnp.arange(NZ)[:, None]
         routed = jnp.sum(jnp.where(pick[:, :, None, None], block[None], 0), axis=1)
+        if step == 0:
+            routed, solved_now = lax.optimization_barrier((routed, solved))
+        if step == 1:
+            routed, rhs_now = lax.optimization_barrier((routed, rhs))
+            state0 = jnp.take(rhs_now, local_pivots, axis=1)
         mine = jnp.sum(swap_z(routed), axis=0)
         part = jnp.dot(mine, inverse[step], preferred_element_type=F32).astype(BF)
         message = to_all(part, NZ)
+        if step == 0:
+            slot_known = jnp.where(my_block >= STEPS, solved_now[:, :TILE], 0.0)
+            known = jnp.concatenate([slot_known, solved_now[:, TILE:]], axis=1).astype(BF)
+            outer = lax.dot_general(
+                known, lower_rows, (((1,), (2,)), ((), ())), preferred_element_type=F32
+            )
+            outer = outer.astype(BF).reshape(NZ, NY, rows_own, STEPS, TILE)
+            outer = outer.transpose(1, 0, 2, 3, 4).reshape(NY, NZ * rows_own * STEPS, TILE)
+            outer_sum = lax.dynamic_index_in_dim(outer, y, 0, False).astype(F32)
+            for other in range(1, NY):
+                theirs = lax.dynamic_index_in_dim(outer, y ^ other, 0, False)
+                outer_sum = outer_sum + pass_y(theirs, other).astype(F32)
+            outer = outer_sum.astype(BF).reshape(NZ, rows_own * STEPS, TILE)
         if step == 1:
             message = jnp.concatenate([message, outer], axis=1)
         back = total(swap_z(message))
@@ -298,7 +313,11 @@
     ]
 
     stacked, message = lax.optimization_barrier((jnp.concatenate(finished, axis=0), message))
-    every = swap_y(to_all(stacked, NY)).reshape(NY, STEPS, NZ, rows_own, TILE)
+    every = [stacked] + [pass_y(stacked, step) for step in range(1, NY)]
+    back = swap_prow(message)
+    last, message = lower_call(1, pos, back, bases[1], [], pack_all)
+    message, every = lax.optimization_barrier((message, every))
+    every = by_place(every, y, NY).reshape(NY, STEPS, NZ, rows_own, TILE)
     every = every.transpose(1, 2, 0, 3, 4).reshape(STEPS, count, TILE)
     bulk = jnp.dot(
         jnp.concatenate(list(every), axis=1),
@@ -313,23 +332,26 @@
     bulk = bulk.reshape(NP, count // NP * slots, TILE)
 
     back = swap_prow(message)
-    last, message = lower_call(1, pos, back, bases[1], [], pack_all)
+    middle, message = lower_call(0, pos, back, bases[0], [last], pack_all)
     back = swap_prow(jnp.concatenate([message, bulk], axis=1))
-    bulk = total(back[:, ROWS:]).astype(BF)
-    middle, message = lower_call(0, pos, back[:, :ROWS], bases[0], [last], pack_all)
-    back = swap_prow(jnp.concatenate([message, to_all(bulk, NP)], axis=1))
-    bulk = back[:, ROWS:].reshape(count, width).astype(F32)
     first = total(back[:, :ROWS]).astype(BF)
 
     window = jnp.concatenate([first, middle, last], axis=0)
     window = window.reshape(STEPS, rows_own, PER, TILE).transpose(0, 2, 1, 3)
-    window = swap_pcol(choose(window.reshape(STEPS * PER, rows_own, TILE), first_tiles))
+    window = choose(window.reshape(STEPS * PER, rows_own, TILE), first_tiles)
+    bulk = total(back[:, ROWS:]).astype(BF)
+    window, bulk = lax.optimization_barrier((window, bulk))
+    window = swap_pcol(window)
+    pair = jnp.stack([bulk, pass_prow(bulk, 1)])
+    pairs = [pair] + [pass_prow(pair, step) for step in range(2, NP, 2)]
+    bulk = by_place([part[side] for part in pairs for side in range(2)], row, NP)
+    bulk = bulk.reshape(count, width).astype(F32)
+    slot_forward = jnp.where(my_block < STEPS, bulk[:, :TILE], state0[:, :TILE] - bulk[:, :TILE])
+    forward = jnp.concatenate([slot_forward, state0[:, TILE:] - bulk[:, TILE:]], axis=1)
+    forward, window = lax.optimization_barrier((forward, window))
     window = window.reshape(count, TILE).astype(F32)
     slot_solution = jnp.where(my_block < STEPS, window, solved[:, :TILE])
     backward = jnp.concatenate([slot_solution, solved[:, TILE:]], axis=1)
-    state0 = jnp.take(rhs, local_pivots, axis=1)
-    slot_forward = jnp.where(my_block < STEPS, bulk[:, :TILE], state0[:, :TILE] - bulk[:, :TILE])
-    forward = jnp.concatenate([slot_forward, state0[:, TILE:] - bulk[:, TILE:]], axis=1)
     return (forward, backward)
 
 

time: 234 us -> 221 us (0.944)
  waiting for transfers between devices: 81.2 us -> 54.7 us
  other arithmetic: 12.1 us -> 20.1 us
  starting transfers between devices: 72.3 us -> 79.5 us
  local copies, waits for them, and re-layouts: 34.1 us -> 28.6 us
  Pallas kernels: 7.34 us -> 11.3 us
    unnamed x20 -> x66, local copies, waits for them, and re-layouts: 15.1 us -> 0.86 us
    all_to_all x5, waiting for transfers between devices: 26.1 us -> 15.6 us  [swap_prow(): return lax.all_to_all(x, 'prow', 0, 0, tiled=True)]
    ppermute x3 -> x9, starting transfers between devices: 4.04 us -> 11.4 us  [pass_y(): return lax.ppermute(x, 'pcol', [(at, at ^ step) for at in range(NC)])]
    all_to_all x1, waiting for transfers between devices: 7.87 us -> 0.53 us  [swap_pcol(): return lax.all_to_all(x, 'pcol', 0, 0, tiled=True)]
    ppermute x3 -> x9, waiting for transfers between devices: 5.56 us -> 0.02 us  [pass_y(): return lax.ppermute(x, 'pcol', [(at, at ^ step) for at in range(NC)])]
    all_to_all x5, starting transfers between devices: 27.6 us -> 32.8 us  [swap_prow(): return lax.all_to_all(x, 'prow', 0, 0, tiled=True)]
    ppermute x0 -> x4, starting transfers between devices: none -> 5.16 us  [pass_prow(): return lax.ppermute(x, 'prow', [(at, at ^ step) for at in range(NP)])]
    all_gather x1, waiting for transfers between devices: 4.95 us -> 0.01 us  [body(): pack_all = lax.all_gather(pack, 'pcol', axis=0)]
  transfers between devices with their start and end apart: 17 -> 26, of which waited for: 13 -> 11; matrix products, arithmetic and copies ran while one was open for 13% -> 23% of each run, Pallas kernels for 1% -> 2%
where the time goes in v4:
time: 221 us; the launch traced here: 219 us
  starting transfers between devices  79.5 us (36%)
  waiting for transfers between devices  54.7 us (25%)
  local copies, waits for them, and re-layouts  28.6 us (13%)
  other arithmetic  20.1 us (9%)
  between operations  17.5 us (8%)
  Pallas kernels  11.3 us (5%)
  matrix products  7.48 us (3%)
    all_to_all x5, waiting for transfers between devices, swap_z(): lax.all_to_all(x, 'pcol', 0, 0, axis_index_groups=Z_GROUPS, tiled=True)  35.6 us
    all_to_all x5, starting transfers between devices, swap_prow(): return lax.all_to_all(x, 'prow', 0, 0, tiled=True)  32.8 us
    all_to_all x5, starting transfers between devices, swap_z(): lax.all_to_all(x, 'pcol', 0, 0, axis_index_groups=Z_GROUPS, tiled=True)  22.2 us
    all_to_all x5, waiting for transfers between devices, swap_prow(): return lax.all_to_all(x, 'prow', 0, 0, tiled=True)  15.6 us
    ppermute x9, starting transfers between devices, pass_y(): return lax.ppermute(x, 'pcol', [(at, at ^ step) for at in range(NC)])  11.4 us
    pallas_call x2, Pallas kernels, lower_call(): pl.pallas_call(lambda *refs: lower_kernel(step, *refs), out_shape=(jax.Sh...  7.83 us
    gather x2, local copies, waits for them, and re-layouts, body(): state0 = jnp.take(rhs_now, local_pivots, axis=1)  6.58 us
    ppermute x4, starting transfers between devices, pass_prow(): return lax.ppermute(x, 'prow', [(at, at ^ step) for at in range(NP)])  5.16 us
  transfers between devices with their start and end apart: 26, of which 11 were waited for; matrix products, arithmetic and copies ran while one was open for 23% of the time, Pallas kernels for 2%

profile of v4, /device:TPU:1, one launch (start us, length us, event | category | flops | bytes accessed | tf_op | source)
XLA Modules:
  0.0 219.1 jit_solution(6541913288389270941)
XLA Ops:
  12.3 3.6 %collective-permute-start.2 = (bf16[512,256]{1,0:T(8,128)(2,1)}, bf16[512,256]{1,0:T(8,128)(2,1)}, u32[]{:S(2)}, u32[]{:S(2)}) collective-permute-start(bf16[512,256]{1,0:T(8,128)(2,1)} %bitcast.11), channel_id=1, source_target_pairs={{0,3},{1,2},{2,1},{3,0},{4,7},{5,6},{6,5},{7,4},{8,11},{9,10},{10,... | collective-permute-start | bytes 786440 | tf_op jit(solution)/shard_map/ppermute | solution.py:32
  20.5 4.1 %all-to-all-start = ((bf16[4,160,256]{2,1,0:T(8,128)(2,1)}), bf16[4,160,256]{2,1,0:T(8,128)(2,1)S(1)}, u32[]{:S(2)}, u32[]{:S(2)}) async-start(bf16[4,160,256]{2,1,0:T(8,128)(2,1)} %pad_maximum_fusion.3), calls=%async_computation | async-start | bytes 655360 | tf_op jit(solution)/shard_map/all_to_all | solution.py:28
  39.9 8.7 %all-to-all-start.1 = ((bf16[8,16,256]{2,1,0:T(8,128)(2,1)}), bf16[8,16,256]{2,1,0:T(8,128)(2,1)}, u32[]{:S(2)}, u32[]{:S(2)}) async-start(bf16[8,16,256]{2,1,0:T(8,128)(2,1)} %select_reduce_fusion.1), calls=%async_computation.1 | async-start | bytes 131072 | tf_op jit(solution)/shard_map/all_to_all | solution.py:47
  52.6 3.4 %all-to-all-done.1 = bf16[8,16,256]{2,1,0:T(8,128)(2,1)} async-done(((bf16[8,16,256]{2,1,0:T(8,128)(2,1)}), bf16[8,16,256]{2,1,0:T(8,128)(2,1)}, u32[]{:S(2)}, u32[]{:S(2)}) %all-to-all-start.1) | async-done | bytes 65568 | tf_op jit(solution)/shard_map/all_to_all | solution.py:47
  63.5 5.5 %all-to-all-done.2 = bf16[8,16,256]{2,1,0:T(8,128)(2,1)S(1)} async-done(((bf16[8,16,256]{2,1,0:T(8,128)(2,1)}), bf16[8,16,256]{2,1,0:T(8,128)(2,1)S(1)}, u32[]{:S(2)}, u32[]{:S(2)}) %all-to-all-start.2) | async-done | bytes 65568 | tf_op jit(solution)/shard_map/all_to_all | solution.py:47
  71.5 10.9 %all-to-all-start.3 = ((bf16[8,16,4,256]{3,1,2,0:T(8,128)(2,1)}), bf16[8,16,4,256]{3,1,2,0:T(8,128)(2,1)S(1)}, u32[]{:S(2)}, u32[]{:S(2)}) async-start(bf16[8,16,4,256]{3,1,2,0:T(8,128)(2,1)} %broadcast_in_dim.172), calls=%async_computation.3 | async-start | bytes 524288 | tf_op jit(solution)/shard_map/all_to_all | solution.py:55
  91.9 3.4 %all-to-all-start.4 = ((bf16[8,16,256]{2,1,0:T(8,128)(2,1)}), bf16[8,16,256]{2,1,0:T(8,128)(2,1)S(1)}, u32[]{:S(2)}, u32[]{:S(2)}) async-start(bf16[8,16,256]{2,1,0:T(8,128)(2,1)} %select_reduce_fusion), calls=%async_computation.4 | async-start | bytes 131072 | tf_op jit(solution)/shard_map/all_to_all | solution.py:47
  95.4 7.8 %all-to-all-done.4 = bf16[8,16,256]{2,1,0:T(8,128)(2,1)S(1)} async-done(((bf16[8,16,256]{2,1,0:T(8,128)(2,1)}), bf16[8,16,256]{2,1,0:T(8,128)(2,1)S(1)}, u32[]{:S(2)}, u32[]{:S(2)}) %all-to-all-start.4) | async-done | bytes 65568 | tf_op jit(solution)/shard_map/all_to_all | solution.py:47
  104.0 3.4 %all-to-all-start.5 = ((bf16[8,22,256]{2,1,0:T(8,128)(2,1)}), bf16[8,22,256]{2,1,0:T(8,128)(2,1)S(1)}, u32[]{:S(2)}, u32[]{:S(2)}) async-start(bf16[8,22,256]{2,1,0:T(8,128)(2,1)} %pad_maximum_fusion.6), calls=%async_computation.5 | async-start | bytes 196608 | tf_op jit(solution)/shard_map/all_to_all | solution.py:47
  108.9 7.0 %all-to-all-done.5 = bf16[8,22,256]{2,1,0:T(8,128)(2,1)S(1)} async-done(((bf16[8,22,256]{2,1,0:T(8,128)(2,1)}), bf16[8,22,256]{2,1,0:T(8,128)(2,1)S(1)}, u32[]{:S(2)}, u32[]{:S(2)}) %all-to-all-start.5) | async-done | bytes 90144 | tf_op jit(solution)/shard_map/all_to_all | solution.py:47
  118.0 7.9 %all-to-all-start.6 = ((bf16[8,16,4,256]{3,1,2,0:T(8,128)(2,1)}), bf16[8,16,4,256]{3,1,2,0:T(8,128)(2,1)S(1)}, u32[]{:S(2)}, u32[]{:S(2)}) async-start(bf16[8,16,4,256]{3,1,2,0:T(8,128)(2,1)} %broadcast_in_dim.178), calls=%async_computation.6 | async-start | bytes 524288 | tf_op jit(solution)/shard_map/all_to_all | solution.py:55
  126.4 5.5 %gather_fusion.1 = f32[2048,64]{1,0:T(8,128)S(1)} fusion(f32[64,2048]{0,1:T(8,128)S(1)} %copy.66, s32[2048]{0:T(1024)S(1)} %fusion.32), kind=kCustom, calls=%fused_computation.1 | custom fusion | bytes 1056768 | tf_op jit(solution)/shard_map/jit(_take)/gather | solution.py:269
  133.9 3.4 %all-to-all-start.7 = ((bf16[32,16,256]{2,1,0:T(8,128)(2,1)}), bf16[32,16,256]{2,1,0:T(8,128)(2,1)S(1)}, u32[]{:S(2)}, u32[]{:S(2)}) async-start(bf16[32,16,256]{2,1,0:T(8,128)(2,1)} %bitcast.26), calls=%async_computation.7 | async-start | bytes 524288 | tf_op jit(solution)/shard_map/all_to_all | solution.py:47
  137.6 11.9 %all-to-all-done.7.got = bf16[32,16,256]{2,1,0:T(8,128)(2,1)S(1)} async-done(((bf16[32,16,256]{2,1,0:T(8,128)(2,1)}), bf16[32,16,256]{2,1,0:T(8,128)(2,1)S(1)}, u32[]{:S(2)}, u32[]{:S(2)}) %all-to-all-start.7) | async-done | bytes 262176 | tf_op jit(solution)/shard_map/all_to_all | solution.py:47
  149.6 3.4 %last_block.1 = (bf16[16,256]{1,0:T(8,128)(2,1)S(1)}, bf16[8,16,256]{2,1,0:T(8,128)(2,1)}) custom-call(s32[8]{0:T(128)S(1)} %xor_add_fusion.pos, bf16[32,16,256]{2,1,0:T(8,128)(2,1)S(1)} %all-to-all-done.7.got, bf16[16,16]{1,0:T(8,128)(2,1)S(1)} %fusion.31.pick_own, f32[16,256]{1,0:T(8,128)S(1)} %broadcast_bitcast_fusion.outer, bf16[32,768,256]{2,1,0:T(8,128)(2,1)} %bitcast.120), custom_call_target="tpu_custom_call" | custom-call | tf_op jit(solution)/shard_map/last_block/pallas_call | solution.py:114
  157.0 5.8 %all-to-all-start.8 = ((bf16[8,16,256]{2,1,0:T(8,128)(2,1)}), bf16[8,16,256]{2,1,0:T(8,128)(2,1)S(1)}, u32[]{:S(2)}, u32[]{:S(2)}) async-start(bf16[8,16,256]{2,1,0:T(8,128)(2,1)} %get-tuple-element.28), calls=%async_computation.8 | async-start | bytes 131072 | tf_op jit(solution)/shard_map/all_to_all | solution.py:55
  163.0 4.7 %all-to-all-done.8.refs_1_ = bf16[8,16,256]{2,1,0:T(8,128)(2,1)S(1)} async-done(((bf16[8,16,256]{2,1,0:T(8,128)(2,1)}), bf16[8,16,256]{2,1,0:T(8,128)(2,1)S(1)}, u32[]{:S(2)}, u32[]{:S(2)}) %all-to-all-start.8) | async-done | bytes 65568 | tf_op jit(solution)/shard_map/all_to_all | solution.py:55
  167.7 3.9 %lower_block_1.1 = (bf16[16,256]{1,0:T(8,128)(2,1)S(1)}, bf16[8,16,256]{2,1,0:T(8,128)(2,1)}) custom-call(s32[24]{0:T(128)S(1)} %select_reduce_fusion.2.refs_0_, bf16[8,16,256]{2,1,0:T(8,128)(2,1)S(1)} %all-to-all-done.8.refs_1_, f32[16,256]{1,0:T(8,128)S(1)} %convolution_subtract_fusion.1.refs_2_, bf16[32,768,256]{2,1,0:T(8,128)(2,1)} %bitcast.121), custom_call_target="tpu_custom_call" | custom-call | tf_op jit(solution)/shard_map/lower_block_1/pallas_call | solution.py:182
  171.9 4.0 %all-to-all-start.9 = ((bf16[8,16,256]{2,1,0:T(8,128)(2,1)}), bf16[8,16,256]{2,1,0:T(8,128)(2,1)S(1)}, u32[]{:S(2)}, u32[]{:S(2)}) async-start(bf16[8,16,256]{2,1,0:T(8,128)(2,1)} %get-tuple-element.31), calls=%async_computation.9 | async-start | bytes 131072 | tf_op jit(solution)/shard_map/all_to_all | solution.py:55
  176.9 3.9 %all-to-all-done.9.refs_1_ = bf16[8,16,256]{2,1,0:T(8,128)(2,1)S(1)} async-done(((bf16[8,16,256]{2,1,0:T(8,128)(2,1)}), bf16[8,16,256]{2,1,0:T(8,128)(2,1)S(1)}, u32[]{:S(2)}, u32[]{:S(2)}) %all-to-all-start.9) | async-done | bytes 65568 | tf_op jit(solution)/shard_map/all_to_all | solution.py:55
  180.8 4.0 %lower_block_0.1 = (bf16[16,256]{1,0:T(8,128)(2,1)S(1)}, bf16[8,16,256]{2,1,0:T(8,128)(2,1)S(1)}) custom-call(s32[24]{0:T(128)S(1)} %select_reduce_fusion.2.refs_0_, bf16[8,16,256]{2,1,0:T(8,128)(2,1)S(1)} %all-to-all-done.9.refs_1_, f32[16,256]{1,0:T(8,128)S(1)} %convolution_subtract_fusion.refs_2_, bf16[16,256]{1,0:T(8,128)(2,1)S(1)} %get-tuple-element.32.refs_3_, ...), custom_call_target="tpu_custom_call" | custom-call | tf_op jit(solution)/shard_map/lower_block_0/pallas_call | solution.py:182
  185.5 4.1 %all-to-all-start.10 = ((bf16[8,80,256]{2,1,0:T(8,128)(2,1)}), bf16[8,80,256]{2,1,0:T(8,128)(2,1)S(1)}, u32[]{:S(2)}, u32[]{:S(2)}) async-start(bf16[8,80,256]{2,1,0:T(8,128)(2,1)} %pad_maximum_fusion.4), calls=%async_computation.10 | async-start | bytes 655360 | tf_op jit(solution)/shard_map/all_to_all | solution.py:55
  189.7 7.1 %all-to-all-done.10 = bf16[8,80,256]{2,1,0:T(8,128)(2,1)S(1)} async-done(((bf16[8,80,256]{2,1,0:T(8,128)(2,1)}), bf16[8,80,256]{2,1,0:T(8,128)(2,1)S(1)}, u32[]{:S(2)}, u32[]{:S(2)}) %all-to-all-start.10) | async-done | bytes 327712 | tf_op jit(solution)/shard_map/all_to_all | solution.py:55
  198.9 3.9 %all-to-all-start.11 = ((bf16[32,2,256]{2,1,0:T(2,128)(2,1)}), bf16[32,2,256]{2,1,0:T(2,128)(2,1)S(1)}, u32[]{:S(2)}, u32[]{:S(2)}) async-start(bf16[32,2,256]{2,1,0:T(2,128)(2,1)} %reshape.501), calls=%async_computation.11 | async-start | bytes 65536 | tf_op jit(solution)/shard_map/all_to_all | solution.py:51
  (212 shorter events, 70.6 us)
Async XLA Ops:
  7.2 142.4 %all-gather.3.cloned.1.call-start = ((), (), s32[]{:S(2)}) async-start(), calls=%async_computation.12 | async-start | bytes 12976128 | tf_op jit(solution)/shard_map/all_gather | solution.py:235
  12.3 36.9 %collective-permute-start.2 = (bf16[512,256]{1,0:T(8,128)(2,1)}, bf16[512,256]{1,0:T(8,128)(2,1)}, u32[]{:S(2)}, u32[]{:S(2)}) collective-permute-start(bf16[512,256]{1,0:T(8,128)(2,1)} %bitcast.11), channel_id=1, source_target_pairs={{0,3},{1,2},{2,1},{3,0},{4,7},{5,6},{6,5},{7,4},{8,11},{9,10},{10,... | collective-permute-start | bytes 786440 | tf_op jit(solution)/shard_map/ppermute | solution.py:32
  15.9 35.0 %collective-permute-start.1 = (bf16[512,256]{1,0:T(8,128)(2,1)}, bf16[512,256]{1,0:T(8,128)(2,1)}, u32[]{:S(2)}, u32[]{:S(2)}) collective-permute-start(bf16[512,256]{1,0:T(8,128)(2,1)} %bitcast.11), channel_id=1, source_target_pairs={{0,2},{1,3},{2,0},{3,1},{4,6},{5,7},{6,4},{7,5},{8,10},{9,11},{10,... | collective-permute-start | bytes 786440 | tf_op jit(solution)/shard_map/ppermute | solution.py:32
  16.3 45.6 %collective-permute-start = (bf16[512,256]{1,0:T(8,128)(2,1)}, bf16[512,256]{1,0:T(8,128)(2,1)}, u32[]{:S(2)}, u32[]{:S(2)}) collective-permute-start(bf16[512,256]{1,0:T(8,128)(2,1)} %bitcast.11), channel_id=1, source_target_pairs={{0,1},{1,0},{2,3},{3,2},{4,5},{5,4},{6,7},{7,6},{8,9},{9,8},{10,11... | collective-permute-start | bytes 786440 | tf_op jit(solution)/shard_map/ppermute | solution.py:32
  20.5 15.2 %all-to-all-start = ((bf16[4,160,256]{2,1,0:T(8,128)(2,1)}), bf16[4,160,256]{2,1,0:T(8,128)(2,1)S(1)}, u32[]{:S(2)}, u32[]{:S(2)}) async-start(bf16[4,160,256]{2,1,0:T(8,128)(2,1)} %pad_maximum_fusion.3), calls=%async_computation | async-start | bytes 655360 | tf_op jit(solution)/shard_map/all_to_all | solution.py:28
  39.9 16.0 %all-to-all-start.1 = ((bf16[8,16,256]{2,1,0:T(8,128)(2,1)}), bf16[8,16,256]{2,1,0:T(8,128)(2,1)}, u32[]{:S(2)}, u32[]{:S(2)}) async-start(bf16[8,16,256]{2,1,0:T(8,128)(2,1)} %select_reduce_fusion.1), calls=%async_computation.1 | async-start | bytes 131072 | tf_op jit(solution)/shard_map/all_to_all | solution.py:47
  58.5 10.5 %all-to-all-start.2 = ((bf16[8,16,256]{2,1,0:T(8,128)(2,1)}), bf16[8,16,256]{2,1,0:T(8,128)(2,1)S(1)}, u32[]{:S(2)}, u32[]{:S(2)}) async-start(bf16[8,16,256]{2,1,0:T(8,128)(2,1)} %broadcast_in_dim.169), calls=%async_computation.2 | async-start | bytes 131072 | tf_op jit(solution)/shard_map/all_to_all | solution.py:47
  71.5 18.2 %all-to-all-start.3 = ((bf16[8,16,4,256]{3,1,2,0:T(8,128)(2,1)}), bf16[8,16,4,256]{3,1,2,0:T(8,128)(2,1)S(1)}, u32[]{:S(2)}, u32[]{:S(2)}) async-start(bf16[8,16,4,256]{3,1,2,0:T(8,128)(2,1)} %broadcast_in_dim.172), calls=%async_computation.3 | async-start | bytes 524288 | tf_op jit(solution)/shard_map/all_to_all | solution.py:55
  86.3 9.0 %collective-permute-start.5 = (bf16[48,256]{1,0:T(8,128)(2,1)S(1)}, bf16[48,256]{1,0:T(8,128)(2,1)S(1)}, u32[]{:S(2)}, u32[]{:S(2)}) collective-permute-start(bf16[48,256]{1,0:T(8,128)(2,1)S(1)} %bitcast.143), channel_id=1, source_target_pairs={{0,3},{1,2},{2,1},{3,0},{4,7},{5,6},{6,5},{7,4},{8,11},{9,10},{10,... | collective-permute-start | bytes 73736 | tf_op jit(solution)/shard_map/ppermute | solution.py:32
  86.6 8.7 %collective-permute-start.4 = (bf16[48,256]{1,0:T(8,128)(2,1)S(1)}, bf16[48,256]{1,0:T(8,128)(2,1)S(1)}, u32[]{:S(2)}, u32[]{:S(2)}) collective-permute-start(bf16[48,256]{1,0:T(8,128)(2,1)S(1)} %bitcast.144), channel_id=1, source_target_pairs={{0,2},{1,3},{2,0},{3,1},{4,6},{5,7},{6,4},{7,5},{8,10},{9,11},{10,... | collective-permute-start | bytes 73736 | tf_op jit(solution)/shard_map/ppermute | solution.py:32
  87.7 7.6 %collective-permute-start.3 = (bf16[48,256]{1,0:T(8,128)(2,1)S(1)}, bf16[48,256]{1,0:T(8,128)(2,1)S(1)}, u32[]{:S(2)}, u32[]{:S(2)}) collective-permute-start(bf16[48,256]{1,0:T(8,128)(2,1)S(1)} %bitcast.145), channel_id=1, source_target_pairs={{0,1},{1,0},{2,3},{3,2},{4,5},{5,4},{6,7},{7,6},{8,9},{9,8},{10,11... | collective-permute-start | bytes 73736 | tf_op jit(solution)/shard_map/ppermute | solution.py:32
  91.9 11.2 %all-to-all-start.4 = ((bf16[8,16,256]{2,1,0:T(8,128)(2,1)}), bf16[8,16,256]{2,1,0:T(8,128)(2,1)S(1)}, u32[]{:S(2)}, u32[]{:S(2)}) async-start(bf16[8,16,256]{2,1,0:T(8,128)(2,1)} %select_reduce_fusion), calls=%async_computation.4 | async-start | bytes 131072 | tf_op jit(solution)/shard_map/all_to_all | solution.py:47
  104.0 11.9 %all-to-all-start.5 = ((bf16[8,22,256]{2,1,0:T(8,128)(2,1)}), bf16[8,22,256]{2,1,0:T(8,128)(2,1)S(1)}, u32[]{:S(2)}, u32[]{:S(2)}) async-start(bf16[8,22,256]{2,1,0:T(8,128)(2,1)} %pad_maximum_fusion.6), calls=%async_computation.5 | async-start | bytes 196608 | tf_op jit(solution)/shard_map/all_to_all | solution.py:47
  118.0 15.0 %all-to-all-start.6 = ((bf16[8,16,4,256]{3,1,2,0:T(8,128)(2,1)}), bf16[8,16,4,256]{3,1,2,0:T(8,128)(2,1)S(1)}, u32[]{:S(2)}, u32[]{:S(2)}) async-start(bf16[8,16,4,256]{3,1,2,0:T(8,128)(2,1)} %broadcast_in_dim.178), calls=%async_computation.6 | async-start | bytes 524288 | tf_op jit(solution)/shard_map/all_to_all | solution.py:55
  133.9 15.7 %all-to-all-start.7 = ((bf16[32,16,256]{2,1,0:T(8,128)(2,1)}), bf16[32,16,256]{2,1,0:T(8,128)(2,1)S(1)}, u32[]{:S(2)}, u32[]{:S(2)}) async-start(bf16[32,16,256]{2,1,0:T(8,128)(2,1)} %bitcast.26), calls=%async_computation.7 | async-start | bytes 524288 | tf_op jit(solution)/shard_map/all_to_all | solution.py:47
  153.1 18.5 %collective-permute-start.6 = (bf16[48,256]{1,0:T(8,128)(2,1)S(1)}, bf16[48,256]{1,0:T(8,128)(2,1)S(1)}, u32[]{:S(2)}, u32[]{:S(2)}) collective-permute-start(bf16[48,256]{1,0:T(8,128)(2,1)S(1)} %pad_maximum_fusion.11), channel_id=1, source_target_pairs={{0,1},{1,0},{2,3},{3,2},{4,5},{5,4},{6,7},{7,6},{8,9},{9,8},{10,11... | collective-permute-start | bytes 73736 | tf_op jit(solution)/shard_map/ppermute | solution.py:32
  153.2 18.4 %collective-permute-start.7 = (bf16[48,256]{1,0:T(8,128)(2,1)S(1)}, bf16[48,256]{1,0:T(8,128)(2,1)S(1)}, u32[]{:S(2)}, u32[]{:S(2)}) collective-permute-start(bf16[48,256]{1,0:T(8,128)(2,1)S(1)} %pad_maximum_fusion.11), channel_id=1, source_target_pairs={{0,2},{1,3},{2,0},{3,1},{4,6},{5,7},{6,4},{7,5},{8,10},{9,11},{10,... | collective-permute-start | bytes 73736 | tf_op jit(solution)/shard_map/ppermute | solution.py:32
  154.5 17.0 %collective-permute-start.8 = (bf16[48,256]{1,0:T(8,128)(2,1)S(1)}, bf16[48,256]{1,0:T(8,128)(2,1)S(1)}, u32[]{:S(2)}, u32[]{:S(2)}) collective-permute-start(bf16[48,256]{1,0:T(8,128)(2,1)S(1)} %pad_maximum_fusion.11), channel_id=1, source_target_pairs={{0,3},{1,2},{2,1},{3,0},{4,7},{5,6},{6,5},{7,4},{8,11},{9,10},{10,... | collective-permute-start | bytes 73736 | tf_op jit(solution)/shard_map/ppermute | solution.py:32
  157.0 10.6 %all-to-all-start.8 = ((bf16[8,16,256]{2,1,0:T(8,128)(2,1)}), bf16[8,16,256]{2,1,0:T(8,128)(2,1)S(1)}, u32[]{:S(2)}, u32[]{:S(2)}) async-start(bf16[8,16,256]{2,1,0:T(8,128)(2,1)} %get-tuple-element.28), calls=%async_computation.8 | async-start | bytes 131072 | tf_op jit(solution)/shard_map/all_to_all | solution.py:55
  171.9 8.9 %all-to-all-start.9 = ((bf16[8,16,256]{2,1,0:T(8,128)(2,1)}), bf16[8,16,256]{2,1,0:T(8,128)(2,1)S(1)}, u32[]{:S(2)}, u32[]{:S(2)}) async-start(bf16[8,16,256]{2,1,0:T(8,128)(2,1)} %get-tuple-element.31), calls=%async_computation.9 | async-start | bytes 131072 | tf_op jit(solution)/shard_map/all_to_all | solution.py:55
  185.5 11.2 %all-to-all-start.10 = ((bf16[8,80,256]{2,1,0:T(8,128)(2,1)}), bf16[8,80,256]{2,1,0:T(8,128)(2,1)S(1)}, u32[]{:S(2)}, u32[]{:S(2)}) async-start(bf16[8,80,256]{2,1,0:T(8,128)(2,1)} %pad_maximum_fusion.4), calls=%async_computation.10 | async-start | bytes 655360 | tf_op jit(solution)/shard_map/all_to_all | solution.py:55
  197.7 5.1 %collective-permute-start.9 = (bf16[64,256]{1,0:T(8,128)(2,1)S(1)}, bf16[64,256]{1,0:T(8,128)(2,1)S(1)}, u32[]{:S(2)}, u32[]{:S(2)}) collective-permute-start(bf16[64,256]{1,0:T(8,128)(2,1)S(1)} %slice_reduce_fusion), channel_id=1, source_target_pairs={{0,32},{32,0},{64,96},{96,64},{128,160},{160,128},{192,224},{224,1... | collective-permute-start | bytes 98312 | tf_op jit(solution)/shard_map/ppermute | solution.py:36
  198.9 12.5 %all-to-all-start.11 = ((bf16[32,2,256]{2,1,0:T(2,128)(2,1)}), bf16[32,2,256]{2,1,0:T(2,128)(2,1)S(1)}, u32[]{:S(2)}, u32[]{:S(2)}) async-start(bf16[32,2,256]{2,1,0:T(2,128)(2,1)} %reshape.501), calls=%async_computation.11 | async-start | bytes 65536 | tf_op jit(solution)/shard_map/all_to_all | solution.py:51
  203.2 5.3 %collective-permute-start.11 = (bf16[2,64,256]{2,1,0:T(8,128)(2,1)S(1)}, bf16[2,64,256]{2,1,0:T(8,128)(2,1)S(1)}, u32[]{:S(2)}, u32[]{:S(2)}) collective-permute-start(bf16[2,64,256]{2,1,0:T(8,128)(2,1)S(1)} %pad_maximum_fusion.10), channel_id=1, source_target_pairs={{0,128},{32,160},{64,192},{96,224},{128,0},{160,32},{192,64},{224,... | collective-permute-start | bytes 196616 | tf_op jit(solution)/shard_map/ppermute | solution.py:36
  (28 other events, 475.0 us)
Sparse Core Ops, SparseCore 0:
  11.2 127.1 all-gather.2

commit v5 on v4

--- a/solution.py
+++ b/solution.py
@@ -22,6 +22,10 @@
 LOWER_AT = UPPER_AT + PIECE
 PACK = LOWER_AT + (STEPS - 1) * TILE
 ROWS = 16
+GRANT = 49 << 20
+VMEM = pl.BlockSpec(memory_space=pltpu.VMEM)
+SMEM = pl.BlockSpec(memory_space=pltpu.SMEM)
+HBM = pl.BlockSpec(memory_space=pltpu.HBM)
 
 
 def swap_y(x):
@@ -99,7 +103,12 @@
     for copy in copies:
         copy.start()
     copies[0].wait()
-    block = jnp.concatenate([got[pos[place]] for place in range(PER)], axis=1)
+    _, y = plane()
+    block = []
+    for place in range(PER):
+        at = pos[(STEPS - 1) * PER + place]
+        block.append(got[at - at % NY + ((at % NY) ^ y)])
+    block = jnp.concatenate(block, axis=1)
     value = dot_nn(block, upper[...].reshape(NB, TILE)).astype(BF)
     solved_out[...] = value
     resid = (dot_nn(pick_own[...], value) - outer[...]).astype(BF)
@@ -130,73 +139,172 @@
             pltpu.VMEM((NC, PIECE, TILE), BF),
             pltpu.SemaphoreType.DMA((2,)),
         ],
-        compiler_params=pltpu.CompilerParams(vmem_limit_bytes=50 << 20),
+        compiler_params=pltpu.CompilerParams(vmem_limit_bytes=GRANT),
         name="last_block",
     )(pos, got, pick_own, outer, pack)
 
 
-def lower_kernel(step, pos, back, base, *rest):
-    known = rest[: STEPS - 2 - step]
-    pack, value_out, message_out, tiles, inverse, sems = rest[STEPS - 2 - step :]
-    later = list(range(step + 1, STEPS))
-    first = pltpu.make_async_copy(
-        pack.at[:, pl.ds(step * PIECE, PIECE), :], inverse, sems.at[len(later) * PER]
-    )
-    copies = []
-    for at, block in enumerate(later):
-        for place in range(PER):
-            slot = at * PER + place
-            copy = pltpu.make_async_copy(
-                pack.at[pos[block * PER + place], pl.ds(LOWER_AT + step * TILE, TILE), :],
-                tiles.at[at, :, pl.ds(place * TILE, TILE)],
-                sems.at[slot],
-            )
-            copy.start()
-            copies.append(copy)
-    first.start()
+def call(kernel, name, outs, in_specs, args, scratch=(), out_specs=None, grant=None):
+    return pl.pallas_call(
+        kernel,
+        out_shape=tuple(jax.ShapeDtypeStruct(shape, dtype) for shape, dtype in outs),
+        in_specs=in_specs,
+        out_specs=tuple(out_specs or [VMEM] * len(outs)),
+        scratch_shapes=list(scratch),
+        compiler_params=pltpu.CompilerParams(vmem_limit_bytes=grant or 8 << 20),
+        name=name,
+    )(*args)
+
+
+def pack_kernel(lower_inverse, upper_inverse, lower, out):
+    out[pl.ds(0, UPPER_AT), :] = lower_inverse[...].reshape(UPPER_AT, TILE)
+    out[pl.ds(UPPER_AT, PIECE), :] = upper_inverse[0]
+    out[pl.ds(LOWER_AT, PACK - LOWER_AT), :] = lower[...].reshape(PACK - LOWER_AT, TILE)
+
+
+def pos_kernel(tile_of, pos):
+    stride = tile_of.shape[0] // NC
+
+    def put(index, carry):
+        pos[tile_of[index * stride]] = index
+        return carry
+
+    lax.fori_loop(0, NC, put, 0)
+
+
+def plane():
+    col = lax.axis_index("pcol")
+    return col // NY, col % NY
+
+
+def plane_tile(tile_of, z, other):
+    return tile_of[(z * NY + other) * (tile_of.shape[0] // NC)]
+
+
+def first_kernel(tile_of, got, tiles, routed):
+    z, y = plane()
+    routed[...] = jnp.zeros_like(routed)
+    for step in range(NY):
+        other = y ^ step
+        value = got[other, pl.ds(0, ROWS), :].astype(F32)
+        value = value + got[other, pl.ds(ROWS, ROWS), :].astype(F32)
+        tiles[step] = value
+        tile = plane_tile(tile_of, z, other)
+
+        @pl.when(tile // PER == 0)
+        def _():
+            routed[tile % PER] = value.astype(BF)
+
+
+def inverse_kernel(step, back, got, *rest):
+    message = rest[-1]
+    mine = jnp.sum(back[...].astype(F32), axis=0).astype(BF)
+    at = 2 * ROWS + step * PIECE
+    weights = jnp.concatenate([got[other, pl.ds(at, PIECE), :] for other in range(NY)], axis=0)
+    part = dot_nn(mine, weights).astype(BF)
+    for index in range(NZ):
+        message[index, pl.ds(0, ROWS), :] = part
+        if len(rest) > 1:
+            message[index, pl.ds(ROWS, ROWS), :] = rest[0][index]
+
+
+def update_kernel(step, back, own, near_1, near_2, near_3, solved_out, message, *outer):
+    sums = jnp.sum(back[...].astype(F32), axis=0)
+    value = sums[:ROWS].astype(BF)
+    solved_out[...] = value
+    if outer:
+        outer[0][...] = sums[ROWS:]
+    for index, near in enumerate((own, near_1, near_2, near_3)):
+        update = dot_nn(value, near[pl.ds(step * TILE, TILE), :]).astype(BF)
+        for other in range(NP):
+            message[other, pl.ds(index * ROWS, ROWS), :] = update
+
+
+def state_kernel(step, tile_of, back, tiles, *outs):
+    z, y = plane()
+    sums = jnp.sum(back[...].astype(F32), axis=0)
+    if step == 0:
+        later, routed = outs
+        routed[...] = jnp.zeros_like(routed)
+    for index in range(NY):
+        tile = plane_tile(tile_of, z, y ^ index)
+        keep = (tile // PER > step).astype(F32)
+        value = tiles[index] - keep * sums[index * ROWS : (index + 1) * ROWS]
+        if step == 0:
+            later[index] = value
+
+            @pl.when(tile // PER == 1)
+            def _():
+                routed[tile % PER] = value.astype(BF)
+
+        else:
+            for other in range(NZ):
+                outs[0][other * NY + index] = value.astype(BF)
+
+
+def fetch_kernel(step, pos, pack, tiles, inverse, sems):
+    copies = [
+        pltpu.make_async_copy(
+            pack.at[pos[(step + 1 + at) * PER + place], pl.ds(LOWER_AT + step * TILE, TILE), :],
+            tiles.at[at, :, pl.ds(place * TILE, TILE)],
+            sems.at[at * PER + place],
+        )
+        for at in range(STEPS - 1 - step)
+        for place in range(PER)
+    ]
+    copies.append(
+        pltpu.make_async_copy(
+            pack.at[:, pl.ds(step * PIECE, PIECE), :], inverse, sems.at[len(copies)]
+        )
+    )
+    for copy in copies:
+        copy.start()
+    for copy in copies:
+        copy.wait()
+
+
+def fetch_call(step, pos, pack):
+    later = STEPS - 1 - step
+    return call(
+        lambda *refs: fetch_kernel(step, *refs),
+        f"fetch_block_{step}",
+        [((later, TILE, NB), BF), ((NC, PIECE, TILE), BF)],
+        [SMEM, HBM],
+        (pos, pack),
+        [pltpu.SemaphoreType.DMA((later * PER + 1,))],
+        grant=GRANT,
+    )
+
+
+def lower_kernel(step, back, base, tiles, inverse, *rest):
+    known = rest[:-2]
+    value_out, message_out = rest[-2:]
     value = jnp.sum(back[...].astype(F32), axis=0).astype(BF)
     value_out[...] = value
     sums = jnp.zeros((ROWS, TILE), F32)
-    for at in reversed(range(len(later))):
+    for at in range(STEPS - 1 - step):
         solved = value if at == 0 else known[at - 1][...]
         wide = jnp.concatenate(
             [jnp.where(place_mask(place), solved, jnp.zeros_like(solved)) for place in range(PER)],
             axis=1,
         )
-        for place in range(PER):
-            copies[at * PER + place].wait()
         sums = sums + dot_nt(wide, tiles[at])
     sums = jnp.sum(sums.reshape(ROWS // PER, PER, TILE), axis=1, keepdims=True)
     sums = jnp.broadcast_to(sums, (ROWS // PER, PER, TILE)).reshape(ROWS, TILE)
-    resid = (base[...] - sums).astype(BF)
-    first.wait()
-    part = lower_part(resid, inverse)
+    part = lower_part((base[...] - sums).astype(BF), inverse)
     for index in range(NP):
         message_out[index] = part
 
 
-def lower_call(step, pos, back, base, known, pack):
-    vmem = pl.BlockSpec(memory_space=pltpu.VMEM)
-    later = STEPS - 1 - step
-    count = later * PER
-    return pl.pallas_call(
+def lower_call(step, back, base, weights, known):
+    return call(
         lambda *refs: lower_kernel(step, *refs),
-        out_shape=(
-            jax.ShapeDtypeStruct((ROWS, TILE), BF),
-            jax.ShapeDtypeStruct((NP, ROWS, TILE), BF),
-        ),
-        in_specs=[pl.BlockSpec(memory_space=pltpu.SMEM), vmem, vmem]
-        + [vmem] * len(known)
-        + [pl.BlockSpec(memory_space=pltpu.HBM)],
-        out_specs=(vmem, vmem),
-        scratch_shapes=[
-            pltpu.VMEM((later, TILE, NB), BF),
-            pltpu.VMEM((NC, PIECE, TILE), BF),
-            pltpu.SemaphoreType.DMA((count + 1,)),
-        ],
-        compiler_params=pltpu.CompilerParams(vmem_limit_bytes=50 << 20),
-        name=f"lower_block_{step}",
-    )(pos, back, base, *known, pack)
+        f"lower_block_{step}",
+        [((ROWS, TILE), BF), ((NP, ROWS, TILE), BF)],
+        [VMEM] * (4 + len(known)),
+        (back, base, *weights, *known),
+        grant=16 << 20,
+    )
 
 
 def body(rhs, pivots, tile_of, upper_rows, upper_inv, lower_rows, lower_inv, solved):
@@ -212,26 +320,20 @@
     my_tile = first_tiles[col]
     my_block = my_tile // PER
     my_place = my_tile % PER
-    plane_tiles = jnp.stack([first_tiles[z * NY + (y ^ step)] for step in range(NY)])
-    plane_blocks = plane_tiles // PER
-    pos = jnp.sum(
-        jnp.where(
-            first_tiles[None, :] == jnp.arange(STEPS * PER)[:, None],
-            jnp.arange(NC, dtype=jnp.int32)[None, :],
-            0,
-        ),
-        axis=1,
-        dtype=jnp.int32,
-    )
-
-    pack = jnp.concatenate(
-        [
-            jnp.swapaxes(lower_inv, 1, 2).reshape(STEPS * PIECE, TILE),
-            upper_inv[STEPS - 1],
-            lower_rows[: STEPS - 1, :, :TILE].reshape((STEPS - 1) * TILE, TILE),
+
+    pack = pl.pallas_call(
+        pack_kernel,
+        out_shape=jax.ShapeDtypeStruct((PACK, TILE), BF),
+        grid=(1,),
+        in_specs=[
+            pl.BlockSpec((STEPS, PIECE, TILE), lambda at: (0, 0, 0)),
+            pl.BlockSpec((1, PIECE, TILE), lambda at: (STEPS - 1, 0, 0)),
+            pl.BlockSpec((STEPS - 1, TILE, TILE), lambda at: (0, 0, 0)),
         ],
-        axis=0,
-    )
+        out_specs=pl.BlockSpec((PACK, TILE), lambda at: (0, 0)),
+        compiler_params=pltpu.CompilerParams(vmem_limit_bytes=8 << 20),
+        name="pack_window",
+    )(jnp.swapaxes(lower_inv, 1, 2), upper_inv, lower_rows)
     pack_all = lax.all_gather(pack, "pcol", axis=0)
 
     local_pivots = pivots - col * width
@@ -240,36 +342,36 @@
     own_high = own.astype(BF)
     own_low = (own - own_high.astype(F32)).astype(BF)
     first_inverses = upper_inv[: STEPS - 1].reshape((STEPS - 1) * PIECE, TILE)
-    got = swap_y(jnp.concatenate([own_high, own_low, to_all(first_inverses, NY)], axis=1))
-    tiles = got[:, :rows_z].astype(F32) + got[:, rows_z : 2 * rows_z].astype(F32)
-    tiles = jnp.stack(
-        [lax.dynamic_index_in_dim(tiles, y ^ step, 0, False) for step in range(NY)]
-    )
-    inverse = []
-    for step in range(STEPS - 1):
-        start = 2 * rows_z + step * PIECE
-        inverse.append(got[:, start : start + PIECE].reshape(TILE, TILE))
-
+    start = swap_y(jnp.concatenate([own_high, own_low, to_all(first_inverses, NY)], axis=1))
+    tiles, routed = call(
+        first_kernel,
+        "first_state",
+        [((NY, ROWS, TILE), F32), ((NZ, ROWS, TILE), BF)],
+        [SMEM, VMEM],
+        (tile_of, start),
+    )
     upper_pack = upper_rows[: STEPS - 1, :, :TILE].reshape((STEPS - 1) * TILE, TILE)
     near = [upper_pack] + [pass_y(upper_pack, step) for step in range(1, NY)]
-    upper_tiles = [
-        jnp.stack([part[step * TILE : (step + 1) * TILE] for part in near])
-        for step in range(STEPS - 1)
-    ]
+    routed, solved_now, tile_now = lax.optimization_barrier((routed, solved, tile_of))
+    (pos,) = call(
+        pos_kernel, "tile_places", [((NC,), jnp.int32)], [SMEM], (tile_now,), out_specs=[SMEM]
+    )
 
     finished = []
     for step in range(STEPS - 1):
-        block = tiles.astype(BF)
-        pick = plane_tiles[None, :] == step * PER + jnp.arange(NZ)[:, None]
-        routed = jnp.sum(jnp.where(pick[:, :, None, None], block[None], 0), axis=1)
-        if step == 0:
-            routed, solved_now = lax.optimization_barrier((routed, solved))
         if step == 1:
             routed, rhs_now = lax.optimization_barrier((routed, rhs))
             state0 = jnp.take(rhs_now, local_pivots, axis=1)
-        mine = jnp.sum(swap_z(routed), axis=0)
-        part = jnp.dot(mine, inverse[step], preferred_element_type=F32).astype(BF)
-        message = to_all(part, NZ)
+        back = swap_z(routed)
+        extra = [outer] if step == 1 else []
+        rows = ROWS * (1 + step)
+        (message,) = call(
+            lambda *refs: inverse_kernel(step, *refs),
+            f"inverse_part_{step}",
+            [((NZ, rows, TILE), BF)],
+            [VMEM] * (2 + len(extra)),
+            (back, start, *extra),
+        )
         if step == 0:
             slot_known = jnp.where(my_block >= STEPS, solved_now[:, :TILE], 0.0)
             known = jnp.concatenate([slot_known, solved_now[:, TILE:]], axis=1).astype(BF)
@@ -283,40 +385,55 @@
                 theirs = lax.dynamic_index_in_dim(outer, y ^ other, 0, False)
                 outer_sum = outer_sum + pass_y(theirs, other).astype(F32)
             outer = outer_sum.astype(BF).reshape(NZ, rows_own * STEPS, TILE)
+            outer = jnp.pad(outer, ((0, 0), (0, ROWS - rows_own * STEPS), (0, 0)))
+        outs = [((ROWS, TILE), BF), ((NP, NY * ROWS, TILE), BF)]
         if step == 1:
-            message = jnp.concatenate([message, outer], axis=1)
-        back = total(swap_z(message))
-        solved_rows = back[:rows_z].astype(BF)
-        if step == 1:
-            outer = back[rows_z:].reshape(rows_own, STEPS, TILE)
-        finished.append(solved_rows)
-        update = lax.dot_general(
-            solved_rows, upper_tiles[step], (((1,), (1,)), ((), ())), preferred_element_type=F32
-        )
-        update = total(swap_prow(to_all(update.astype(BF), NP)))
-        update = update.transpose(1, 0, 2)
-        tiles = tiles - jnp.where((plane_blocks > step)[:, None, None], update, 0.0)
-
-    got = swap_z(to_all(tiles.astype(BF), NZ).reshape(NZ * NY, rows_z, TILE))
+            outs.append(((ROWS, TILE), F32))
+        value, message, *sums = call(
+            lambda *refs: update_kernel(step, *refs),
+            f"upper_update_{step}",
+            outs,
+            [VMEM] * (1 + NY),
+            (swap_z(message), *near),
+        )
+        finished.append(value)
+        outs = [((NZ * NY, ROWS, TILE), BF)]
+        if step == 0:
+            outs = [((NY, ROWS, TILE), F32), ((NZ, ROWS, TILE), BF)]
+        found = call(
+            lambda *refs: state_kernel(step, *refs),
+            f"next_state_{step}",
+            outs,
+            [SMEM, VMEM, VMEM],
+            (tile_of, swap_prow(message), tiles),
+        )
+        if step == 0:
+            tiles, routed = found
+
+    got = swap_z(found[0])
     order = jnp.arange(ROWS)
     pick_own = (
         (order[None, :] // rows_own == z) & (order[None, :] % rows_own == order[:, None] // PER)
     ).astype(BF)
+    outer = sums[0][: rows_own * STEPS].reshape(rows_own, STEPS, TILE)
     outer = jnp.repeat(outer.transpose(1, 0, 2), PER, axis=1)
-    last_pos = pos[(STEPS - 1) * PER :]
-    last_pos = last_pos - last_pos % NY + ((last_pos % NY) ^ y)
-    last, message = last_call(last_pos, got, pick_own, outer[STEPS - 1], pack_all)
+    last, message = last_call(pos, got, pick_own, outer[STEPS - 1], pack_all)
     finished.append(last)
     bases = [
         jnp.dot(pick_own, finished[step], preferred_element_type=F32) - outer[step]
         for step in range(STEPS - 1)
     ]
 
-    stacked, message = lax.optimization_barrier((jnp.concatenate(finished, axis=0), message))
+    message, pos_now = lax.optimization_barrier((message, pos))
+    weights = fetch_call(1, pos_now, pack_all)
+    back = swap_prow(message)
+    last, message = lower_call(1, back, bases[1], weights, [])
+
+    message, stacked, pos_now = lax.optimization_barrier(
+        (message, jnp.concatenate(finished, axis=0), pos)
+    )
+    weights = fetch_call(0, pos_now, pack_all)
     every = [stacked] + [pass_y(stacked, step) for step in range(1, NY)]
-    back = swap_prow(message)
-    last, message = lower_call(1, pos, back, bases[1], [], pack_all)
-    message, every = lax.optimization_barrier((message, every))
     every = by_place(every, y, NY).reshape(NY, STEPS, NZ, rows_own, TILE)
     every = every.transpose(1, 2, 0, 3, 4).reshape(STEPS, count, TILE)
     bulk = jnp.dot(
@@ -332,7 +449,7 @@
     bulk = bulk.reshape(NP, count // NP * slots, TILE)
 
     back = swap_prow(message)
-    middle, message = lower_call(0, pos, back, bases[0], [last], pack_all)
+    middle, message = lower_call(0, back, bases[0], weights, [last])
     back = swap_prow(jnp.concatenate([message, bulk], axis=1))
     first = total(back[:, :ROWS]).astype(BF)
 

time: 221 us -> 217 us (0.982)
  other arithmetic: 20.1 us -> 7.1 us
  Pallas kernels: 11.3 us -> 22 us
  starting transfers between devices: 79.5 us -> 83.6 us
  local copies, waits for them, and re-layouts: 28.6 us -> 24.9 us
    pallas_call x2 -> x13, Pallas kernels: 7.83 us -> 18.6 us  [the longest x12 17.8 us: call(): pl.pallas_call(kernel, out_shape=tuple((jax.ShapeDtypeStruct(shape, dtype...]
    all_to_all x5, waiting for transfers between devices: 15.6 us -> 8.51 us  [swap_prow(): return lax.all_to_all(x, 'prow', 0, 0, tiled=True)]
    unnamed x66 -> x50, local copies, waits for them, and re-layouts: 0.86 us -> 6.49 us
    another operation x3 -> x0, local copies, waits for them, and re-layouts: 4.96 us -> none  [body(): jnp.stack([part[step * TILE:(step + 1) * TILE] for part in near])]
    all_gather x1, waiting for transfers between devices: 0.01 us -> 4.72 us  [body(): pack_all = lax.all_gather(pack, 'pcol', axis=0)]
    reduce_sum x5 -> x0, other arithmetic: 3.76 us -> none  [the longest x2 2.11 us: body(): routed = jnp.sum(jnp.where(pick[:, :, None, None], block[None], 0), axis=1)]
    gt x2 -> x0, other arithmetic: 3.76 us -> none  [body(): tiles = tiles - jnp.where((plane_blocks > step)[:, None, None], update, 0.0)]
    dot_general x4 -> x0, matrix products: 3.59 us -> none  [the longest x2 2.41 us: body(): lax.dot_general(solved_rows, upper_tiles[step], (((1,), (1,)), ((), ())),...]
  transfers between devices with their start and end apart: 26 -> 26, of which waited for: 11 -> 11; matrix products, arithmetic and copies ran while one was open for 23% -> 14% of each run, Pallas kernels for 2% -> 7%
where the time goes in v5:
time: 217 us; the launch traced here: 215 us
  starting transfers between devices  83.6 us (39%)
  waiting for transfers between devices  54.3 us (25%)
  local copies, waits for them, and re-layouts  24.9 us (11%)
  Pallas kernels  22 us (10%)
  between operations  17.3 us (8%)
  other arithmetic  7.1 us (3%)
  matrix products  5.9 us (3%)
    all_to_all x5, waiting for transfers between devices, swap_z(): lax.all_to_all(x, 'pcol', 0, 0, axis_index_groups=Z_GROUPS, tiled=True)  37.5 us
    all_to_all x5, starting transfers between devices, swap_prow(): return lax.all_to_all(x, 'prow', 0, 0, tiled=True)  32.7 us
    all_to_all x5, starting transfers between devices, swap_z(): lax.all_to_all(x, 'pcol', 0, 0, axis_index_groups=Z_GROUPS, tiled=True)  24.8 us
    pallas_call x12, Pallas kernels, call(): pl.pallas_call(kernel, out_shape=tuple((jax.ShapeDtypeStruct(shape, dtype...  17.8 us
    ppermute x9, starting transfers between devices, pass_y(): return lax.ppermute(x, 'pcol', [(at, at ^ step) for at in range(NC)])  10.5 us
    all_to_all x5, waiting for transfers between devices, swap_prow(): return lax.all_to_all(x, 'prow', 0, 0, tiled=True)  8.51 us
    gather x2, local copies, waits for them, and re-layouts, body(): state0 = jnp.take(rhs_now, local_pivots, axis=1)  6.58 us
    unnamed x50, local copies, waits for them, and re-layouts  6.49 us
  transfers between devices with their start and end apart: 26, of which 11 were waited for; matrix products, arithmetic and copies ran while one was open for 14% of the time, Pallas kernels for 7%

profile of v5, /device:TPU:1, one launch (start us, length us, event | category | flops | bytes accessed | tf_op | source)
XLA Modules:
  0.0 215.2 jit_solution(579679830038671050)
XLA Ops:
  13.7 5.0 %all-to-all-start = ((bf16[4,160,256]{2,1,0:T(8,128)(2,1)}), bf16[4,160,256]{2,1,0:T(8,128)(2,1)S(1)}, u32[]{:S(2)}, u32[]{:S(2)}) async-start(bf16[4,160,256]{2,1,0:T(8,128)(2,1)} %pad_maximum_fusion.2), calls=%async_computation | async-start | bytes 655360 | tf_op jit(solution)/shard_map/all_to_all | solution.py:32
  26.8 8.2 %all-to-all-start.1 = ((bf16[8,16,256]{2,1,0:T(8,128)(2,1)}), bf16[8,16,256]{2,1,0:T(8,128)(2,1)S(1)}, u32[]{:S(2)}, u32[]{:S(2)}) async-start(bf16[8,16,256]{2,1,0:T(8,128)(2,1)} %copy-done.8), calls=%async_computation.1 | async-start | bytes 131072 | tf_op jit(solution)/shard_map/all_to_all | solution.py:51
  43.5 6.5 %all-to-all-start.2 = ((bf16[8,16,256]{2,1,0:T(8,128)(2,1)}), bf16[8,16,256]{2,1,0:T(8,128)(2,1)S(1)}, u32[]{:S(2)}, u32[]{:S(2)}) async-start(bf16[8,16,256]{2,1,0:T(8,128)(2,1)} %copy-done.3), calls=%async_computation.2 | async-start | bytes 131072 | tf_op jit(solution)/shard_map/all_to_all | solution.py:51
  51.5 6.1 %all-to-all-done.2.refs_0_ = bf16[8,16,256]{2,1,0:T(8,128)(2,1)S(1)} async-done(((bf16[8,16,256]{2,1,0:T(8,128)(2,1)}), bf16[8,16,256]{2,1,0:T(8,128)(2,1)S(1)}, u32[]{:S(2)}, u32[]{:S(2)}) %all-to-all-start.2) | async-done | bytes 65568 | tf_op jit(solution)/shard_map/all_to_all | solution.py:51
  59.7 9.3 %all-to-all-start.3 = ((bf16[8,64,256]{2,1,0:T(8,128)(2,1)}), bf16[8,64,256]{2,1,0:T(8,128)(2,1)}, u32[]{:S(2)}, u32[]{:S(2)}) async-start(bf16[8,64,256]{2,1,0:T(8,128)(2,1)} %copy-done.4), calls=%async_computation.3 | async-start | bytes 524288 | tf_op jit(solution)/shard_map/all_to_all | solution.py:59
  69.0 2.8 %convolution_convert_fusion = bf16[64,3,256]{2,0,1:T(8,128)(2,1)} fusion(bf16[3,256,2048]{2,1,0:T(8,128)(2,1)S(1)} %copy-done.1, bf16[64,1792]{1,0:T(8,128)(2,1)} %slice.150, bf16[64,256]{1,0:T(8,128)(2,1)} %select_convert_fusion), kind=kOutput, calls=%fused_computation.2 | convolution fusion | flops 201900032 | bytes 3506176 | tf_op jit(solution)/shard_map/dot_general | solution.py:378
  78.1 3.4 %all-to-all-start.4 = ((bf16[8,16,256]{2,1,0:T(8,128)(2,1)}), bf16[8,16,256]{2,1,0:T(8,128)(2,1)S(1)}, u32[]{:S(2)}, u32[]{:S(2)}) async-start(bf16[8,16,256]{2,1,0:T(8,128)(2,1)} %get-tuple-element.41), calls=%async_computation.4 | async-start | bytes 131072 | tf_op jit(solution)/shard_map/all_to_all | solution.py:51
  81.5 7.3 %all-to-all-done.4.refs_0_ = bf16[8,16,256]{2,1,0:T(8,128)(2,1)S(1)} async-done(((bf16[8,16,256]{2,1,0:T(8,128)(2,1)}), bf16[8,16,256]{2,1,0:T(8,128)(2,1)S(1)}, u32[]{:S(2)}, u32[]{:S(2)}) %all-to-all-start.4) | async-done | bytes 65568 | tf_op jit(solution)/shard_map/all_to_all | solution.py:51
  89.6 3.4 %all-to-all-start.5 = ((bf16[8,32,256]{2,1,0:T(8,128)(2,1)}), bf16[8,32,256]{2,1,0:T(8,128)(2,1)S(1)}, u32[]{:S(2)}, u32[]{:S(2)}) async-start(bf16[8,32,256]{2,1,0:T(8,128)(2,1)} %inverse_part_1.1), calls=%async_computation.5 | async-start | bytes 262144 | tf_op jit(solution)/shard_map/all_to_all | solution.py:51
  93.0 9.2 %all-to-all-done.5.refs_0_ = bf16[8,32,256]{2,1,0:T(8,128)(2,1)S(1)} async-done(((bf16[8,32,256]{2,1,0:T(8,128)(2,1)}), bf16[8,32,256]{2,1,0:T(8,128)(2,1)S(1)}, u32[]{:S(2)}, u32[]{:S(2)}) %all-to-all-start.5) | async-done | bytes 131104 | tf_op jit(solution)/shard_map/all_to_all | solution.py:51
  104.3 8.1 %all-to-all-start.6 = ((bf16[8,64,256]{2,1,0:T(8,128)(2,1)}), bf16[8,64,256]{2,1,0:T(8,128)(2,1)S(1)}, u32[]{:S(2)}, u32[]{:S(2)}) async-start(bf16[8,64,256]{2,1,0:T(8,128)(2,1)} %get-tuple-element.43), calls=%async_computation.6 | async-start | bytes 524288 | tf_op jit(solution)/shard_map/all_to_all | solution.py:59
  114.4 5.5 %gather_fusion.1 = f32[2048,64]{1,0:T(8,128)S(1)} fusion(f32[64,2048]{0,1:T(8,128)S(1)} %copy.28, s32[2048]{0:T(1024)S(1)} %fusion.14), kind=kCustom, calls=%fused_computation.1 | custom fusion | bytes 1056768 | tf_op jit(solution)/shard_map/jit(_take)/gather | solution.py:364
  122.3 3.4 %all-to-all-start.7 = ((bf16[32,16,256]{2,1,0:T(8,128)(2,1)}), bf16[32,16,256]{2,1,0:T(8,128)(2,1)S(1)}, u32[]{:S(2)}, u32[]{:S(2)}) async-start(bf16[32,16,256]{2,1,0:T(8,128)(2,1)} %next_state_1.1), calls=%async_computation.7 | async-start | bytes 524288 | tf_op jit(solution)/shard_map/all_to_all | solution.py:51
  125.9 14.7 %all-to-all-done.7.got = bf16[32,16,256]{2,1,0:T(8,128)(2,1)S(1)} async-done(((bf16[32,16,256]{2,1,0:T(8,128)(2,1)}), bf16[32,16,256]{2,1,0:T(8,128)(2,1)S(1)}, u32[]{:S(2)}, u32[]{:S(2)}) %all-to-all-start.7) | async-done | bytes 262176 | tf_op jit(solution)/shard_map/all_to_all | solution.py:51
  140.6 4.7 %all-gather.3.cloned.1.call-done = bf16[24576,256]{1,0:T(8,128)(2,1)} async-done(((bf16[768,256]{1,0:T(8,128)(2,1)}), bf16[24576,256]{1,0:T(8,128)(2,1)}) %all-gather.3.cloned.1.call-update) | async-done | bytes 12582928 | tf_op jit(solution)/shard_map/all_gather | solution.py:337
  145.4 3.4 %last_block.1 = (bf16[16,256]{1,0:T(8,128)(2,1)S(1)}, bf16[8,16,256]{2,1,0:T(8,128)(2,1)}) custom-call(s32[32]{0:T(128)S(1)} %tile_places.1.pos.refs_0_, bf16[32,16,256]{2,1,0:T(8,128)(2,1)S(1)} %all-to-all-done.7.got, bf16[16,16]{1,0:T(8,128)(2,1)S(1)} %fusion.13.pick_own, f32[16,256]{1,0:T(8,128)S(1)} %broadcast_bitcast_fusion.outer, ...), custom_call_target="tpu_custom_call" | custom-call | tf_op jit(solution)/shard_map/last_block/pallas_call | solution.py:123
  148.8 5.6 %all-to-all-start.8 = ((bf16[8,16,256]{2,1,0:T(8,128)(2,1)}), bf16[8,16,256]{2,1,0:T(8,128)(2,1)S(1)}, u32[]{:S(2)}, u32[]{:S(2)}) async-start(bf16[8,16,256]{2,1,0:T(8,128)(2,1)} %get-tuple-element.47), calls=%async_computation.8 | async-start | bytes 131072 | tf_op jit(solution)/shard_map/all_to_all | solution.py:59
  156.7 2.6 %all-to-all-done.8.refs_0_ = bf16[8,16,256]{2,1,0:T(8,128)(2,1)S(1)} async-done(((bf16[8,16,256]{2,1,0:T(8,128)(2,1)}), bf16[8,16,256]{2,1,0:T(8,128)(2,1)S(1)}, u32[]{:S(2)}, u32[]{:S(2)}) %all-to-all-start.8) | async-done | bytes 65568 | tf_op jit(solution)/shard_map/all_to_all | solution.py:59
  164.6 4.9 %all-to-all-start.9 = ((bf16[8,16,256]{2,1,0:T(8,128)(2,1)}), bf16[8,16,256]{2,1,0:T(8,128)(2,1)S(1)}, u32[]{:S(2)}, u32[]{:S(2)}) async-start(bf16[8,16,256]{2,1,0:T(8,128)(2,1)} %get-tuple-element.55), calls=%async_computation.9 | async-start | bytes 131072 | tf_op jit(solution)/shard_map/all_to_all | solution.py:59
  169.5 2.7 %fetch_block_0.1 = (bf16[2,256,2048]{2,1,0:T(8,128)(2,1)S(1)}, bf16[32,64,256]{2,1,0:T(8,128)(2,1)S(1)}) custom-call(s32[32]{0:T(128)S(1)} %tile_places.1.pos.refs_0_, bf16[32,768,256]{2,1,0:T(8,128)(2,1)} %bitcast.80), custom_call_target="tpu_custom_call" | custom-call | tf_op jit(solution)/shard_map/fetch_block_0/pallas_call | solution.py:148
  172.6 2.6 %fusion.2 = bf16[64,2048]{1,0:T(8,128)(2,1)S(1)} fusion(bf16[768,2048]{1,0:T(8,128)(2,1)} %bitcast.81, bf16[64,256]{1,0:T(8,128)(2,1)S(1)} %unstack.23, bf16[64,256]{1,0:T(8,128)(2,1)S(1)} %unstack.21, bf16[64,256]{1,0:T(8,128)(2,1)S(1)} %unstack.19), kind=kOutput, calls=%fused_computation.21 | convolution fusion | flops 201621504 | bytes 3506176 | tf_op jit(solution)/shard_map/dot_general | solution.py:439
  179.3 4.8 %all-to-all-start.10 = ((bf16[8,80,256]{2,1,0:T(8,128)(2,1)}), bf16[8,80,256]{2,1,0:T(8,128)(2,1)S(1)}, u32[]{:S(2)}, u32[]{:S(2)}) async-start(bf16[8,80,256]{2,1,0:T(8,128)(2,1)} %pad_maximum_fusion.3), calls=%async_computation.10 | async-start | bytes 655360 | tf_op jit(solution)/shard_map/all_to_all | solution.py:59
  185.3 5.9 %all-to-all-done.10 = bf16[8,80,256]{2,1,0:T(8,128)(2,1)S(1)} async-done(((bf16[8,80,256]{2,1,0:T(8,128)(2,1)}), bf16[8,80,256]{2,1,0:T(8,128)(2,1)S(1)}, u32[]{:S(2)}, u32[]{:S(2)}) %all-to-all-start.10) | async-done | bytes 327712 | tf_op jit(solution)/shard_map/all_to_all | solution.py:59
  193.4 5.4 %all-to-all-start.11 = ((bf16[32,2,256]{2,1,0:T(2,128)(2,1)}), bf16[32,2,256]{2,1,0:T(2,128)(2,1)S(1)}, u32[]{:S(2)}, u32[]{:S(2)}) async-start(bf16[32,2,256]{2,1,0:T(2,128)(2,1)} %reshape.197), calls=%async_computation.11 | async-start | bytes 65536 | tf_op jit(solution)/shard_map/all_to_all | solution.py:55
  (171 shorter events, 62.5 us)
Async XLA Ops:
  7.2 138.2 %all-gather.3.cloned.1.call-start = ((), (), s32[]{:S(2)}) async-start(), calls=%async_computation.12 | async-start | bytes 12976128 | tf_op jit(solution)/shard_map/all_gather | solution.py:337
  13.7 11.2 %all-to-all-start = ((bf16[4,160,256]{2,1,0:T(8,128)(2,1)}), bf16[4,160,256]{2,1,0:T(8,128)(2,1)S(1)}, u32[]{:S(2)}, u32[]{:S(2)}) async-start(bf16[4,160,256]{2,1,0:T(8,128)(2,1)} %pad_maximum_fusion.2), calls=%async_computation | async-start | bytes 655360 | tf_op jit(solution)/shard_map/all_to_all | solution.py:32
  20.4 31.1 %collective-permute-start = (bf16[512,256]{1,0:T(8,128)(2,1)}, bf16[512,256]{1,0:T(8,128)(2,1)}, u32[]{:S(2)}, u32[]{:S(2)}) collective-permute-start(bf16[512,256]{1,0:T(8,128)(2,1)} %bitcast.4.refs_1_), channel_id=1, source_target_pairs={{0,1},{1,0},{2,3},{3,2},{4,5},{5,4},{6,7},{7,6},{8,9},{9,8},{10,11... | collective-permute-start | bytes 786440 | tf_op jit(solution)/shard_map/ppermute | solution.py:36
  21.8 29.6 %collective-permute-start.1 = (bf16[512,256]{1,0:T(8,128)(2,1)}, bf16[512,256]{1,0:T(8,128)(2,1)}, u32[]{:S(2)}, u32[]{:S(2)}) collective-permute-start(bf16[512,256]{1,0:T(8,128)(2,1)} %bitcast.4.refs_1_), channel_id=1, source_target_pairs={{0,2},{1,3},{2,0},{3,1},{4,6},{5,7},{6,4},{7,5},{8,10},{9,11},{10,... | collective-permute-start | bytes 786440 | tf_op jit(solution)/shard_map/ppermute | solution.py:36
  24.2 27.2 %collective-permute-start.2 = (bf16[512,256]{1,0:T(8,128)(2,1)}, bf16[512,256]{1,0:T(8,128)(2,1)}, u32[]{:S(2)}, u32[]{:S(2)}) collective-permute-start(bf16[512,256]{1,0:T(8,128)(2,1)} %bitcast.4.refs_1_), channel_id=1, source_target_pairs={{0,3},{1,2},{2,1},{3,0},{4,7},{5,6},{6,5},{7,4},{8,11},{9,10},{10,... | collective-permute-start | bytes 786440 | tf_op jit(solution)/shard_map/ppermute | solution.py:36
  26.8 15.9 %all-to-all-start.1 = ((bf16[8,16,256]{2,1,0:T(8,128)(2,1)}), bf16[8,16,256]{2,1,0:T(8,128)(2,1)S(1)}, u32[]{:S(2)}, u32[]{:S(2)}) async-start(bf16[8,16,256]{2,1,0:T(8,128)(2,1)} %copy-done.8), calls=%async_computation.1 | async-start | bytes 131072 | tf_op jit(solution)/shard_map/all_to_all | solution.py:51
  43.5 14.1 %all-to-all-start.2 = ((bf16[8,16,256]{2,1,0:T(8,128)(2,1)}), bf16[8,16,256]{2,1,0:T(8,128)(2,1)S(1)}, u32[]{:S(2)}, u32[]{:S(2)}) async-start(bf16[8,16,256]{2,1,0:T(8,128)(2,1)} %copy-done.3), calls=%async_computation.2 | async-start | bytes 131072 | tf_op jit(solution)/shard_map/all_to_all | solution.py:51
  59.7 16.7 %all-to-all-start.3 = ((bf16[8,64,256]{2,1,0:T(8,128)(2,1)}), bf16[8,64,256]{2,1,0:T(8,128)(2,1)}, u32[]{:S(2)}, u32[]{:S(2)}) async-start(bf16[8,64,256]{2,1,0:T(8,128)(2,1)} %copy-done.4), calls=%async_computation.3 | async-start | bytes 524288 | tf_op jit(solution)/shard_map/all_to_all | solution.py:59
  73.0 8.4 %collective-permute-start.5 = (bf16[48,256]{1,0:T(8,128)(2,1)S(1)}, bf16[48,256]{1,0:T(8,128)(2,1)S(1)}, u32[]{:S(2)}, u32[]{:S(2)}) collective-permute-start(bf16[48,256]{1,0:T(8,128)(2,1)S(1)} %bitcast.94), channel_id=1, source_target_pairs={{0,3},{1,2},{2,1},{3,0},{4,7},{5,6},{6,5},{7,4},{8,11},{9,10},{10,... | collective-permute-start | bytes 73736 | tf_op jit(solution)/shard_map/ppermute | solution.py:36
  74.7 6.7 %collective-permute-start.4 = (bf16[48,256]{1,0:T(8,128)(2,1)S(1)}, bf16[48,256]{1,0:T(8,128)(2,1)S(1)}, u32[]{:S(2)}, u32[]{:S(2)}) collective-permute-start(bf16[48,256]{1,0:T(8,128)(2,1)S(1)} %bitcast.95), channel_id=1, source_target_pairs={{0,2},{1,3},{2,0},{3,1},{4,6},{5,7},{6,4},{7,5},{8,10},{9,11},{10,... | collective-permute-start | bytes 73736 | tf_op jit(solution)/shard_map/ppermute | solution.py:36
  75.4 6.1 %collective-permute-start.3 = (bf16[48,256]{1,0:T(8,128)(2,1)S(1)}, bf16[48,256]{1,0:T(8,128)(2,1)S(1)}, u32[]{:S(2)}, u32[]{:S(2)}) collective-permute-start(bf16[48,256]{1,0:T(8,128)(2,1)S(1)} %bitcast.96), channel_id=1, source_target_pairs={{0,1},{1,0},{2,3},{3,2},{4,5},{5,4},{6,7},{7,6},{8,9},{9,8},{10,11... | collective-permute-start | bytes 73736 | tf_op jit(solution)/shard_map/ppermute | solution.py:36
  78.1 10.7 %all-to-all-start.4 = ((bf16[8,16,256]{2,1,0:T(8,128)(2,1)}), bf16[8,16,256]{2,1,0:T(8,128)(2,1)S(1)}, u32[]{:S(2)}, u32[]{:S(2)}) async-start(bf16[8,16,256]{2,1,0:T(8,128)(2,1)} %get-tuple-element.41), calls=%async_computation.4 | async-start | bytes 131072 | tf_op jit(solution)/shard_map/all_to_all | solution.py:51
  89.6 12.6 %all-to-all-start.5 = ((bf16[8,32,256]{2,1,0:T(8,128)(2,1)}), bf16[8,32,256]{2,1,0:T(8,128)(2,1)S(1)}, u32[]{:S(2)}, u32[]{:S(2)}) async-start(bf16[8,32,256]{2,1,0:T(8,128)(2,1)} %inverse_part_1.1), calls=%async_computation.5 | async-start | bytes 262144 | tf_op jit(solution)/shard_map/all_to_all | solution.py:51
  104.3 16.6 %all-to-all-start.6 = ((bf16[8,64,256]{2,1,0:T(8,128)(2,1)}), bf16[8,64,256]{2,1,0:T(8,128)(2,1)S(1)}, u32[]{:S(2)}, u32[]{:S(2)}) async-start(bf16[8,64,256]{2,1,0:T(8,128)(2,1)} %get-tuple-element.43), calls=%async_computation.6 | async-start | bytes 524288 | tf_op jit(solution)/shard_map/all_to_all | solution.py:59
  122.3 18.4 %all-to-all-start.7 = ((bf16[32,16,256]{2,1,0:T(8,128)(2,1)}), bf16[32,16,256]{2,1,0:T(8,128)(2,1)S(1)}, u32[]{:S(2)}, u32[]{:S(2)}) async-start(bf16[32,16,256]{2,1,0:T(8,128)(2,1)} %next_state_1.1), calls=%async_computation.7 | async-start | bytes 524288 | tf_op jit(solution)/shard_map/all_to_all | solution.py:51
  148.8 10.4 %all-to-all-start.8 = ((bf16[8,16,256]{2,1,0:T(8,128)(2,1)}), bf16[8,16,256]{2,1,0:T(8,128)(2,1)S(1)}, u32[]{:S(2)}, u32[]{:S(2)}) async-start(bf16[8,16,256]{2,1,0:T(8,128)(2,1)} %get-tuple-element.47), calls=%async_computation.8 | async-start | bytes 131072 | tf_op jit(solution)/shard_map/all_to_all | solution.py:59
  161.1 11.0 %collective-permute-start.8 = (bf16[48,256]{1,0:T(8,128)(2,1)S(1)}, bf16[48,256]{1,0:T(8,128)(2,1)S(1)}, u32[]{:S(2)}, u32[]{:S(2)}) collective-permute-start(bf16[48,256]{1,0:T(8,128)(2,1)S(1)} %pad_maximum_fusion.8), channel_id=1, source_target_pairs={{0,3},{1,2},{2,1},{3,0},{4,7},{5,6},{6,5},{7,4},{8,11},{9,10},{10,... | collective-permute-start | bytes 73736 | tf_op jit(solution)/shard_map/ppermute | solution.py:36
  161.7 10.4 %collective-permute-start.7 = (bf16[48,256]{1,0:T(8,128)(2,1)S(1)}, bf16[48,256]{1,0:T(8,128)(2,1)S(1)}, u32[]{:S(2)}, u32[]{:S(2)}) collective-permute-start(bf16[48,256]{1,0:T(8,128)(2,1)S(1)} %pad_maximum_fusion.8), channel_id=1, source_target_pairs={{0,2},{1,3},{2,0},{3,1},{4,6},{5,7},{6,4},{7,5},{8,10},{9,11},{10,... | collective-permute-start | bytes 73736 | tf_op jit(solution)/shard_map/ppermute | solution.py:36
  162.9 9.3 %collective-permute-start.6 = (bf16[48,256]{1,0:T(8,128)(2,1)S(1)}, bf16[48,256]{1,0:T(8,128)(2,1)S(1)}, u32[]{:S(2)}, u32[]{:S(2)}) collective-permute-start(bf16[48,256]{1,0:T(8,128)(2,1)S(1)} %pad_maximum_fusion.8), channel_id=1, source_target_pairs={{0,1},{1,0},{2,3},{3,2},{4,5},{5,4},{6,7},{7,6},{8,9},{9,8},{10,11... | collective-permute-start | bytes 73736 | tf_op jit(solution)/shard_map/ppermute | solution.py:36
  164.6 12.4 %all-to-all-start.9 = ((bf16[8,16,256]{2,1,0:T(8,128)(2,1)}), bf16[8,16,256]{2,1,0:T(8,128)(2,1)S(1)}, u32[]{:S(2)}, u32[]{:S(2)}) async-start(bf16[8,16,256]{2,1,0:T(8,128)(2,1)} %get-tuple-element.55), calls=%async_computation.9 | async-start | bytes 131072 | tf_op jit(solution)/shard_map/all_to_all | solution.py:59
  179.3 11.9 %all-to-all-start.10 = ((bf16[8,80,256]{2,1,0:T(8,128)(2,1)}), bf16[8,80,256]{2,1,0:T(8,128)(2,1)S(1)}, u32[]{:S(2)}, u32[]{:S(2)}) async-start(bf16[8,80,256]{2,1,0:T(8,128)(2,1)} %pad_maximum_fusion.3), calls=%async_computation.10 | async-start | bytes 655360 | tf_op jit(solution)/shard_map/all_to_all | solution.py:59
  192.1 6.7 %collective-permute-start.9 = (bf16[64,256]{1,0:T(8,128)(2,1)S(1)}, bf16[64,256]{1,0:T(8,128)(2,1)S(1)}, u32[]{:S(2)}, u32[]{:S(2)}) collective-permute-start(bf16[64,256]{1,0:T(8,128)(2,1)S(1)} %slice_reduce_fusion), channel_id=1, source_target_pairs={{0,32},{32,0},{64,96},{96,64},{128,160},{160,128},{192,224},{224,1... | collective-permute-start | bytes 98312 | tf_op jit(solution)/shard_map/ppermute | solution.py:40
  193.4 14.1 %all-to-all-start.11 = ((bf16[32,2,256]{2,1,0:T(2,128)(2,1)}), bf16[32,2,256]{2,1,0:T(2,128)(2,1)S(1)}, u32[]{:S(2)}, u32[]{:S(2)}) async-start(bf16[32,2,256]{2,1,0:T(2,128)(2,1)} %reshape.197), calls=%async_computation.11 | async-start | bytes 65536 | tf_op jit(solution)/shard_map/all_to_all | solution.py:55
  199.2 5.2 %collective-permute-start.11 = (bf16[2,64,256]{2,1,0:T(8,128)(2,1)S(1)}, bf16[2,64,256]{2,1,0:T(8,128)(2,1)S(1)}, u32[]{:S(2)}, u32[]{:S(2)}) collective-permute-start(bf16[2,64,256]{2,1,0:T(8,128)(2,1)S(1)} %pad_maximum_fusion.7), channel_id=1, source_target_pairs={{0,128},{32,160},{64,192},{96,224},{128,0},{160,32},{192,64},{224,... | collective-permute-start | bytes 196616 | tf_op jit(solution)/shard_map/ppermute | solution.py:40
  (21 other events, 289.3 us)
Sparse Core Ops, SparseCore 0:
  11.8 133.4 all-gather.2

commit v6 on v5

--- a/solution.py
+++ b/solution.py
@@ -156,12 +156,6 @@
     )(*args)
 
 
-def pack_kernel(lower_inverse, upper_inverse, lower, out):
-    out[pl.ds(0, UPPER_AT), :] = lower_inverse[...].reshape(UPPER_AT, TILE)
-    out[pl.ds(UPPER_AT, PIECE), :] = upper_inverse[0]
-    out[pl.ds(LOWER_AT, PACK - LOWER_AT), :] = lower[...].reshape(PACK - LOWER_AT, TILE)
-
-
 def pos_kernel(tile_of, pos):
     stride = tile_of.shape[0] // NC
 
@@ -321,19 +315,14 @@
     my_block = my_tile // PER
     my_place = my_tile % PER
 
-    pack = pl.pallas_call(
-        pack_kernel,
-        out_shape=jax.ShapeDtypeStruct((PACK, TILE), BF),
-        grid=(1,),
-        in_specs=[
-            pl.BlockSpec((STEPS, PIECE, TILE), lambda at: (0, 0, 0)),
-            pl.BlockSpec((1, PIECE, TILE), lambda at: (STEPS - 1, 0, 0)),
-            pl.BlockSpec((STEPS - 1, TILE, TILE), lambda at: (0, 0, 0)),
+    pack = jnp.concatenate(
+        [
+            jnp.swapaxes(lower_inv, 1, 2).reshape(UPPER_AT, TILE),
+            upper_inv[STEPS - 1],
+            lower_rows[: STEPS - 1, :, :TILE].reshape(PACK - LOWER_AT, TILE),
         ],
-        out_specs=pl.BlockSpec((PACK, TILE), lambda at: (0, 0)),
-        compiler_params=pltpu.CompilerParams(vmem_limit_bytes=8 << 20),
-        name="pack_window",
-    )(jnp.swapaxes(lower_inv, 1, 2), upper_inv, lower_rows)
+        axis=0,
+    )
     pack_all = lax.all_gather(pack, "pcol", axis=0)
 
     local_pivots = pivots - col * width
@@ -426,14 +415,15 @@
 
     message, pos_now = lax.optimization_barrier((message, pos))
     weights = fetch_call(1, pos_now, pack_all)
+    stacked = jnp.concatenate(finished, axis=0)
+    pair = jnp.stack([stacked, pass_y(stacked, 1)])
     back = swap_prow(message)
     last, message = lower_call(1, back, bases[1], weights, [])
-
-    message, stacked, pos_now = lax.optimization_barrier(
-        (message, jnp.concatenate(finished, axis=0), pos)
-    )
+    message, pair, pos_now = lax.optimization_barrier((message, pair, pos))
     weights = fetch_call(0, pos_now, pack_all)
-    every = [stacked] + [pass_y(stacked, step) for step in range(1, NY)]
+
+    other = pass_y(pair, 2)
+    every = [pair[0], pair[1], other[0], other[1]]
     every = by_place(every, y, NY).reshape(NY, STEPS, NZ, rows_own, TILE)
     every = every.transpose(1, 2, 0, 3, 4).reshape(STEPS, count, TILE)
     bulk = jnp.dot(

time: 217 us -> 216 us (level)
  waiting for transfers between devices: 54.3 us -> 65.9 us
  local copies, waits for them, and re-layouts: 24.9 us -> 14.8 us
  starting transfers between devices: 83.6 us -> 81.4 us
    unnamed x50 -> x29, local copies, waits for them, and re-layouts: 6.49 us -> 0.24 us
    all_to_all x1, waiting for transfers between devices: 0.01 us -> 5.84 us  [swap_y(): lax.all_to_all(x, 'pcol', 0, 0, axis_index_groups=Y_GROUPS, tiled=True)]
    all_to_all x5, waiting for transfers between devices: 37.5 us -> 41.7 us  [swap_z(): lax.all_to_all(x, 'pcol', 0, 0, axis_index_groups=Z_GROUPS, tiled=True)]
    all_to_all x5, waiting for transfers between devices: 8.51 us -> 11.5 us  [swap_prow(): return lax.all_to_all(x, 'prow', 0, 0, tiled=True)]
    ppermute x9 -> x8, starting transfers between devices: 10.5 us -> 10 us  [pass_y(): return lax.ppermute(x, 'pcol', [(at, at ^ step) for at in range(NC)])]
  transfers between devices with their start and end apart: 26 -> 25, of which waited for: 11 -> 13; matrix products, arithmetic and copies ran while one was open for 14% -> 11% of each run, Pallas kernels for 7% -> 6%
where the time goes in v6:
time: 216 us; the launch traced here: 214 us
  starting transfers between devices  81.4 us (38%)
  waiting for transfers between devices  65.9 us (31%)
  Pallas kernels  20.5 us (9%)
  between operations  17.5 us (8%)
  local copies, waits for them, and re-layouts  14.8 us (7%)
  other arithmetic  7.99 us (4%)
  matrix products  6.11 us (3%)
    all_to_all x5, waiting for transfers between devices, swap_z(): lax.all_to_all(x, 'pcol', 0, 0, axis_index_groups=Z_GROUPS, tiled=True)  41.7 us
    all_to_all x5, starting transfers between devices, swap_prow(): return lax.all_to_all(x, 'prow', 0, 0, tiled=True)  32.8 us
    all_to_all x5, starting transfers between devices, swap_z(): lax.all_to_all(x, 'pcol', 0, 0, axis_index_groups=Z_GROUPS, tiled=True)  23.1 us
    pallas_call x12, Pallas kernels, call(): pl.pallas_call(kernel, out_shape=tuple((jax.ShapeDtypeStruct(shape, dtype...  17 us
    all_to_all x5, waiting for transfers between devices, swap_prow(): return lax.all_to_all(x, 'prow', 0, 0, tiled=True)  11.5 us
    ppermute x8, starting transfers between devices, pass_y(): return lax.ppermute(x, 'pcol', [(at, at ^ step) for at in range(NC)])  10 us
    gather x2, local copies, waits for them, and re-layouts, body(): state0 = jnp.take(rhs_now, local_pivots, axis=1)  6.58 us
    all_to_all x1, starting transfers between devices, swap_pcol(): return lax.all_to_all(x, 'pcol', 0, 0, tiled=True)  6.34 us
  transfers between devices with their start and end apart: 25, of which 13 were waited for; matrix products, arithmetic and copies ran while one was open for 11% of the time, Pallas kernels for 6%

profile of v6, /device:TPU:1, one launch (start us, length us, event | category | flops | bytes accessed | tf_op | source)
XLA Modules:
  0.0 214.2 jit_solution(3634130313033820055)
XLA Ops:
  20.0 3.9 %all-to-all-start = ((bf16[4,160,256]{2,1,0:T(8,128)(2,1)}), bf16[4,160,256]{2,1,0:T(8,128)(2,1)S(1)}, u32[]{:S(2)}, u32[]{:S(2)}) async-start(bf16[4,160,256]{2,1,0:T(8,128)(2,1)} %pad_maximum_fusion.3), calls=%async_computation | async-start | bytes 655360 | tf_op jit(solution)/shard_map/all_to_all | solution.py:32
  27.5 5.8 %all-to-all-done.got.refs_1_ = bf16[4,160,256]{2,1,0:T(8,128)(2,1)S(1)} async-done(((bf16[4,160,256]{2,1,0:T(8,128)(2,1)}), bf16[4,160,256]{2,1,0:T(8,128)(2,1)S(1)}, u32[]{:S(2)}, u32[]{:S(2)}) %all-to-all-start) | async-done | bytes 327712 | tf_op jit(solution)/shard_map/all_to_all | solution.py:32
  34.6 9.6 %all-to-all-start.1 = ((bf16[8,16,256]{2,1,0:T(8,128)(2,1)}), bf16[8,16,256]{2,1,0:T(8,128)(2,1)S(1)}, u32[]{:S(2)}, u32[]{:S(2)}) async-start(bf16[8,16,256]{2,1,0:T(8,128)(2,1)} %get-tuple-element.37), calls=%async_computation.1 | async-start | bytes 131072 | tf_op jit(solution)/shard_map/all_to_all | solution.py:51
  44.3 7.7 %all-to-all-done.1.refs_0_ = bf16[8,16,256]{2,1,0:T(8,128)(2,1)S(1)} async-done(((bf16[8,16,256]{2,1,0:T(8,128)(2,1)}), bf16[8,16,256]{2,1,0:T(8,128)(2,1)S(1)}, u32[]{:S(2)}, u32[]{:S(2)}) %all-to-all-start.1) | async-done | bytes 65568 | tf_op jit(solution)/shard_map/all_to_all | solution.py:51
  52.8 3.4 %all-to-all-start.2 = ((bf16[8,16,256]{2,1,0:T(8,128)(2,1)}), bf16[8,16,256]{2,1,0:T(8,128)(2,1)S(1)}, u32[]{:S(2)}, u32[]{:S(2)}) async-start(bf16[8,16,256]{2,1,0:T(8,128)(2,1)} %inverse_part_0.1), calls=%async_computation.2 | async-start | bytes 131072 | tf_op jit(solution)/shard_map/all_to_all | solution.py:51
  59.3 4.1 %all-to-all-done.2.refs_0_ = bf16[8,16,256]{2,1,0:T(8,128)(2,1)S(1)} async-done(((bf16[8,16,256]{2,1,0:T(8,128)(2,1)}), bf16[8,16,256]{2,1,0:T(8,128)(2,1)S(1)}, u32[]{:S(2)}, u32[]{:S(2)}) %all-to-all-start.2) | async-done | bytes 65568 | tf_op jit(solution)/shard_map/all_to_all | solution.py:51
  64.3 11.3 %all-to-all-start.3 = ((bf16[8,64,256]{2,1,0:T(8,128)(2,1)}), bf16[8,64,256]{2,1,0:T(8,128)(2,1)S(1)}, u32[]{:S(2)}, u32[]{:S(2)}) async-start(bf16[8,64,256]{2,1,0:T(8,128)(2,1)} %get-tuple-element.38), calls=%async_computation.3 | async-start | bytes 524288 | tf_op jit(solution)/shard_map/all_to_all | solution.py:59
  76.1 3.1 %collective-permute-start.3 = (bf16[48,256]{1,0:T(8,128)(2,1)S(1)}, bf16[48,256]{1,0:T(8,128)(2,1)S(1)}, u32[]{:S(2)}, u32[]{:S(2)}) collective-permute-start(bf16[48,256]{1,0:T(8,128)(2,1)S(1)} %bitcast.102), channel_id=1, source_target_pairs={{0,1},{1,0},{2,3},{3,2},{4,5},{5,4},{6,7},{7,6},{8,9},{9,8},{10,11... | collective-permute-start | bytes 73736 | tf_op jit(solution)/shard_map/ppermute | solution.py:36
  79.2 3.0 %all-to-all-done.3.refs_1_ = bf16[8,64,256]{2,1,0:T(8,128)(2,1)S(1)} async-done(((bf16[8,64,256]{2,1,0:T(8,128)(2,1)}), bf16[8,64,256]{2,1,0:T(8,128)(2,1)S(1)}, u32[]{:S(2)}, u32[]{:S(2)}) %all-to-all-start.3) | async-done | bytes 262176 | tf_op jit(solution)/shard_map/all_to_all | solution.py:59
  83.5 3.4 %all-to-all-start.4 = ((bf16[8,16,256]{2,1,0:T(8,128)(2,1)}), bf16[8,16,256]{2,1,0:T(8,128)(2,1)S(1)}, u32[]{:S(2)}, u32[]{:S(2)}) async-start(bf16[8,16,256]{2,1,0:T(8,128)(2,1)} %get-tuple-element.41), calls=%async_computation.4 | async-start | bytes 131072 | tf_op jit(solution)/shard_map/all_to_all | solution.py:51
  86.9 7.5 %all-to-all-done.4.refs_0_ = bf16[8,16,256]{2,1,0:T(8,128)(2,1)S(1)} async-done(((bf16[8,16,256]{2,1,0:T(8,128)(2,1)}), bf16[8,16,256]{2,1,0:T(8,128)(2,1)S(1)}, u32[]{:S(2)}, u32[]{:S(2)}) %all-to-all-start.4) | async-done | bytes 65568 | tf_op jit(solution)/shard_map/all_to_all | solution.py:51
  95.3 3.4 %all-to-all-start.5 = ((bf16[8,32,256]{2,1,0:T(8,128)(2,1)}), bf16[8,32,256]{2,1,0:T(8,128)(2,1)S(1)}, u32[]{:S(2)}, u32[]{:S(2)}) async-start(bf16[8,32,256]{2,1,0:T(8,128)(2,1)} %inverse_part_1.1), calls=%async_computation.5 | async-start | bytes 262144 | tf_op jit(solution)/shard_map/all_to_all | solution.py:51
  100.2 7.8 %all-to-all-done.5.refs_0_ = bf16[8,32,256]{2,1,0:T(8,128)(2,1)S(1)} async-done(((bf16[8,32,256]{2,1,0:T(8,128)(2,1)}), bf16[8,32,256]{2,1,0:T(8,128)(2,1)S(1)}, u32[]{:S(2)}, u32[]{:S(2)}) %all-to-all-start.5) | async-done | bytes 131104 | tf_op jit(solution)/shard_map/all_to_all | solution.py:51
  108.9 6.5 %all-to-all-start.6 = ((bf16[8,64,256]{2,1,0:T(8,128)(2,1)}), bf16[8,64,256]{2,1,0:T(8,128)(2,1)S(1)}, u32[]{:S(2)}, u32[]{:S(2)}) async-start(bf16[8,64,256]{2,1,0:T(8,128)(2,1)} %get-tuple-element.43), calls=%async_computation.6 | async-start | bytes 524288 | tf_op jit(solution)/shard_map/all_to_all | solution.py:59
  115.8 5.5 %gather_fusion.1 = f32[2048,64]{1,0:T(8,128)S(1)} fusion(f32[64,2048]{0,1:T(8,128)S(1)} %copy.28, s32[2048]{0:T(1024)S(1)} %fusion.14), kind=kCustom, calls=%fused_computation.1 | custom fusion | bytes 1056768 | tf_op jit(solution)/shard_map/jit(_take)/gather | solution.py:353
  123.7 3.4 %all-to-all-start.7 = ((bf16[32,16,256]{2,1,0:T(8,128)(2,1)}), bf16[32,16,256]{2,1,0:T(8,128)(2,1)S(1)}, u32[]{:S(2)}, u32[]{:S(2)}) async-start(bf16[32,16,256]{2,1,0:T(8,128)(2,1)} %next_state_1.1), calls=%async_computation.7 | async-start | bytes 524288 | tf_op jit(solution)/shard_map/all_to_all | solution.py:51
  127.4 14.4 %all-to-all-done.7.got = bf16[32,16,256]{2,1,0:T(8,128)(2,1)S(1)} async-done(((bf16[32,16,256]{2,1,0:T(8,128)(2,1)}), bf16[32,16,256]{2,1,0:T(8,128)(2,1)S(1)}, u32[]{:S(2)}, u32[]{:S(2)}) %all-to-all-start.7) | async-done | bytes 262176 | tf_op jit(solution)/shard_map/all_to_all | solution.py:51
  141.8 3.4 %all-gather.3.cloned.1.call-done = bf16[24576,256]{1,0:T(8,128)(2,1)} async-done(((bf16[768,256]{1,0:T(8,128)(2,1)}), bf16[24576,256]{1,0:T(8,128)(2,1)}) %all-gather.3.cloned.1.call-update) | async-done | bytes 12582928 | tf_op jit(solution)/shard_map/all_gather | solution.py:326
  145.2 3.4 %last_block.1 = (bf16[16,256]{1,0:T(8,128)(2,1)S(1)}, bf16[8,16,256]{2,1,0:T(8,128)(2,1)}) custom-call(s32[32]{0:T(128)S(1)} %tile_places.1.pos.refs_0_, bf16[32,16,256]{2,1,0:T(8,128)(2,1)S(1)} %all-to-all-done.7.got, bf16[16,16]{1,0:T(8,128)(2,1)S(1)} %fusion.13.pick_own, f32[16,256]{1,0:T(8,128)S(1)} %broadcast_bitcast_fusion.outer, ...), custom_call_target="tpu_custom_call" | custom-call | tf_op jit(solution)/shard_map/last_block/pallas_call | solution.py:123
  148.9 5.6 %all-to-all-start.8 = ((bf16[8,16,256]{2,1,0:T(8,128)(2,1)}), bf16[8,16,256]{2,1,0:T(8,128)(2,1)S(1)}, u32[]{:S(2)}, u32[]{:S(2)}) async-start(bf16[8,16,256]{2,1,0:T(8,128)(2,1)} %get-tuple-element.47), calls=%async_computation.8 | async-start | bytes 131072 | tf_op jit(solution)/shard_map/all_to_all | solution.py:59
  163.1 4.3 %all-to-all-start.9 = ((bf16[8,16,256]{2,1,0:T(8,128)(2,1)}), bf16[8,16,256]{2,1,0:T(8,128)(2,1)S(1)}, u32[]{:S(2)}, u32[]{:S(2)}) async-start(bf16[8,16,256]{2,1,0:T(8,128)(2,1)} %get-tuple-element.55), calls=%async_computation.9 | async-start | bytes 131072 | tf_op jit(solution)/shard_map/all_to_all | solution.py:59
  177.2 5.0 %all-to-all-start.10 = ((bf16[8,80,256]{2,1,0:T(8,128)(2,1)}), bf16[8,80,256]{2,1,0:T(8,128)(2,1)S(1)}, u32[]{:S(2)}, u32[]{:S(2)}) async-start(bf16[8,80,256]{2,1,0:T(8,128)(2,1)} %pad_maximum_fusion.4), calls=%async_computation.10 | async-start | bytes 655360 | tf_op jit(solution)/shard_map/all_to_all | solution.py:59
  183.4 5.9 %all-to-all-done.10 = bf16[8,80,256]{2,1,0:T(8,128)(2,1)S(1)} async-done(((bf16[8,80,256]{2,1,0:T(8,128)(2,1)}), bf16[8,80,256]{2,1,0:T(8,128)(2,1)S(1)}, u32[]{:S(2)}, u32[]{:S(2)}) %all-to-all-start.10) | async-done | bytes 327712 | tf_op jit(solution)/shard_map/all_to_all | solution.py:59
  191.4 6.3 %all-to-all-start.11 = ((bf16[32,2,256]{2,1,0:T(2,128)(2,1)}), bf16[32,2,256]{2,1,0:T(2,128)(2,1)S(1)}, u32[]{:S(2)}, u32[]{:S(2)}) async-start(bf16[32,2,256]{2,1,0:T(2,128)(2,1)} %reshape.205), calls=%async_computation.11 | async-start | bytes 65536 | tf_op jit(solution)/shard_map/all_to_all | solution.py:55
  (150 shorter events, 58.7 us)
Async XLA Ops:
  7.2 138.0 %all-gather.3.cloned.1.call-start = ((), (), s32[]{:S(2)}) async-start(), calls=%async_computation.12 | async-start | bytes 12976128 | tf_op jit(solution)/shard_map/all_gather | solution.py:326
  11.7 47.6 %collective-permute-start = (bf16[512,256]{1,0:T(8,128)(2,1)S(1)}, bf16[512,256]{1,0:T(8,128)(2,1)S(1)}, u32[]{:S(2)}, u32[]{:S(2)}) collective-permute-start(bf16[512,256]{1,0:T(8,128)(2,1)S(1)} %bitcast.79), channel_id=1, source_target_pairs={{0,1},{1,0},{2,3},{3,2},{4,5},{5,4},{6,7},{7,6},{8,9},{9,8},{10,11... | collective-permute-start | bytes 786440 | tf_op jit(solution)/shard_map/ppermute | solution.py:36
  13.9 45.4 %collective-permute-start.1 = (bf16[512,256]{1,0:T(8,128)(2,1)S(1)}, bf16[512,256]{1,0:T(8,128)(2,1)S(1)}, u32[]{:S(2)}, u32[]{:S(2)}) collective-permute-start(bf16[512,256]{1,0:T(8,128)(2,1)S(1)} %bitcast.80), channel_id=1, source_target_pairs={{0,2},{1,3},{2,0},{3,1},{4,6},{5,7},{6,4},{7,5},{8,10},{9,11},{10,... | collective-permute-start | bytes 786440 | tf_op jit(solution)/shard_map/ppermute | solution.py:36
  16.5 42.8 %collective-permute-start.2 = (bf16[512,256]{1,0:T(8,128)(2,1)S(1)}, bf16[512,256]{1,0:T(8,128)(2,1)S(1)}, u32[]{:S(2)}, u32[]{:S(2)}) collective-permute-start(bf16[512,256]{1,0:T(8,128)(2,1)S(1)} %bitcast.81), channel_id=1, source_target_pairs={{0,3},{1,2},{2,1},{3,0},{4,7},{5,6},{6,5},{7,4},{8,11},{9,10},{10,... | collective-permute-start | bytes 786440 | tf_op jit(solution)/shard_map/ppermute | solution.py:36
  20.0 13.4 %all-to-all-start = ((bf16[4,160,256]{2,1,0:T(8,128)(2,1)}), bf16[4,160,256]{2,1,0:T(8,128)(2,1)S(1)}, u32[]{:S(2)}, u32[]{:S(2)}) async-start(bf16[4,160,256]{2,1,0:T(8,128)(2,1)} %pad_maximum_fusion.3), calls=%async_computation | async-start | bytes 655360 | tf_op jit(solution)/shard_map/all_to_all | solution.py:32
  34.6 17.4 %all-to-all-start.1 = ((bf16[8,16,256]{2,1,0:T(8,128)(2,1)}), bf16[8,16,256]{2,1,0:T(8,128)(2,1)S(1)}, u32[]{:S(2)}, u32[]{:S(2)}) async-start(bf16[8,16,256]{2,1,0:T(8,128)(2,1)} %get-tuple-element.37), calls=%async_computation.1 | async-start | bytes 131072 | tf_op jit(solution)/shard_map/all_to_all | solution.py:51
  52.8 10.6 %all-to-all-start.2 = ((bf16[8,16,256]{2,1,0:T(8,128)(2,1)}), bf16[8,16,256]{2,1,0:T(8,128)(2,1)S(1)}, u32[]{:S(2)}, u32[]{:S(2)}) async-start(bf16[8,16,256]{2,1,0:T(8,128)(2,1)} %inverse_part_0.1), calls=%async_computation.2 | async-start | bytes 131072 | tf_op jit(solution)/shard_map/all_to_all | solution.py:51
  64.3 17.8 %all-to-all-start.3 = ((bf16[8,64,256]{2,1,0:T(8,128)(2,1)}), bf16[8,64,256]{2,1,0:T(8,128)(2,1)S(1)}, u32[]{:S(2)}, u32[]{:S(2)}) async-start(bf16[8,64,256]{2,1,0:T(8,128)(2,1)} %get-tuple-element.38), calls=%async_computation.3 | async-start | bytes 524288 | tf_op jit(solution)/shard_map/all_to_all | solution.py:59
  75.9 11.0 %collective-permute-start.5 = (bf16[48,256]{1,0:T(8,128)(2,1)S(1)}, bf16[48,256]{1,0:T(8,128)(2,1)S(1)}, u32[]{:S(2)}, u32[]{:S(2)}) collective-permute-start(bf16[48,256]{1,0:T(8,128)(2,1)S(1)} %bitcast.100), channel_id=1, source_target_pairs={{0,3},{1,2},{2,1},{3,0},{4,7},{5,6},{6,5},{7,4},{8,11},{9,10},{10,... | collective-permute-start | bytes 73736 | tf_op jit(solution)/shard_map/ppermute | solution.py:36
  76.0 10.9 %collective-permute-start.4 = (bf16[48,256]{1,0:T(8,128)(2,1)S(1)}, bf16[48,256]{1,0:T(8,128)(2,1)S(1)}, u32[]{:S(2)}, u32[]{:S(2)}) collective-permute-start(bf16[48,256]{1,0:T(8,128)(2,1)S(1)} %bitcast.101), channel_id=1, source_target_pairs={{0,2},{1,3},{2,0},{3,1},{4,6},{5,7},{6,4},{7,5},{8,10},{9,11},{10,... | collective-permute-start | bytes 73736 | tf_op jit(solution)/shard_map/ppermute | solution.py:36
  76.1 10.8 %collective-permute-start.3 = (bf16[48,256]{1,0:T(8,128)(2,1)S(1)}, bf16[48,256]{1,0:T(8,128)(2,1)S(1)}, u32[]{:S(2)}, u32[]{:S(2)}) collective-permute-start(bf16[48,256]{1,0:T(8,128)(2,1)S(1)} %bitcast.102), channel_id=1, source_target_pairs={{0,1},{1,0},{2,3},{3,2},{4,5},{5,4},{6,7},{7,6},{8,9},{9,8},{10,11... | collective-permute-start | bytes 73736 | tf_op jit(solution)/shard_map/ppermute | solution.py:36
  83.5 11.0 %all-to-all-start.4 = ((bf16[8,16,256]{2,1,0:T(8,128)(2,1)}), bf16[8,16,256]{2,1,0:T(8,128)(2,1)S(1)}, u32[]{:S(2)}, u32[]{:S(2)}) async-start(bf16[8,16,256]{2,1,0:T(8,128)(2,1)} %get-tuple-element.41), calls=%async_computation.4 | async-start | bytes 131072 | tf_op jit(solution)/shard_map/all_to_all | solution.py:51
  95.3 12.8 %all-to-all-start.5 = ((bf16[8,32,256]{2,1,0:T(8,128)(2,1)}), bf16[8,32,256]{2,1,0:T(8,128)(2,1)S(1)}, u32[]{:S(2)}, u32[]{:S(2)}) async-start(bf16[8,32,256]{2,1,0:T(8,128)(2,1)} %inverse_part_1.1), calls=%async_computation.5 | async-start | bytes 262144 | tf_op jit(solution)/shard_map/all_to_all | solution.py:51
  108.9 13.5 %all-to-all-start.6 = ((bf16[8,64,256]{2,1,0:T(8,128)(2,1)}), bf16[8,64,256]{2,1,0:T(8,128)(2,1)S(1)}, u32[]{:S(2)}, u32[]{:S(2)}) async-start(bf16[8,64,256]{2,1,0:T(8,128)(2,1)} %get-tuple-element.43), calls=%async_computation.6 | async-start | bytes 524288 | tf_op jit(solution)/shard_map/all_to_all | solution.py:59
  123.7 18.1 %all-to-all-start.7 = ((bf16[32,16,256]{2,1,0:T(8,128)(2,1)}), bf16[32,16,256]{2,1,0:T(8,128)(2,1)S(1)}, u32[]{:S(2)}, u32[]{:S(2)}) async-start(bf16[32,16,256]{2,1,0:T(8,128)(2,1)} %next_state_1.1), calls=%async_computation.7 | async-start | bytes 524288 | tf_op jit(solution)/shard_map/all_to_all | solution.py:51
  148.6 8.2 %collective-permute-start.6 = (bf16[48,256]{1,0:T(8,128)(2,1)S(1)}, bf16[48,256]{1,0:T(8,128)(2,1)S(1)}, u32[]{:S(2)}, u32[]{:S(2)}) collective-permute-start(bf16[48,256]{1,0:T(8,128)(2,1)S(1)} %constant_dynamic-update-slice_fusion), channel_id=1, source_target_pairs={{0,1},{1,0},{2,3},{3,2},{4,5},{5,4},{6,7},{7,6},{8,9},{9,8},{10,11... | collective-permute-start | bytes 73736 | tf_op jit(solution)/shard_map/ppermute | solution.py:36
  148.9 10.5 %all-to-all-start.8 = ((bf16[8,16,256]{2,1,0:T(8,128)(2,1)}), bf16[8,16,256]{2,1,0:T(8,128)(2,1)S(1)}, u32[]{:S(2)}, u32[]{:S(2)}) async-start(bf16[8,16,256]{2,1,0:T(8,128)(2,1)} %get-tuple-element.47), calls=%async_computation.8 | async-start | bytes 131072 | tf_op jit(solution)/shard_map/all_to_all | solution.py:59
  161.3 8.8 %collective-permute-start.7 = (bf16[2,48,256]{2,1,0:T(8,128)(2,1)S(1)}, bf16[2,48,256]{2,1,0:T(8,128)(2,1)S(1)}, u32[]{:S(2)}, u32[]{:S(2)}) collective-permute-start(bf16[2,48,256]{2,1,0:T(8,128)(2,1)S(1)} %pad_maximum_fusion.8), channel_id=1, source_target_pairs={{0,2},{1,3},{2,0},{3,1},{4,6},{5,7},{6,4},{7,5},{8,10},{9,11},{10,... | collective-permute-start | bytes 147464 | tf_op jit(solution)/shard_map/ppermute | solution.py:36
  163.1 11.8 %all-to-all-start.9 = ((bf16[8,16,256]{2,1,0:T(8,128)(2,1)}), bf16[8,16,256]{2,1,0:T(8,128)(2,1)S(1)}, u32[]{:S(2)}, u32[]{:S(2)}) async-start(bf16[8,16,256]{2,1,0:T(8,128)(2,1)} %get-tuple-element.55), calls=%async_computation.9 | async-start | bytes 131072 | tf_op jit(solution)/shard_map/all_to_all | solution.py:59
  177.2 12.1 %all-to-all-start.10 = ((bf16[8,80,256]{2,1,0:T(8,128)(2,1)}), bf16[8,80,256]{2,1,0:T(8,128)(2,1)S(1)}, u32[]{:S(2)}, u32[]{:S(2)}) async-start(bf16[8,80,256]{2,1,0:T(8,128)(2,1)} %pad_maximum_fusion.4), calls=%async_computation.10 | async-start | bytes 655360 | tf_op jit(solution)/shard_map/all_to_all | solution.py:59
  190.2 7.6 %collective-permute-start.8 = (bf16[64,256]{1,0:T(8,128)(2,1)S(1)}, bf16[64,256]{1,0:T(8,128)(2,1)S(1)}, u32[]{:S(2)}, u32[]{:S(2)}) collective-permute-start(bf16[64,256]{1,0:T(8,128)(2,1)S(1)} %slice_reduce_fusion), channel_id=1, source_target_pairs={{0,32},{32,0},{64,96},{96,64},{128,160},{160,128},{192,224},{224,1... | collective-permute-start | bytes 98312 | tf_op jit(solution)/shard_map/ppermute | solution.py:40
  191.4 15.0 %all-to-all-start.11 = ((bf16[32,2,256]{2,1,0:T(2,128)(2,1)}), bf16[32,2,256]{2,1,0:T(2,128)(2,1)S(1)}, u32[]{:S(2)}, u32[]{:S(2)}) async-start(bf16[32,2,256]{2,1,0:T(2,128)(2,1)} %reshape.205), calls=%async_computation.11 | async-start | bytes 65536 | tf_op jit(solution)/shard_map/all_to_all | solution.py:55
  198.2 5.2 %collective-permute-start.10 = (bf16[2,64,256]{2,1,0:T(8,128)(2,1)S(1)}, bf16[2,64,256]{2,1,0:T(8,128)(2,1)S(1)}, u32[]{:S(2)}, u32[]{:S(2)}) collective-permute-start(bf16[2,64,256]{2,1,0:T(8,128)(2,1)S(1)} %pad_maximum_fusion.7), channel_id=1, source_target_pairs={{0,128},{32,160},{64,192},{96,224},{128,0},{160,32},{192,64},{224,... | collective-permute-start | bytes 196616 | tf_op jit(solution)/shard_map/ppermute | solution.py:40
  200.0 4.9 %collective-permute-start.11 = (bf16[2,64,256]{2,1,0:T(8,128)(2,1)S(1)}, bf16[2,64,256]{2,1,0:T(8,128)(2,1)S(1)}, u32[]{:S(2)}, u32[]{:S(2)}) collective-permute-start(bf16[2,64,256]{2,1,0:T(8,128)(2,1)S(1)} %pad_maximum_fusion.7), channel_id=1, source_target_pairs={{0,192},{32,224},{64,128},{96,160},{128,64},{160,96},{192,0},{224,... | collective-permute-start | bytes 196616 | tf_op jit(solution)/shard_map/ppermute | solution.py:40
  (7 other events, 174.6 us)
Sparse Core Ops, SparseCore 0:
  11.2 133.9 all-gather.2

commit v7 on v6

--- a/solution.py
+++ b/solution.py
@@ -18,9 +18,10 @@
 Z_GROUPS = [[z * NY + y for z in range(NZ)] for y in range(NY)]
 BF = jnp.bfloat16
 F32 = jnp.float32
-UPPER_AT = STEPS * PIECE
-LOWER_AT = UPPER_AT + PIECE
+LOWER_AT = (STEPS - 1) * PIECE
 PACK = LOWER_AT + (STEPS - 1) * TILE
+UPPER_FIRST = 32
+LOWER_LAST = UPPER_FIRST + PIECE
 ROWS = 16
 GRANT = 49 << 20
 VMEM = pl.BlockSpec(memory_space=pltpu.VMEM)
@@ -91,57 +92,6 @@
     for place in range(1, PER):
         part = jnp.where(place_mask(place), full[:, place * TILE : (place + 1) * TILE], part)
     return part.astype(BF)
-
-
-def last_kernel(pos, got, pick_own, outer, pack, solved_out, message_out, upper, inverse, sems):
-    copies = [
-        pltpu.make_async_copy(pack.at[:, pl.ds(UPPER_AT, PIECE), :], upper, sems.at[0]),
-        pltpu.make_async_copy(
-            pack.at[:, pl.ds((STEPS - 1) * PIECE, PIECE), :], inverse, sems.at[1]
-        ),
-    ]
-    for copy in copies:
-        copy.start()
-    copies[0].wait()
-    _, y = plane()
-    block = []
-    for place in range(PER):
-        at = pos[(STEPS - 1) * PER + place]
-        block.append(got[at - at % NY + ((at % NY) ^ y)])
-    block = jnp.concatenate(block, axis=1)
-    value = dot_nn(block, upper[...].reshape(NB, TILE)).astype(BF)
-    solved_out[...] = value
-    resid = (dot_nn(pick_own[...], value) - outer[...]).astype(BF)
-    copies[1].wait()
-    part = lower_part(resid, inverse)
-    for index in range(NP):
-        message_out[index] = part
-
-
-def last_call(pos, got, pick_own, outer, pack):
-    vmem = pl.BlockSpec(memory_space=pltpu.VMEM)
-    return pl.pallas_call(
-        last_kernel,
-        out_shape=(
-            jax.ShapeDtypeStruct((ROWS, TILE), BF),
-            jax.ShapeDtypeStruct((NP, ROWS, TILE), BF),
-        ),
-        in_specs=[
-            pl.BlockSpec(memory_space=pltpu.SMEM),
-            vmem,
-            vmem,
-            vmem,
-            pl.BlockSpec(memory_space=pltpu.HBM),
-        ],
-        out_specs=(vmem, vmem),
-        scratch_shapes=[
-            pltpu.VMEM((NC, PIECE, TILE), BF),
-            pltpu.VMEM((NC, PIECE, TILE), BF),
-            pltpu.SemaphoreType.DMA((2,)),
-        ],
-        compiler_params=pltpu.CompilerParams(vmem_limit_bytes=GRANT),
-        name="last_block",
-    )(pos, got, pick_own, outer, pack)
 
 
 def call(kernel, name, outs, in_specs, args, scratch=(), out_specs=None, grant=None):
@@ -175,9 +125,11 @@
     return tile_of[(z * NY + other) * (tile_of.shape[0] // NC)]
 
 
-def first_kernel(tile_of, got, tiles, routed):
+def first_kernel(tile_of, got, inverses, tiles, message):
     z, y = plane()
-    routed[...] = jnp.zeros_like(routed)
+    for index in range(NZ):
+        message[index, pl.ds(0, ROWS), :] = jnp.zeros((ROWS, TILE), BF)
+        message[index, pl.ds(ROWS, (STEPS - 1) * PIECE), :] = inverses[...]
     for step in range(NY):
         other = y ^ step
         value = got[other, pl.ds(0, ROWS), :].astype(F32)
@@ -187,19 +139,26 @@
 
         @pl.when(tile // PER == 0)
         def _():
-            routed[tile % PER] = value.astype(BF)
-
-
-def inverse_kernel(step, back, got, *rest):
-    message = rest[-1]
-    mine = jnp.sum(back[...].astype(F32), axis=0).astype(BF)
-    at = 2 * ROWS + step * PIECE
-    weights = jnp.concatenate([got[other, pl.ds(at, PIECE), :] for other in range(NY)], axis=0)
-    part = dot_nn(mine, weights).astype(BF)
+            message[tile % PER, pl.ds(0, ROWS), :] = value.astype(BF)
+
+
+def stacked_rows(got, at):
+    return jnp.concatenate([got[other, pl.ds(at, PIECE), :] for other in range(NY)], axis=0)
+
+
+def inverse_kernel(tile_of, back, got, message, picked):
+    mine = jnp.sum(back[:, pl.ds(0, ROWS), :].astype(F32), axis=0).astype(BF)
+    part = dot_nn(mine, stacked_rows(got, UPPER_FIRST)).astype(BF)
     for index in range(NZ):
-        message[index, pl.ds(0, ROWS), :] = part
-        if len(rest) > 1:
-            message[index, pl.ds(ROWS, ROWS), :] = rest[0][index]
+        message[index] = part
+    z, _ = plane()
+    for other in range(NY):
+        tile = plane_tile(tile_of, z, other)
+        near = back[tile % PER, pl.ds(ROWS, PIECE), :]
+        far = back[tile % PER, pl.ds(ROWS + PIECE, PIECE), :]
+        one = (tile // PER == 1).astype(BF)
+        two = (tile // PER == 2).astype(BF)
+        picked[other] = near * one + far * two
 
 
 def update_kernel(step, back, own, near_1, near_2, near_3, solved_out, message, *outer):
@@ -214,26 +173,42 @@
             message[other, pl.ds(index * ROWS, ROWS), :] = update
 
 
-def state_kernel(step, tile_of, back, tiles, *outs):
+def state_kernel(step, tile_of, back, tiles, parts, *rest):
     z, y = plane()
     sums = jnp.sum(back[...].astype(F32), axis=0)
-    if step == 0:
-        later, routed = outs
-        routed[...] = jnp.zeros_like(routed)
+    message = rest[-1]
+    part = jnp.zeros((ROWS, TILE), F32)
     for index in range(NY):
-        tile = plane_tile(tile_of, z, y ^ index)
+        other = y ^ index
+        tile = plane_tile(tile_of, z, other)
         keep = (tile // PER > step).astype(F32)
         value = tiles[index] - keep * sums[index * ROWS : (index + 1) * ROWS]
         if step == 0:
-            later[index] = value
-
-            @pl.when(tile // PER == 1)
-            def _():
-                routed[tile % PER] = value.astype(BF)
-
-        else:
-            for other in range(NZ):
-                outs[0][other * NY + index] = value.astype(BF)
+            rest[2][index] = value
+        block = (value * (tile // PER == step + 1).astype(F32)).astype(BF)
+        weights = jnp.concatenate([parts[sub ^ y, other] for sub in range(NY)], axis=0)
+        part = part + dot_nn(block, weights)
+    part = part.astype(BF)
+    for index in range(NZ):
+        message[index, pl.ds(0, ROWS), :] = part
+        if step == 0:
+            message[index, pl.ds(ROWS, ROWS), :] = rest[0][...]
+            message[index, pl.ds(2 * ROWS, ROWS), :] = rest[1][index]
+
+
+def last_kernel(back, outer, got, solved_out, message):
+    value = jnp.sum(back[...].astype(F32), axis=0).astype(BF)
+    solved_out[...] = value
+    resid = (value.astype(F32) - outer[...]).astype(BF)
+    part = dot_nt(resid, stacked_rows(got, LOWER_LAST)).astype(BF)
+    for index in range(NP):
+        message[index] = part
+
+
+def share_kernel(back, message):
+    value = jnp.sum(back[...].astype(F32), axis=0).astype(BF)
+    for index in range(NZ):
+        message[index] = value
 
 
 def fetch_kernel(step, pos, pack, tiles, inverse, sems):
@@ -273,7 +248,14 @@
 def lower_kernel(step, back, base, tiles, inverse, *rest):
     known = rest[:-2]
     value_out, message_out = rest[-2:]
-    value = jnp.sum(back[...].astype(F32), axis=0).astype(BF)
+    if step == STEPS - 2:
+        pick_own = known[0][...]
+        value = jnp.zeros((ROWS, TILE), F32)
+        for place in range(PER):
+            value = jnp.where(place_mask(place), dot_nn(pick_own, back[place]), value)
+        value = value.astype(BF)
+    else:
+        value = jnp.sum(back[...].astype(F32), axis=0).astype(BF)
     value_out[...] = value
     sums = jnp.zeros((ROWS, TILE), F32)
     for at in range(STEPS - 1 - step):
@@ -315,10 +297,10 @@
     my_block = my_tile // PER
     my_place = my_tile % PER
 
+    lower_turned = jnp.swapaxes(lower_inv, 1, 2)
     pack = jnp.concatenate(
         [
-            jnp.swapaxes(lower_inv, 1, 2).reshape(UPPER_AT, TILE),
-            upper_inv[STEPS - 1],
+            lower_turned[: STEPS - 1].reshape(LOWER_AT, TILE),
             lower_rows[: STEPS - 1, :, :TILE].reshape(PACK - LOWER_AT, TILE),
         ],
         axis=0,
@@ -330,54 +312,51 @@
     own = own.reshape(NZ, NY, rows_own, TILE).transpose(1, 0, 2, 3).reshape(NY, rows_z, TILE)
     own_high = own.astype(BF)
     own_low = (own - own_high.astype(F32)).astype(BF)
-    first_inverses = upper_inv[: STEPS - 1].reshape((STEPS - 1) * PIECE, TILE)
-    start = swap_y(jnp.concatenate([own_high, own_low, to_all(first_inverses, NY)], axis=1))
-    tiles, routed = call(
+    both = jnp.concatenate([upper_inv[0], lower_turned[STEPS - 1]], axis=0)
+    start = swap_y(jnp.concatenate([own_high, own_low, to_all(both, NY)], axis=1))
+    tiles, message = call(
         first_kernel,
         "first_state",
-        [((NY, ROWS, TILE), F32), ((NZ, ROWS, TILE), BF)],
-        [SMEM, VMEM],
-        (tile_of, start),
+        [((NY, ROWS, TILE), F32), ((NZ, ROWS + (STEPS - 1) * PIECE, TILE), BF)],
+        [SMEM, VMEM, VMEM],
+        (tile_of, start, upper_inv[1:].reshape((STEPS - 1) * PIECE, TILE)),
     )
     upper_pack = upper_rows[: STEPS - 1, :, :TILE].reshape((STEPS - 1) * TILE, TILE)
     near = [upper_pack] + [pass_y(upper_pack, step) for step in range(1, NY)]
-    routed, solved_now, tile_now = lax.optimization_barrier((routed, solved, tile_of))
+    message, solved_now, tile_now = lax.optimization_barrier((message, solved, tile_of))
     (pos,) = call(
         pos_kernel, "tile_places", [((NC,), jnp.int32)], [SMEM], (tile_now,), out_specs=[SMEM]
     )
+    message, picked = call(
+        inverse_kernel,
+        "inverse_part_0",
+        [((NZ, ROWS, TILE), BF), ((NY, PIECE, TILE), BF)],
+        [SMEM, VMEM, VMEM],
+        (tile_of, swap_z(message), start),
+    )
+    parts = jnp.stack([picked] + [pass_y(picked, step) for step in range(1, NY)])
+
+    slot_known = jnp.where(my_block >= STEPS, solved_now[:, :TILE], 0.0)
+    known = jnp.concatenate([slot_known, solved_now[:, TILE:]], axis=1).astype(BF)
+    outer = lax.dot_general(
+        known, lower_rows, (((1,), (2,)), ((), ())), preferred_element_type=F32
+    )
+    outer = outer.astype(BF).reshape(NZ, NY, rows_own, STEPS, TILE)
+    outer = outer.transpose(1, 0, 2, 3, 4).reshape(NY, NZ * rows_own * STEPS, TILE)
+    outer_sum = lax.dynamic_index_in_dim(outer, y, 0, False).astype(F32)
+    for other in range(1, NY):
+        theirs = lax.dynamic_index_in_dim(outer, y ^ other, 0, False)
+        outer_sum = outer_sum + pass_y(theirs, other).astype(F32)
+    outer = outer_sum.astype(BF).reshape(NZ, rows_own, STEPS, TILE)
+    outer_last = outer[:, :, STEPS - 1].reshape(ROWS, TILE)
+    outer_rest = outer[:, :, : STEPS - 1].reshape(NZ, rows_own * (STEPS - 1), TILE)
+    outer_rest = jnp.pad(outer_rest, ((0, 0), (0, ROWS - rows_own * (STEPS - 1)), (0, 0)))
 
     finished = []
     for step in range(STEPS - 1):
-        if step == 1:
-            routed, rhs_now = lax.optimization_barrier((routed, rhs))
-            state0 = jnp.take(rhs_now, local_pivots, axis=1)
-        back = swap_z(routed)
-        extra = [outer] if step == 1 else []
-        rows = ROWS * (1 + step)
-        (message,) = call(
-            lambda *refs: inverse_kernel(step, *refs),
-            f"inverse_part_{step}",
-            [((NZ, rows, TILE), BF)],
-            [VMEM] * (2 + len(extra)),
-            (back, start, *extra),
-        )
-        if step == 0:
-            slot_known = jnp.where(my_block >= STEPS, solved_now[:, :TILE], 0.0)
-            known = jnp.concatenate([slot_known, solved_now[:, TILE:]], axis=1).astype(BF)
-            outer = lax.dot_general(
-                known, lower_rows, (((1,), (2,)), ((), ())), preferred_element_type=F32
-            )
-            outer = outer.astype(BF).reshape(NZ, NY, rows_own, STEPS, TILE)
-            outer = outer.transpose(1, 0, 2, 3, 4).reshape(NY, NZ * rows_own * STEPS, TILE)
-            outer_sum = lax.dynamic_index_in_dim(outer, y, 0, False).astype(F32)
-            for other in range(1, NY):
-                theirs = lax.dynamic_index_in_dim(outer, y ^ other, 0, False)
-                outer_sum = outer_sum + pass_y(theirs, other).astype(F32)
-            outer = outer_sum.astype(BF).reshape(NZ, rows_own * STEPS, TILE)
-            outer = jnp.pad(outer, ((0, 0), (0, ROWS - rows_own * STEPS), (0, 0)))
         outs = [((ROWS, TILE), BF), ((NP, NY * ROWS, TILE), BF)]
         if step == 1:
-            outs.append(((ROWS, TILE), F32))
+            outs.append(((2 * ROWS, TILE), F32))
         value, message, *sums = call(
             lambda *refs: update_kernel(step, *refs),
             f"upper_update_{step}",
@@ -386,41 +365,50 @@
             (swap_z(message), *near),
         )
         finished.append(value)
-        outs = [((NZ * NY, ROWS, TILE), BF)]
+        back = swap_prow(message)
         if step == 0:
-            outs = [((NY, ROWS, TILE), F32), ((NZ, ROWS, TILE), BF)]
-        found = call(
-            lambda *refs: state_kernel(step, *refs),
-            f"next_state_{step}",
-            outs,
-            [SMEM, VMEM, VMEM],
-            (tile_of, swap_prow(message), tiles),
-        )
-        if step == 0:
-            tiles, routed = found
-
-    got = swap_z(found[0])
+            tiles, message = call(
+                lambda *refs: state_kernel(0, *refs),
+                "next_state_0",
+                [((NY, ROWS, TILE), F32), ((NZ, 3 * ROWS, TILE), BF)],
+                [SMEM] + [VMEM] * 5,
+                (tile_of, back, tiles, parts, outer_last, outer_rest),
+            )
+        else:
+            (message,) = call(
+                lambda *refs: state_kernel(1, *refs),
+                "next_state_1",
+                [((NZ, ROWS, TILE), BF)],
+                [SMEM] + [VMEM] * 3,
+                (tile_of, back, tiles, parts),
+            )
+
     order = jnp.arange(ROWS)
     pick_own = (
         (order[None, :] // rows_own == z) & (order[None, :] % rows_own == order[:, None] // PER)
     ).astype(BF)
-    outer = sums[0][: rows_own * STEPS].reshape(rows_own, STEPS, TILE)
+    outer = sums[0][ROWS : ROWS + rows_own * (STEPS - 1)].reshape(rows_own, STEPS - 1, TILE)
     outer = jnp.repeat(outer.transpose(1, 0, 2), PER, axis=1)
-    last, message = last_call(pos, got, pick_own, outer[STEPS - 1], pack_all)
+    last, message = call(
+        last_kernel,
+        "last_block",
+        [((ROWS, TILE), BF), ((NP, ROWS, TILE), BF)],
+        [VMEM] * 3,
+        (swap_z(message), sums[0][:ROWS], start),
+    )
     finished.append(last)
     bases = [
         jnp.dot(pick_own, finished[step], preferred_element_type=F32) - outer[step]
         for step in range(STEPS - 1)
     ]
-
-    message, pos_now = lax.optimization_barrier((message, pos))
-    weights = fetch_call(1, pos_now, pack_all)
     stacked = jnp.concatenate(finished, axis=0)
     pair = jnp.stack([stacked, pass_y(stacked, 1)])
-    back = swap_prow(message)
-    last, message = lower_call(1, back, bases[1], weights, [])
+    (message,) = call(
+        share_kernel, "share_last", [((NZ, ROWS, TILE), BF)], [VMEM], (swap_prow(message),)
+    )
     message, pair, pos_now = lax.optimization_barrier((message, pair, pos))
-    weights = fetch_call(0, pos_now, pack_all)
+    weights = fetch_call(1, pos_now, pack_all)
+    last, message = lower_call(1, swap_z(message), bases[1], weights, [pick_own])
 
     other = pass_y(pair, 2)
     every = [pair[0], pair[1], other[0], other[1]]
@@ -438,10 +426,13 @@
     bulk = jnp.concatenate([slot_bulk, bulk[:, TILE:]], axis=1).astype(BF)
     bulk = bulk.reshape(NP, count // NP * slots, TILE)
 
-    back = swap_prow(message)
-    middle, message = lower_call(0, back, bases[0], weights, [last])
+    message, pos_now = lax.optimization_barrier((message, pos))
+    weights = fetch_call(0, pos_now, pack_all)
     back = swap_prow(jnp.concatenate([message, bulk], axis=1))
-    first = total(back[:, :ROWS]).astype(BF)
+    middle, message = lower_call(0, back[:, :ROWS], bases[0], weights, [last])
+    message, rhs_now = lax.optimization_barrier((message, rhs))
+    state0 = jnp.take(rhs_now, local_pivots, axis=1)
+    first = total(swap_prow(message)).astype(BF)
 
     window = jnp.concatenate([first, middle, last], axis=0)
     window = window.reshape(STEPS, rows_own, PER, TILE).transpose(0, 2, 1, 3)

time: 216 us -> 211 us (0.977)
  waiting for transfers between devices: 65.9 us -> 61.8 us
    all_to_all x5, waiting for transfers between devices: 41.7 us -> 29.8 us  [swap_z(): lax.all_to_all(x, 'pcol', 0, 0, axis_index_groups=Z_GROUPS, tiled=True)]
    all_to_all x5, waiting for transfers between devices: 11.5 us -> 20.5 us  [swap_prow(): return lax.all_to_all(x, 'prow', 0, 0, tiled=True)]
    pallas_call x1 -> x0, Pallas kernels: 3.44 us -> none  [last_call(): pl.pallas_call(last_kernel, out_shape=(jax.ShapeDtypeStruct((ROWS, TILE),...]
    ppermute x8 -> x11, starting transfers between devices: 10 us -> 13.4 us  [pass_y(): return lax.ppermute(x, 'pcol', [(at, at ^ step) for at in range(NC)])]
    all_gather x1, waiting for transfers between devices: 3.35 us -> 0.02 us  [body(): pack_all = lax.all_gather(pack, 'pcol', axis=0)]
    all_to_all x5, starting transfers between devices: 32.8 us -> 30.1 us  [swap_prow(): return lax.all_to_all(x, 'prow', 0, 0, tiled=True)]
    pallas_call x12 -> x13, Pallas kernels: 17 us -> 18.7 us  [call(): pl.pallas_call(kernel, out_shape=tuple((jax.ShapeDtypeStruct(shape, dtype...]
  transfers between devices with their start and end apart: 25 -> 28, of which waited for: 13 -> 13; matrix products, arithmetic and copies ran while one was open for 11% -> 11% of each run, Pallas kernels for 6% -> 7%
where the time goes in v7:
time: 211 us; the launch traced here: 209 us
  starting transfers between devices  82.3 us (39%)
  waiting for transfers between devices  61.8 us (29%)
  Pallas kernels  18.7 us (9%)
  between operations  17.5 us (8%)
  local copies, waits for them, and re-layouts  15.8 us (7%)
  other arithmetic  6.36 us (3%)
  matrix products  6.13 us (3%)
    all_to_all x5, starting transfers between devices, swap_prow(): return lax.all_to_all(x, 'prow', 0, 0, tiled=True)  30.1 us
    all_to_all x5, waiting for transfers between devices, swap_z(): lax.all_to_all(x, 'pcol', 0, 0, axis_index_groups=Z_GROUPS, tiled=True)  29.8 us
    all_to_all x5, starting transfers between devices, swap_z(): lax.all_to_all(x, 'pcol', 0, 0, axis_index_groups=Z_GROUPS, tiled=True)  22.1 us
    all_to_all x5, waiting for transfers between devices, swap_prow(): return lax.all_to_all(x, 'prow', 0, 0, tiled=True)  20.5 us
    pallas_call x13, Pallas kernels, call(): pl.pallas_call(kernel, out_shape=tuple((jax.ShapeDtypeStruct(shape, dtype...  18.7 us
    ppermute x11, starting transfers between devices, pass_y(): return lax.ppermute(x, 'pcol', [(at, at ^ step) for at in range(NC)])  13.4 us
    all_to_all x1, starting transfers between devices, swap_pcol(): return lax.all_to_all(x, 'pcol', 0, 0, tiled=True)  7.24 us
    all_to_all x1, waiting for transfers between devices, swap_y(): lax.all_to_all(x, 'pcol', 0, 0, axis_index_groups=Y_GROUPS, tiled=True)  5.87 us
  transfers between devices with their start and end apart: 28, of which 13 were waited for; matrix products, arithmetic and copies ran while one was open for 11% of the time, Pallas kernels for 7%

profile of v7, /device:TPU:1, one launch (start us, length us, event | category | flops | bytes accessed | tf_op | source)
XLA Modules:
  0.0 208.6 jit_solution(4816083947533440719)
XLA Ops:
  14.1 5.0 %all-to-all-start = ((bf16[4,160,256]{2,1,0:T(8,128)(2,1)}), bf16[4,160,256]{2,1,0:T(8,128)(2,1)S(1)}, u32[]{:S(2)}, u32[]{:S(2)}) async-start(bf16[4,160,256]{2,1,0:T(8,128)(2,1)} %pad_maximum_fusion.3), calls=%async_computation | async-start | bytes 655360 | tf_op jit(solution)/shard_map/all_to_all | solution.py:33
  19.1 5.9 %all-to-all-done.got = bf16[4,160,256]{2,1,0:T(8,128)(2,1)S(1)} async-done(((bf16[4,160,256]{2,1,0:T(8,128)(2,1)}), bf16[4,160,256]{2,1,0:T(8,128)(2,1)S(1)}, u32[]{:S(2)}, u32[]{:S(2)}) %all-to-all-start) | async-done | bytes 327712 | tf_op jit(solution)/shard_map/all_to_all | solution.py:33
  26.5 8.5 %all-to-all-start.1 = ((bf16[8,144,256]{2,1,0:T(8,128)(2,1)}), bf16[8,144,256]{2,1,0:T(8,128)(2,1)S(1)}, u32[]{:S(2)}, u32[]{:S(2)}) async-start(bf16[8,144,256]{2,1,0:T(8,128)(2,1)} %get-tuple-element.38), calls=%async_computation.1 | async-start | bytes 1179648 | tf_op jit(solution)/shard_map/all_to_all | solution.py:52
  50.7 7.7 %all-to-all-done.1.back = bf16[8,144,256]{2,1,0:T(8,128)(2,1)S(1)} async-done(((bf16[8,144,256]{2,1,0:T(8,128)(2,1)}), bf16[8,144,256]{2,1,0:T(8,128)(2,1)S(1)}, u32[]{:S(2)}, u32[]{:S(2)}) %all-to-all-start.1) | async-done | bytes 589856 | tf_op jit(solution)/shard_map/all_to_all | solution.py:52
  59.7 3.4 %all-to-all-start.2 = ((bf16[8,16,256]{2,1,0:T(8,128)(2,1)}), bf16[8,16,256]{2,1,0:T(8,128)(2,1)S(1)}, u32[]{:S(2)}, u32[]{:S(2)}) async-start(bf16[8,16,256]{2,1,0:T(8,128)(2,1)} %get-tuple-element.39), calls=%async_computation.2 | async-start | bytes 131072 | tf_op jit(solution)/shard_map/all_to_all | solution.py:52
  63.2 3.1 %collective-permute-start.5 = (bf16[4,64,256]{2,1,0:T(8,128)(2,1)S(1)}, bf16[4,64,256]{2,1,0:T(8,128)(2,1)S(1)}, u32[]{:S(2)}, u32[]{:S(2)}) collective-permute-start(bf16[4,64,256]{2,1,0:T(8,128)(2,1)S(1)} %get-tuple-element.42), channel_id=1, source_target_pairs={{0,3},{1,2},{2,1},{3,0},{4,7},{5,6},{6,5},{7,4},{8,11},{9,10},{10,... | collective-permute-start | bytes 393224 | tf_op jit(solution)/shard_map/ppermute | solution.py:37
  66.4 3.8 %all-to-all-done.2.refs_0_ = bf16[8,16,256]{2,1,0:T(8,128)(2,1)S(1)} async-done(((bf16[8,16,256]{2,1,0:T(8,128)(2,1)}), bf16[8,16,256]{2,1,0:T(8,128)(2,1)S(1)}, u32[]{:S(2)}, u32[]{:S(2)}) %all-to-all-start.2) | async-done | bytes 65568 | tf_op jit(solution)/shard_map/all_to_all | solution.py:52
  71.1 7.4 %all-to-all-start.3 = ((bf16[8,64,256]{2,1,0:T(8,128)(2,1)}), bf16[8,64,256]{2,1,0:T(8,128)(2,1)S(1)}, u32[]{:S(2)}, u32[]{:S(2)}) async-start(bf16[8,64,256]{2,1,0:T(8,128)(2,1)} %get-tuple-element.40), calls=%async_computation.3 | async-start | bytes 524288 | tf_op jit(solution)/shard_map/all_to_all | solution.py:60
  78.6 6.3 %all-to-all-done.3.refs_1_ = bf16[8,64,256]{2,1,0:T(8,128)(2,1)S(1)} async-done(((bf16[8,64,256]{2,1,0:T(8,128)(2,1)}), bf16[8,64,256]{2,1,0:T(8,128)(2,1)S(1)}, u32[]{:S(2)}, u32[]{:S(2)}) %all-to-all-start.3) | async-done | bytes 262176 | tf_op jit(solution)/shard_map/all_to_all | solution.py:60
  86.4 3.4 %all-to-all-start.4 = ((bf16[8,48,256]{2,1,0:T(8,128)(2,1)}), bf16[8,48,256]{2,1,0:T(8,128)(2,1)S(1)}, u32[]{:S(2)}, u32[]{:S(2)}) async-start(bf16[8,48,256]{2,1,0:T(8,128)(2,1)} %get-tuple-element.44), calls=%async_computation.4 | async-start | bytes 393216 | tf_op jit(solution)/shard_map/all_to_all | solution.py:52
  89.9 9.8 %all-to-all-done.4.refs_0_ = bf16[8,48,256]{2,1,0:T(8,128)(2,1)S(1)} async-done(((bf16[8,48,256]{2,1,0:T(8,128)(2,1)}), bf16[8,48,256]{2,1,0:T(8,128)(2,1)S(1)}, u32[]{:S(2)}, u32[]{:S(2)}) %all-to-all-start.4) | async-done | bytes 196640 | tf_op jit(solution)/shard_map/all_to_all | solution.py:52
  100.6 6.8 %all-to-all-start.5 = ((bf16[8,64,256]{2,1,0:T(8,128)(2,1)}), bf16[8,64,256]{2,1,0:T(8,128)(2,1)S(1)}, u32[]{:S(2)}, u32[]{:S(2)}) async-start(bf16[8,64,256]{2,1,0:T(8,128)(2,1)} %get-tuple-element.45), calls=%async_computation.5 | async-start | bytes 524288 | tf_op jit(solution)/shard_map/all_to_all | solution.py:60
  109.0 5.0 %all-to-all-done.5.refs_1_ = bf16[8,64,256]{2,1,0:T(8,128)(2,1)S(1)} async-done(((bf16[8,64,256]{2,1,0:T(8,128)(2,1)}), bf16[8,64,256]{2,1,0:T(8,128)(2,1)S(1)}, u32[]{:S(2)}, u32[]{:S(2)}) %all-to-all-start.5) | async-done | bytes 262176 | tf_op jit(solution)/shard_map/all_to_all | solution.py:60
  115.4 3.4 %all-to-all-start.6 = ((bf16[8,16,256]{2,1,0:T(8,128)(2,1)}), bf16[8,16,256]{2,1,0:T(8,128)(2,1)S(1)}, u32[]{:S(2)}, u32[]{:S(2)}) async-start(bf16[8,16,256]{2,1,0:T(8,128)(2,1)} %next_state_1.1), calls=%async_computation.6 | async-start | bytes 131072 | tf_op jit(solution)/shard_map/all_to_all | solution.py:52
  118.8 7.8 %all-to-all-done.6.back = bf16[8,16,256]{2,1,0:T(8,128)(2,1)S(1)} async-done(((bf16[8,16,256]{2,1,0:T(8,128)(2,1)}), bf16[8,16,256]{2,1,0:T(8,128)(2,1)S(1)}, u32[]{:S(2)}, u32[]{:S(2)}) %all-to-all-start.6) | async-done | bytes 65568 | tf_op jit(solution)/shard_map/all_to_all | solution.py:52
  129.8 5.7 %all-to-all-start.7 = ((bf16[8,16,256]{2,1,0:T(8,128)(2,1)}), bf16[8,16,256]{2,1,0:T(8,128)(2,1)S(1)}, u32[]{:S(2)}, u32[]{:S(2)}) async-start(bf16[8,16,256]{2,1,0:T(8,128)(2,1)} %get-tuple-element.48), calls=%async_computation.7 | async-start | bytes 131072 | tf_op jit(solution)/shard_map/all_to_all | solution.py:60
  135.5 4.9 %all-to-all-done.7.back = bf16[8,16,256]{2,1,0:T(8,128)(2,1)S(1)} async-done(((bf16[8,16,256]{2,1,0:T(8,128)(2,1)}), bf16[8,16,256]{2,1,0:T(8,128)(2,1)S(1)}, u32[]{:S(2)}, u32[]{:S(2)}) %all-to-all-start.7) | async-done | bytes 65568 | tf_op jit(solution)/shard_map/all_to_all | solution.py:60
  141.0 3.5 %all-to-all-start.8 = ((bf16[8,16,256]{2,1,0:T(8,128)(2,1)}), bf16[8,16,256]{2,1,0:T(8,128)(2,1)S(1)}, u32[]{:S(2)}, u32[]{:S(2)}) async-start(bf16[8,16,256]{2,1,0:T(8,128)(2,1)} %share_last.1), calls=%async_computation.8 | async-start | bytes 131072 | tf_op jit(solution)/shard_map/all_to_all | solution.py:52
  153.7 6.0 %all-to-all-start.9 = ((bf16[8,80,256]{2,1,0:T(8,128)(2,1)}), bf16[8,80,256]{2,1,0:T(8,128)(2,1)}, u32[]{:S(2)}, u32[]{:S(2)}) async-start(bf16[8,80,256]{2,1,0:T(8,128)(2,1)} %pad_maximum_fusion.5), calls=%async_computation.9 | async-start | bytes 655360 | tf_op jit(solution)/shard_map/all_to_all | solution.py:60
  162.5 4.3 %all-to-all-done.9 = bf16[8,80,256]{2,1,0:T(8,128)(2,1)} async-done(((bf16[8,80,256]{2,1,0:T(8,128)(2,1)}), bf16[8,80,256]{2,1,0:T(8,128)(2,1)}, u32[]{:S(2)}, u32[]{:S(2)}) %all-to-all-start.9) | async-done | bytes 327712 | tf_op jit(solution)/shard_map/all_to_all | solution.py:60
  169.9 4.4 %all-to-all-start.10 = ((bf16[8,16,256]{2,1,0:T(8,128)(2,1)}), bf16[8,16,256]{2,1,0:T(8,128)(2,1)S(1)}, u32[]{:S(2)}, u32[]{:S(2)}) async-start(bf16[8,16,256]{2,1,0:T(8,128)(2,1)} %get-tuple-element.65), calls=%async_computation.10 | async-start | bytes 131072 | tf_op jit(solution)/shard_map/all_to_all | solution.py:60
  175.6 5.5 %gather_fusion.1 = f32[2048,64]{1,0:T(8,128)S(1)} fusion(f32[64,2048]{0,1:T(8,128)S(1)} %copy.27, s32[2048]{0:T(1024)S(1)} %fusion.14), kind=kCustom, calls=%fused_computation.1 | custom fusion | bytes 1056768 | tf_op jit(solution)/shard_map/jit(_take)/gather | solution.py:434
  183.5 7.2 %all-to-all-start.11 = ((bf16[32,2,256]{2,1,0:T(2,128)(2,1)}), bf16[32,2,256]{2,1,0:T(2,128)(2,1)S(1)}, u32[]{:S(2)}, u32[]{:S(2)}) async-start(bf16[32,2,256]{2,1,0:T(2,128)(2,1)} %reshape.209), calls=%async_computation.11 | async-start | bytes 65536 | tf_op jit(solution)/shard_map/all_to_all | solution.py:56
  195.0 3.1 %collective-permute-done.13 = bf16[2,64,256]{2,1,0:T(8,128)(2,1)S(1)} collective-permute-done((bf16[2,64,256]{2,1,0:T(8,128)(2,1)S(1)}, bf16[2,64,256]{2,1,0:T(8,128)(2,1)S(1)}, u32[]{:S(2)}, u32[]{:S(2)}) %collective-permute-start.13) | collective-permute-done | bytes 65568 | tf_op jit(solution)/shard_map/ppermute | solution.py:41
  (162 shorter events, 59.5 us)
Async XLA Ops:
  7.2 141.4 %all-gather.3.cloned.1.call-start = ((), (), s32[]{:S(2)}) async-start(), calls=%async_computation.12 | async-start | bytes 10813440 | tf_op jit(solution)/shard_map/all_gather | solution.py:308
  14.1 10.9 %all-to-all-start = ((bf16[4,160,256]{2,1,0:T(8,128)(2,1)}), bf16[4,160,256]{2,1,0:T(8,128)(2,1)S(1)}, u32[]{:S(2)}, u32[]{:S(2)}) async-start(bf16[4,160,256]{2,1,0:T(8,128)(2,1)} %pad_maximum_fusion.3), calls=%async_computation | async-start | bytes 655360 | tf_op jit(solution)/shard_map/all_to_all | solution.py:33
  26.5 31.9 %all-to-all-start.1 = ((bf16[8,144,256]{2,1,0:T(8,128)(2,1)}), bf16[8,144,256]{2,1,0:T(8,128)(2,1)S(1)}, u32[]{:S(2)}, u32[]{:S(2)}) async-start(bf16[8,144,256]{2,1,0:T(8,128)(2,1)} %get-tuple-element.38), calls=%async_computation.1 | async-start | bytes 1179648 | tf_op jit(solution)/shard_map/all_to_all | solution.py:52
  35.9 12.8 %collective-permute-start = (bf16[512,256]{1,0:T(8,128)(2,1)S(1)}, bf16[512,256]{1,0:T(8,128)(2,1)S(1)}, u32[]{:S(2)}, u32[]{:S(2)}) collective-permute-start(bf16[512,256]{1,0:T(8,128)(2,1)S(1)} %bitcast.79), channel_id=1, source_target_pairs={{0,1},{1,0},{2,3},{3,2},{4,5},{5,4},{6,7},{7,6},{8,9},{9,8},{10,11... | collective-permute-start | bytes 786440 | tf_op jit(solution)/shard_map/ppermute | solution.py:37
  36.3 30.1 %collective-permute-start.1 = (bf16[512,256]{1,0:T(8,128)(2,1)S(1)}, bf16[512,256]{1,0:T(8,128)(2,1)S(1)}, u32[]{:S(2)}, u32[]{:S(2)}) collective-permute-start(bf16[512,256]{1,0:T(8,128)(2,1)S(1)} %bitcast.80), channel_id=1, source_target_pairs={{0,2},{1,3},{2,0},{3,1},{4,6},{5,7},{6,4},{7,5},{8,10},{9,11},{10,... | collective-permute-start | bytes 786440 | tf_op jit(solution)/shard_map/ppermute | solution.py:37
  38.1 28.3 %collective-permute-start.2 = (bf16[512,256]{1,0:T(8,128)(2,1)S(1)}, bf16[512,256]{1,0:T(8,128)(2,1)S(1)}, u32[]{:S(2)}, u32[]{:S(2)}) collective-permute-start(bf16[512,256]{1,0:T(8,128)(2,1)S(1)} %bitcast.81), channel_id=1, source_target_pairs={{0,3},{1,2},{2,1},{3,0},{4,7},{5,6},{6,5},{7,4},{8,11},{9,10},{10,... | collective-permute-start | bytes 786440 | tf_op jit(solution)/shard_map/ppermute | solution.py:37
  46.6 16.4 %collective-permute-start.6 = (bf16[48,256]{1,0:T(8,128)(2,1)S(1)}, bf16[48,256]{1,0:T(8,128)(2,1)S(1)}, u32[]{:S(2)}, u32[]{:S(2)}) collective-permute-start(bf16[48,256]{1,0:T(8,128)(2,1)S(1)} %bitcast.106), channel_id=1, source_target_pairs={{0,1},{1,0},{2,3},{3,2},{4,5},{5,4},{6,7},{7,6},{8,9},{9,8},{10,11... | collective-permute-start | bytes 73736 | tf_op jit(solution)/shard_map/ppermute | solution.py:37
  46.7 16.4 %collective-permute-start.7 = (bf16[48,256]{1,0:T(8,128)(2,1)S(1)}, bf16[48,256]{1,0:T(8,128)(2,1)S(1)}, u32[]{:S(2)}, u32[]{:S(2)}) collective-permute-start(bf16[48,256]{1,0:T(8,128)(2,1)S(1)} %bitcast.105), channel_id=1, source_target_pairs={{0,2},{1,3},{2,0},{3,1},{4,6},{5,7},{6,4},{7,5},{8,10},{9,11},{10,... | collective-permute-start | bytes 73736 | tf_op jit(solution)/shard_map/ppermute | solution.py:37
  48.8 17.5 %collective-permute-start.8 = (bf16[48,256]{1,0:T(8,128)(2,1)S(1)}, bf16[48,256]{1,0:T(8,128)(2,1)S(1)}, u32[]{:S(2)}, u32[]{:S(2)}) collective-permute-start(bf16[48,256]{1,0:T(8,128)(2,1)S(1)} %bitcast.104), channel_id=1, source_target_pairs={{0,3},{1,2},{2,1},{3,0},{4,7},{5,6},{6,5},{7,4},{8,11},{9,10},{10,... | collective-permute-start | bytes 73736 | tf_op jit(solution)/shard_map/ppermute | solution.py:37
  59.7 10.5 %all-to-all-start.2 = ((bf16[8,16,256]{2,1,0:T(8,128)(2,1)}), bf16[8,16,256]{2,1,0:T(8,128)(2,1)S(1)}, u32[]{:S(2)}, u32[]{:S(2)}) async-start(bf16[8,16,256]{2,1,0:T(8,128)(2,1)} %get-tuple-element.39), calls=%async_computation.2 | async-start | bytes 131072 | tf_op jit(solution)/shard_map/all_to_all | solution.py:52
  63.0 15.5 %collective-permute-start.4 = (bf16[4,64,256]{2,1,0:T(8,128)(2,1)S(1)}, bf16[4,64,256]{2,1,0:T(8,128)(2,1)S(1)}, u32[]{:S(2)}, u32[]{:S(2)}) collective-permute-start(bf16[4,64,256]{2,1,0:T(8,128)(2,1)S(1)} %get-tuple-element.42), channel_id=1, source_target_pairs={{0,2},{1,3},{2,0},{3,1},{4,6},{5,7},{6,4},{7,5},{8,10},{9,11},{10,... | collective-permute-start | bytes 393224 | tf_op jit(solution)/shard_map/ppermute | solution.py:37
  63.2 15.4 %collective-permute-start.5 = (bf16[4,64,256]{2,1,0:T(8,128)(2,1)S(1)}, bf16[4,64,256]{2,1,0:T(8,128)(2,1)S(1)}, u32[]{:S(2)}, u32[]{:S(2)}) collective-permute-start(bf16[4,64,256]{2,1,0:T(8,128)(2,1)S(1)} %get-tuple-element.42), channel_id=1, source_target_pairs={{0,3},{1,2},{2,1},{3,0},{4,7},{5,6},{6,5},{7,4},{8,11},{9,10},{10,... | collective-permute-start | bytes 393224 | tf_op jit(solution)/shard_map/ppermute | solution.py:37
  66.3 12.3 %collective-permute-start.3 = (bf16[4,64,256]{2,1,0:T(8,128)(2,1)S(1)}, bf16[4,64,256]{2,1,0:T(8,128)(2,1)S(1)}, u32[]{:S(2)}, u32[]{:S(2)}) collective-permute-start(bf16[4,64,256]{2,1,0:T(8,128)(2,1)S(1)} %get-tuple-element.42), channel_id=1, source_target_pairs={{0,1},{1,0},{2,3},{3,2},{4,5},{5,4},{6,7},{7,6},{8,9},{9,8},{10,11... | collective-permute-start | bytes 393224 | tf_op jit(solution)/shard_map/ppermute | solution.py:37
  71.1 13.9 %all-to-all-start.3 = ((bf16[8,64,256]{2,1,0:T(8,128)(2,1)}), bf16[8,64,256]{2,1,0:T(8,128)(2,1)S(1)}, u32[]{:S(2)}, u32[]{:S(2)}) async-start(bf16[8,64,256]{2,1,0:T(8,128)(2,1)} %get-tuple-element.40), calls=%async_computation.3 | async-start | bytes 524288 | tf_op jit(solution)/shard_map/all_to_all | solution.py:60
  86.4 13.3 %all-to-all-start.4 = ((bf16[8,48,256]{2,1,0:T(8,128)(2,1)}), bf16[8,48,256]{2,1,0:T(8,128)(2,1)S(1)}, u32[]{:S(2)}, u32[]{:S(2)}) async-start(bf16[8,48,256]{2,1,0:T(8,128)(2,1)} %get-tuple-element.44), calls=%async_computation.4 | async-start | bytes 393216 | tf_op jit(solution)/shard_map/all_to_all | solution.py:52
  100.6 13.3 %all-to-all-start.5 = ((bf16[8,64,256]{2,1,0:T(8,128)(2,1)}), bf16[8,64,256]{2,1,0:T(8,128)(2,1)S(1)}, u32[]{:S(2)}, u32[]{:S(2)}) async-start(bf16[8,64,256]{2,1,0:T(8,128)(2,1)} %get-tuple-element.45), calls=%async_computation.5 | async-start | bytes 524288 | tf_op jit(solution)/shard_map/all_to_all | solution.py:60
  115.4 11.2 %all-to-all-start.6 = ((bf16[8,16,256]{2,1,0:T(8,128)(2,1)}), bf16[8,16,256]{2,1,0:T(8,128)(2,1)S(1)}, u32[]{:S(2)}, u32[]{:S(2)}) async-start(bf16[8,16,256]{2,1,0:T(8,128)(2,1)} %next_state_1.1), calls=%async_computation.6 | async-start | bytes 131072 | tf_op jit(solution)/shard_map/all_to_all | solution.py:52
  127.4 8.1 %collective-permute-start.9 = (bf16[48,256]{1,0:T(8,128)(2,1)S(1)}, bf16[48,256]{1,0:T(8,128)(2,1)S(1)}, u32[]{:S(2)}, u32[]{:S(2)}) collective-permute-start(bf16[48,256]{1,0:T(8,128)(2,1)S(1)} %constant_dynamic-update-slice_fusion), channel_id=1, source_target_pairs={{0,1},{1,0},{2,3},{3,2},{4,5},{5,4},{6,7},{7,6},{8,9},{9,8},{10,11... | collective-permute-start | bytes 73736 | tf_op jit(solution)/shard_map/ppermute | solution.py:37
  129.8 10.5 %all-to-all-start.7 = ((bf16[8,16,256]{2,1,0:T(8,128)(2,1)}), bf16[8,16,256]{2,1,0:T(8,128)(2,1)S(1)}, u32[]{:S(2)}, u32[]{:S(2)}) async-start(bf16[8,16,256]{2,1,0:T(8,128)(2,1)} %get-tuple-element.48), calls=%async_computation.7 | async-start | bytes 131072 | tf_op jit(solution)/shard_map/all_to_all | solution.py:60
  141.0 10.6 %all-to-all-start.8 = ((bf16[8,16,256]{2,1,0:T(8,128)(2,1)}), bf16[8,16,256]{2,1,0:T(8,128)(2,1)S(1)}, u32[]{:S(2)}, u32[]{:S(2)}) async-start(bf16[8,16,256]{2,1,0:T(8,128)(2,1)} %share_last.1), calls=%async_computation.8 | async-start | bytes 131072 | tf_op jit(solution)/shard_map/all_to_all | solution.py:52
  153.7 13.2 %all-to-all-start.9 = ((bf16[8,80,256]{2,1,0:T(8,128)(2,1)}), bf16[8,80,256]{2,1,0:T(8,128)(2,1)}, u32[]{:S(2)}, u32[]{:S(2)}) async-start(bf16[8,80,256]{2,1,0:T(8,128)(2,1)} %pad_maximum_fusion.5), calls=%async_computation.9 | async-start | bytes 655360 | tf_op jit(solution)/shard_map/all_to_all | solution.py:60
  169.9 12.7 %all-to-all-start.10 = ((bf16[8,16,256]{2,1,0:T(8,128)(2,1)}), bf16[8,16,256]{2,1,0:T(8,128)(2,1)S(1)}, u32[]{:S(2)}, u32[]{:S(2)}) async-start(bf16[8,16,256]{2,1,0:T(8,128)(2,1)} %get-tuple-element.65), calls=%async_computation.10 | async-start | bytes 131072 | tf_op jit(solution)/shard_map/all_to_all | solution.py:60
  183.4 7.4 %collective-permute-start.11 = (bf16[64,256]{1,0:T(8,128)(2,1)S(1)}, bf16[64,256]{1,0:T(8,128)(2,1)S(1)}, u32[]{:S(2)}, u32[]{:S(2)}) collective-permute-start(bf16[64,256]{1,0:T(8,128)(2,1)S(1)} %slice_reduce_fusion), channel_id=1, source_target_pairs={{0,32},{32,0},{64,96},{96,64},{128,160},{160,128},{192,224},{224,1... | collective-permute-start | bytes 98312 | tf_op jit(solution)/shard_map/ppermute | solution.py:41
  183.5 17.4 %all-to-all-start.11 = ((bf16[32,2,256]{2,1,0:T(2,128)(2,1)}), bf16[32,2,256]{2,1,0:T(2,128)(2,1)S(1)}, u32[]{:S(2)}, u32[]{:S(2)}) async-start(bf16[32,2,256]{2,1,0:T(2,128)(2,1)} %reshape.209), calls=%async_computation.11 | async-start | bytes 65536 | tf_op jit(solution)/shard_map/all_to_all | solution.py:56
  (9 other events, 114.6 us)
Sparse Core Ops, SparseCore 0:
  11.2 124.2 all-gather.2

commit v8 on v7

--- a/solution.py
+++ b/solution.py
@@ -246,8 +246,9 @@
 
 
 def lower_kernel(step, back, base, tiles, inverse, *rest):
-    known = rest[:-2]
-    value_out, message_out = rest[-2:]
+    outs = 2 if step == STEPS - 2 else 3
+    known = rest[:-outs]
+    value_out, message_out = rest[-outs : len(rest) - outs + 2]
     if step == STEPS - 2:
         pick_own = known[0][...]
         value = jnp.zeros((ROWS, TILE), F32)
@@ -255,7 +256,9 @@
             value = jnp.where(place_mask(place), dot_nn(pick_own, back[place]), value)
         value = value.astype(BF)
     else:
-        value = jnp.sum(back[...].astype(F32), axis=0).astype(BF)
+        value = jnp.sum(back[:, pl.ds(0, ROWS), :].astype(F32), axis=0).astype(BF)
+        bulk = jnp.sum(back[:, pl.ds(ROWS, back.shape[1] - ROWS), :].astype(F32), axis=0)
+        rest[-1][...] = bulk.astype(BF)
     value_out[...] = value
     sums = jnp.zeros((ROWS, TILE), F32)
     for at in range(STEPS - 1 - step):
@@ -269,14 +272,21 @@
     sums = jnp.broadcast_to(sums, (ROWS // PER, PER, TILE)).reshape(ROWS, TILE)
     part = lower_part((base[...] - sums).astype(BF), inverse)
     for index in range(NP):
-        message_out[index] = part
+        message_out[index, pl.ds(0, ROWS), :] = part
+        if step == STEPS - 2:
+            message_out[index, pl.ds(ROWS, known[1].shape[1]), :] = known[1][index]
 
 
 def lower_call(step, back, base, weights, known):
+    outs = [((ROWS, TILE), BF), ((NP, ROWS, TILE), BF)]
+    if step == STEPS - 2:
+        outs[1] = ((NP, ROWS + known[1].shape[1], TILE), BF)
+    else:
+        outs.append(((back.shape[1] - ROWS, TILE), BF))
     return call(
         lambda *refs: lower_kernel(step, *refs),
         f"lower_block_{step}",
-        [((ROWS, TILE), BF), ((NP, ROWS, TILE), BF)],
+        outs,
         [VMEM] * (4 + len(known)),
         (back, base, *weights, *known),
         grant=16 << 20,
@@ -374,6 +384,8 @@
                 [SMEM] + [VMEM] * 5,
                 (tile_of, back, tiles, parts, outer_last, outer_rest),
             )
+            message, rhs_now = lax.optimization_barrier((message, rhs))
+            state0 = jnp.take(rhs_now, local_pivots, axis=1)
         else:
             (message,) = call(
                 lambda *refs: state_kernel(1, *refs),
@@ -382,6 +394,7 @@
                 [SMEM] + [VMEM] * 3,
                 (tile_of, back, tiles, parts),
             )
+            message, state0 = lax.optimization_barrier((message, state0))
 
     order = jnp.arange(ROWS)
     pick_own = (
@@ -408,7 +421,7 @@
     )
     message, pair, pos_now = lax.optimization_barrier((message, pair, pos))
     weights = fetch_call(1, pos_now, pack_all)
-    last, message = lower_call(1, swap_z(message), bases[1], weights, [pick_own])
+    shared = swap_z(message)
 
     other = pass_y(pair, 2)
     every = [pair[0], pair[1], other[0], other[1]]
@@ -426,19 +439,16 @@
     bulk = jnp.concatenate([slot_bulk, bulk[:, TILE:]], axis=1).astype(BF)
     bulk = bulk.reshape(NP, count // NP * slots, TILE)
 
+    last, message = lower_call(1, shared, bases[1], weights, [pick_own, bulk])
     message, pos_now = lax.optimization_barrier((message, pos))
     weights = fetch_call(0, pos_now, pack_all)
-    back = swap_prow(jnp.concatenate([message, bulk], axis=1))
-    middle, message = lower_call(0, back[:, :ROWS], bases[0], weights, [last])
-    message, rhs_now = lax.optimization_barrier((message, rhs))
-    state0 = jnp.take(rhs_now, local_pivots, axis=1)
+    back = swap_prow(message)
+    middle, message, bulk = lower_call(0, back, bases[0], weights, [last])
     first = total(swap_prow(message)).astype(BF)
 
     window = jnp.concatenate([first, middle, last], axis=0)
     window = window.reshape(STEPS, rows_own, PER, TILE).transpose(0, 2, 1, 3)
     window = choose(window.reshape(STEPS * PER, rows_own, TILE), first_tiles)
-    bulk = total(back[:, ROWS:]).astype(BF)
-    window, bulk = lax.optimization_barrier((window, bulk))
     window = swap_pcol(window)
     pair = jnp.stack([bulk, pass_prow(bulk, 1)])
     pairs = [pair] + [pass_prow(pair, step) for step in range(2, NP, 2)]

time: 211 us -> 209 us (level)
  waiting for transfers between devices: 61.8 us -> 54.8 us
  local copies, waits for them, and re-layouts: 15.8 us -> 19.6 us
    all_to_all x1, waiting for transfers between devices: 0.01 us -> 5.59 us  [swap_pcol(): return lax.all_to_all(x, 'pcol', 0, 0, tiled=True)]
    all_to_all x1, waiting for transfers between devices: 5.87 us -> 0.78 us  [swap_y(): lax.all_to_all(x, 'pcol', 0, 0, axis_index_groups=Y_GROUPS, tiled=True)]
    ppermute x4, waiting for transfers between devices: 4.66 us -> 0.01 us  [pass_prow(): return lax.ppermute(x, 'prow', [(at, at ^ step) for at in range(NP)])]
    gather x2, local copies, waits for them, and re-layouts: 5.78 us -> 10.4 us  [body(): state0 = jnp.take(rhs_now, local_pivots, axis=1)]
    all_to_all x5, waiting for transfers between devices: 29.8 us -> 26.3 us  [swap_z(): lax.all_to_all(x, 'pcol', 0, 0, axis_index_groups=Z_GROUPS, tiled=True)]
    all_to_all x5, starting transfers between devices: 22.1 us -> 25.6 us  [swap_z(): lax.all_to_all(x, 'pcol', 0, 0, axis_index_groups=Z_GROUPS, tiled=True)]
  transfers between devices with their start and end apart: 28 -> 28, of which waited for: 13 -> 11; matrix products, arithmetic and copies ran while one was open for 11% -> 14% of each run, Pallas kernels for 7% -> 7%
where the time goes in v8:
time: 209 us; the launch traced here: 207 us
  starting transfers between devices  83.6 us (40%)
  waiting for transfers between devices  54.8 us (26%)
  local copies, waits for them, and re-layouts  19.6 us (9%)
  Pallas kernels  18.8 us (9%)
  between operations  17.4 us (8%)
  other arithmetic  7.17 us (3%)
  matrix products  6.12 us (3%)
    all_to_all x5, starting transfers between devices, swap_prow(): return lax.all_to_all(x, 'prow', 0, 0, tiled=True)  28.3 us
    all_to_all x5, waiting for transfers between devices, swap_z(): lax.all_to_all(x, 'pcol', 0, 0, axis_index_groups=Z_GROUPS, tiled=True)  26.3 us
    all_to_all x5, starting transfers between devices, swap_z(): lax.all_to_all(x, 'pcol', 0, 0, axis_index_groups=Z_GROUPS, tiled=True)  25.6 us
    all_to_all x5, waiting for transfers between devices, swap_prow(): return lax.all_to_all(x, 'prow', 0, 0, tiled=True)  22.1 us
    pallas_call x13, Pallas kernels, call(): pl.pallas_call(kernel, out_shape=tuple((jax.ShapeDtypeStruct(shape, dtype...  18.8 us
    ppermute x11, starting transfers between devices, pass_y(): return lax.ppermute(x, 'pcol', [(at, at ^ step) for at in range(NC)])  14.1 us
    gather x2, local copies, waits for them, and re-layouts, body(): state0 = jnp.take(rhs_now, local_pivots, axis=1)  10.4 us
    all_to_all x1, waiting for transfers between devices, swap_pcol(): return lax.all_to_all(x, 'pcol', 0, 0, tiled=True)  5.59 us
  transfers between devices with their start and end apart: 28, of which 11 were waited for; matrix products, arithmetic and copies ran while one was open for 14% of the time, Pallas kernels for 7%

profile of v8, /device:TPU:1, one launch (start us, length us, event | category | flops | bytes accessed | tf_op | source)
XLA Modules:
  0.0 207.4 jit_solution(11413124849490288952)
XLA Ops:
  14.1 5.0 %all-to-all-start = ((bf16[4,160,256]{2,1,0:T(8,128)(2,1)}), bf16[4,160,256]{2,1,0:T(8,128)(2,1)S(1)}, u32[]{:S(2)}, u32[]{:S(2)}) async-start(bf16[4,160,256]{2,1,0:T(8,128)(2,1)} %pad_maximum_fusion.3), calls=%async_computation | async-start | bytes 655360 | tf_op jit(solution)/shard_map/all_to_all | solution.py:33
  26.5 8.5 %all-to-all-start.1 = ((bf16[8,144,256]{2,1,0:T(8,128)(2,1)}), bf16[8,144,256]{2,1,0:T(8,128)(2,1)S(1)}, u32[]{:S(2)}, u32[]{:S(2)}) async-start(bf16[8,144,256]{2,1,0:T(8,128)(2,1)} %get-tuple-element.39), calls=%async_computation.1 | async-start | bytes 1179648 | tf_op jit(solution)/shard_map/all_to_all | solution.py:52
  38.3 3.0 %convolution_convert_fusion = bf16[64,3,256]{2,0,1:T(8,128)(2,1)S(1)} fusion(bf16[3,256,2048]{2,1,0:T(8,128)(2,1)} %param.13, bf16[64,1792]{1,0:T(8,128)(2,1)S(1)} %slice.167, bf16[64,256]{1,0:T(8,128)(2,1)S(1)} %select_convert_fusion), kind=kOutput, calls=%fused_computation.2 | convolution fusion | flops 201900032 | bytes 3506176 | tf_op jit(solution)/shard_map/dot_general | solution.py:351
  45.7 12.8 %all-to-all-done.1.back = bf16[8,144,256]{2,1,0:T(8,128)(2,1)S(1)} async-done(((bf16[8,144,256]{2,1,0:T(8,128)(2,1)}), bf16[8,144,256]{2,1,0:T(8,128)(2,1)S(1)}, u32[]{:S(2)}, u32[]{:S(2)}) %all-to-all-start.1) | async-done | bytes 589856 | tf_op jit(solution)/shard_map/all_to_all | solution.py:52
  59.8 3.4 %all-to-all-start.2 = ((bf16[8,16,256]{2,1,0:T(8,128)(2,1)}), bf16[8,16,256]{2,1,0:T(8,128)(2,1)S(1)}, u32[]{:S(2)}, u32[]{:S(2)}) async-start(bf16[8,16,256]{2,1,0:T(8,128)(2,1)} %get-tuple-element.40), calls=%async_computation.2 | async-start | bytes 131072 | tf_op jit(solution)/shard_map/all_to_all | solution.py:52
  66.1 4.2 %all-to-all-done.2.refs_0_ = bf16[8,16,256]{2,1,0:T(8,128)(2,1)S(1)} async-done(((bf16[8,16,256]{2,1,0:T(8,128)(2,1)}), bf16[8,16,256]{2,1,0:T(8,128)(2,1)S(1)}, u32[]{:S(2)}, u32[]{:S(2)}) %all-to-all-start.2) | async-done | bytes 65568 | tf_op jit(solution)/shard_map/all_to_all | solution.py:52
  71.2 8.7 %all-to-all-start.3 = ((bf16[8,64,256]{2,1,0:T(8,128)(2,1)}), bf16[8,64,256]{2,1,0:T(8,128)(2,1)S(1)}, u32[]{:S(2)}, u32[]{:S(2)}) async-start(bf16[8,64,256]{2,1,0:T(8,128)(2,1)} %get-tuple-element.41), calls=%async_computation.3 | async-start | bytes 524288 | tf_op jit(solution)/shard_map/all_to_all | solution.py:60
  80.1 6.3 %all-to-all-done.3.refs_1_ = bf16[8,64,256]{2,1,0:T(8,128)(2,1)S(1)} async-done(((bf16[8,64,256]{2,1,0:T(8,128)(2,1)}), bf16[8,64,256]{2,1,0:T(8,128)(2,1)S(1)}, u32[]{:S(2)}, u32[]{:S(2)}) %all-to-all-start.3) | async-done | bytes 262176 | tf_op jit(solution)/shard_map/all_to_all | solution.py:60
  87.8 3.4 %all-to-all-start.4 = ((bf16[8,48,256]{2,1,0:T(8,128)(2,1)}), bf16[8,48,256]{2,1,0:T(8,128)(2,1)S(1)}, u32[]{:S(2)}, u32[]{:S(2)}) async-start(bf16[8,48,256]{2,1,0:T(8,128)(2,1)} %get-tuple-element.46), calls=%async_computation.4 | async-start | bytes 393216 | tf_op jit(solution)/shard_map/all_to_all | solution.py:52
  94.1 8.8 %gather_fusion.1 = f32[2048,64]{1,0:T(8,128)} fusion(f32[64,2048]{0,1:T(8,128)} %copy.26, s32[2048]{0:T(1024)S(1)} %fusion.14), kind=kCustom, calls=%fused_computation.1 | custom fusion | bytes 1056768 | tf_op jit(solution)/shard_map/jit(_take)/gather | solution.py:388
  105.4 4.3 %all-to-all-start.5 = ((bf16[8,64,256]{2,1,0:T(8,128)(2,1)}), bf16[8,64,256]{2,1,0:T(8,128)(2,1)S(1)}, u32[]{:S(2)}, u32[]{:S(2)}) async-start(bf16[8,64,256]{2,1,0:T(8,128)(2,1)} %get-tuple-element.47), calls=%async_computation.5 | async-start | bytes 524288 | tf_op jit(solution)/shard_map/all_to_all | solution.py:60
  110.6 5.7 %all-to-all-done.5.refs_1_ = bf16[8,64,256]{2,1,0:T(8,128)(2,1)S(1)} async-done(((bf16[8,64,256]{2,1,0:T(8,128)(2,1)}), bf16[8,64,256]{2,1,0:T(8,128)(2,1)S(1)}, u32[]{:S(2)}, u32[]{:S(2)}) %all-to-all-start.5) | async-done | bytes 262176 | tf_op jit(solution)/shard_map/all_to_all | solution.py:60
  117.7 6.8 %all-to-all-start.6 = ((bf16[8,16,256]{2,1,0:T(8,128)(2,1)}), bf16[8,16,256]{2,1,0:T(8,128)(2,1)S(1)}, u32[]{:S(2)}, u32[]{:S(2)}) async-start(bf16[8,16,256]{2,1,0:T(8,128)(2,1)} %next_state_1.1), calls=%async_computation.6 | async-start | bytes 131072 | tf_op jit(solution)/shard_map/all_to_all | solution.py:52
  124.6 7.9 %all-to-all-done.6.back = bf16[8,16,256]{2,1,0:T(8,128)(2,1)S(1)} async-done(((bf16[8,16,256]{2,1,0:T(8,128)(2,1)}), bf16[8,16,256]{2,1,0:T(8,128)(2,1)S(1)}, u32[]{:S(2)}, u32[]{:S(2)}) %all-to-all-start.6) | async-done | bytes 65568 | tf_op jit(solution)/shard_map/all_to_all | solution.py:52
  134.9 6.0 %all-to-all-start.7 = ((bf16[8,16,256]{2,1,0:T(8,128)(2,1)}), bf16[8,16,256]{2,1,0:T(8,128)(2,1)S(1)}, u32[]{:S(2)}, u32[]{:S(2)}) async-start(bf16[8,16,256]{2,1,0:T(8,128)(2,1)} %get-tuple-element.52), calls=%async_computation.7 | async-start | bytes 131072 | tf_op jit(solution)/shard_map/all_to_all | solution.py:60
  140.9 4.9 %all-to-all-done.7.back = bf16[8,16,256]{2,1,0:T(8,128)(2,1)S(1)} async-done(((bf16[8,16,256]{2,1,0:T(8,128)(2,1)}), bf16[8,16,256]{2,1,0:T(8,128)(2,1)S(1)}, u32[]{:S(2)}, u32[]{:S(2)}) %all-to-all-start.7) | async-done | bytes 65568 | tf_op jit(solution)/shard_map/all_to_all | solution.py:60
  148.1 3.5 %all-to-all-start.8 = ((bf16[8,16,256]{2,1,0:T(8,128)(2,1)}), bf16[8,16,256]{2,1,0:T(8,128)(2,1)S(1)}, u32[]{:S(2)}, u32[]{:S(2)}) async-start(bf16[8,16,256]{2,1,0:T(8,128)(2,1)} %share_last.1), calls=%async_computation.8 | async-start | bytes 131072 | tf_op jit(solution)/shard_map/all_to_all | solution.py:52
  152.0 2.6 %fusion.2 = bf16[64,2048]{1,0:T(8,128)(2,1)S(1)} fusion(bf16[768,2048]{1,0:T(8,128)(2,1)} %bitcast.89, bf16[64,256]{1,0:T(8,128)(2,1)S(1)} %unstack.23, bf16[64,256]{1,0:T(8,128)(2,1)S(1)} %unstack.21, bf16[64,256]{1,0:T(8,128)(2,1)S(1)} %unstack.19), kind=kOutput, calls=%fused_computation.20 | convolution fusion | flops 201621504 | bytes 3506176 | tf_op jit(solution)/shard_map/dot_general | solution.py:430
  160.6 5.5 %all-to-all-start.9 = ((bf16[8,80,256]{2,1,0:T(8,128)(2,1)}), bf16[8,80,256]{2,1,0:T(8,128)(2,1)S(1)}, u32[]{:S(2)}, u32[]{:S(2)}) async-start(bf16[8,80,256]{2,1,0:T(8,128)(2,1)} %get-tuple-element.63), calls=%async_computation.9 | async-start | bytes 655360 | tf_op jit(solution)/shard_map/all_to_all | solution.py:60
  166.4 2.7 %fetch_block_0.1 = (bf16[2,256,2048]{2,1,0:T(8,128)(2,1)S(1)}, bf16[32,64,256]{2,1,0:T(8,128)(2,1)S(1)}) custom-call(s32[32]{0:T(128)S(1)} %tile_places.1.refs_0_, bf16[32,640,256]{2,1,0:T(8,128)(2,1)} %bitcast.88), custom_call_target="tpu_custom_call" | custom-call | tf_op jit(solution)/shard_map/fetch_block_0/pallas_call | solution.py:98
  169.0 4.3 %all-to-all-done.9.refs_0_ = bf16[8,80,256]{2,1,0:T(8,128)(2,1)S(1)} async-done(((bf16[8,80,256]{2,1,0:T(8,128)(2,1)}), bf16[8,80,256]{2,1,0:T(8,128)(2,1)S(1)}, u32[]{:S(2)}, u32[]{:S(2)}) %all-to-all-start.9) | async-done | bytes 327712 | tf_op jit(solution)/shard_map/all_to_all | solution.py:60
  176.1 3.8 %all-to-all-start.10 = ((bf16[8,16,256]{2,1,0:T(8,128)(2,1)}), bf16[8,16,256]{2,1,0:T(8,128)(2,1)S(1)}, u32[]{:S(2)}, u32[]{:S(2)}) async-start(bf16[8,16,256]{2,1,0:T(8,128)(2,1)} %copy-done), calls=%async_computation.10 | async-start | bytes 131072 | tf_op jit(solution)/shard_map/all_to_all | solution.py:60
  185.6 5.4 %all-to-all-start.11 = ((bf16[32,2,256]{2,1,0:T(2,128)(2,1)}), bf16[32,2,256]{2,1,0:T(2,128)(2,1)S(1)}, u32[]{:S(2)}, u32[]{:S(2)}) async-start(bf16[32,2,256]{2,1,0:T(2,128)(2,1)} %reshape.209), calls=%async_computation.11 | async-start | bytes 65536 | tf_op jit(solution)/shard_map/all_to_all | solution.py:56
  194.1 5.6 %all-to-all-done.11 = bf16[32,2,256]{2,1,0:T(2,128)(2,1)S(1)} async-done(((bf16[32,2,256]{2,1,0:T(2,128)(2,1)}), bf16[32,2,256]{2,1,0:T(2,128)(2,1)S(1)}, u32[]{:S(2)}, u32[]{:S(2)}) %all-to-all-start.11) | async-done | bytes 32800 | tf_op jit(solution)/shard_map/all_to_all | solution.py:56
  (163 shorter events, 57.1 us)
Async XLA Ops:
  7.2 147.6 %all-gather.3.cloned.1.call-start = ((), (), s32[]{:S(2)}) async-start(), calls=%async_computation.12 | async-start | bytes 10813440 | tf_op jit(solution)/shard_map/all_gather | solution.py:318
  14.1 10.9 %all-to-all-start = ((bf16[4,160,256]{2,1,0:T(8,128)(2,1)}), bf16[4,160,256]{2,1,0:T(8,128)(2,1)S(1)}, u32[]{:S(2)}, u32[]{:S(2)}) async-start(bf16[4,160,256]{2,1,0:T(8,128)(2,1)} %pad_maximum_fusion.3), calls=%async_computation | async-start | bytes 655360 | tf_op jit(solution)/shard_map/all_to_all | solution.py:33
  20.1 24.3 %collective-permute-start = (bf16[512,256]{1,0:T(8,128)(2,1)S(1)}, bf16[512,256]{1,0:T(8,128)(2,1)S(1)}, u32[]{:S(2)}, u32[]{:S(2)}) collective-permute-start(bf16[512,256]{1,0:T(8,128)(2,1)S(1)} %bitcast.79), channel_id=1, source_target_pairs={{0,1},{1,0},{2,3},{3,2},{4,5},{5,4},{6,7},{7,6},{8,9},{9,8},{10,11... | collective-permute-start | bytes 786440 | tf_op jit(solution)/shard_map/ppermute | solution.py:37
  21.6 44.5 %collective-permute-start.1 = (bf16[512,256]{1,0:T(8,128)(2,1)S(1)}, bf16[512,256]{1,0:T(8,128)(2,1)S(1)}, u32[]{:S(2)}, u32[]{:S(2)}) collective-permute-start(bf16[512,256]{1,0:T(8,128)(2,1)S(1)} %bitcast.80), channel_id=1, source_target_pairs={{0,2},{1,3},{2,0},{3,1},{4,6},{5,7},{6,4},{7,5},{8,10},{9,11},{10,... | collective-permute-start | bytes 786440 | tf_op jit(solution)/shard_map/ppermute | solution.py:37
  24.0 42.1 %collective-permute-start.2 = (bf16[512,256]{1,0:T(8,128)(2,1)S(1)}, bf16[512,256]{1,0:T(8,128)(2,1)S(1)}, u32[]{:S(2)}, u32[]{:S(2)}) collective-permute-start(bf16[512,256]{1,0:T(8,128)(2,1)S(1)} %bitcast.81), channel_id=1, source_target_pairs={{0,3},{1,2},{2,1},{3,0},{4,7},{5,6},{6,5},{7,4},{8,11},{9,10},{10,... | collective-permute-start | bytes 786440 | tf_op jit(solution)/shard_map/ppermute | solution.py:37
  26.5 32.0 %all-to-all-start.1 = ((bf16[8,144,256]{2,1,0:T(8,128)(2,1)}), bf16[8,144,256]{2,1,0:T(8,128)(2,1)S(1)}, u32[]{:S(2)}, u32[]{:S(2)}) async-start(bf16[8,144,256]{2,1,0:T(8,128)(2,1)} %get-tuple-element.39), calls=%async_computation.1 | async-start | bytes 1179648 | tf_op jit(solution)/shard_map/all_to_all | solution.py:52
  41.6 21.6 %collective-permute-start.6 = (bf16[48,256]{1,0:T(8,128)(2,1)S(1)}, bf16[48,256]{1,0:T(8,128)(2,1)S(1)}, u32[]{:S(2)}, u32[]{:S(2)}) collective-permute-start(bf16[48,256]{1,0:T(8,128)(2,1)S(1)} %bitcast.106), channel_id=1, source_target_pairs={{0,1},{1,0},{2,3},{3,2},{4,5},{5,4},{6,7},{7,6},{8,9},{9,8},{10,11... | collective-permute-start | bytes 73736 | tf_op jit(solution)/shard_map/ppermute | solution.py:37
  42.0 22.3 %collective-permute-start.7 = (bf16[48,256]{1,0:T(8,128)(2,1)S(1)}, bf16[48,256]{1,0:T(8,128)(2,1)S(1)}, u32[]{:S(2)}, u32[]{:S(2)}) collective-permute-start(bf16[48,256]{1,0:T(8,128)(2,1)S(1)} %bitcast.105), channel_id=1, source_target_pairs={{0,2},{1,3},{2,0},{3,1},{4,6},{5,7},{6,4},{7,5},{8,10},{9,11},{10,... | collective-permute-start | bytes 73736 | tf_op jit(solution)/shard_map/ppermute | solution.py:37
  44.4 21.6 %collective-permute-start.8 = (bf16[48,256]{1,0:T(8,128)(2,1)S(1)}, bf16[48,256]{1,0:T(8,128)(2,1)S(1)}, u32[]{:S(2)}, u32[]{:S(2)}) collective-permute-start(bf16[48,256]{1,0:T(8,128)(2,1)S(1)} %bitcast.104), channel_id=1, source_target_pairs={{0,3},{1,2},{2,1},{3,0},{4,7},{5,6},{6,5},{7,4},{8,11},{9,10},{10,... | collective-permute-start | bytes 73736 | tf_op jit(solution)/shard_map/ppermute | solution.py:37
  59.8 10.5 %all-to-all-start.2 = ((bf16[8,16,256]{2,1,0:T(8,128)(2,1)}), bf16[8,16,256]{2,1,0:T(8,128)(2,1)S(1)}, u32[]{:S(2)}, u32[]{:S(2)}) async-start(bf16[8,16,256]{2,1,0:T(8,128)(2,1)} %get-tuple-element.40), calls=%async_computation.2 | async-start | bytes 131072 | tf_op jit(solution)/shard_map/all_to_all | solution.py:52
  63.2 16.8 %collective-permute-start.4 = (bf16[4,64,256]{2,1,0:T(8,128)(2,1)S(1)}, bf16[4,64,256]{2,1,0:T(8,128)(2,1)S(1)}, u32[]{:S(2)}, u32[]{:S(2)}) collective-permute-start(bf16[4,64,256]{2,1,0:T(8,128)(2,1)S(1)} %get-tuple-element.43), channel_id=1, source_target_pairs={{0,2},{1,3},{2,0},{3,1},{4,6},{5,7},{6,4},{7,5},{8,10},{9,11},{10,... | collective-permute-start | bytes 393224 | tf_op jit(solution)/shard_map/ppermute | solution.py:37
  64.2 15.7 %collective-permute-start.5 = (bf16[4,64,256]{2,1,0:T(8,128)(2,1)S(1)}, bf16[4,64,256]{2,1,0:T(8,128)(2,1)S(1)}, u32[]{:S(2)}, u32[]{:S(2)}) collective-permute-start(bf16[4,64,256]{2,1,0:T(8,128)(2,1)S(1)} %get-tuple-element.43), channel_id=1, source_target_pairs={{0,3},{1,2},{2,1},{3,0},{4,7},{5,6},{6,5},{7,4},{8,11},{9,10},{10,... | collective-permute-start | bytes 393224 | tf_op jit(solution)/shard_map/ppermute | solution.py:37
  66.0 14.0 %collective-permute-start.3 = (bf16[4,64,256]{2,1,0:T(8,128)(2,1)S(1)}, bf16[4,64,256]{2,1,0:T(8,128)(2,1)S(1)}, u32[]{:S(2)}, u32[]{:S(2)}) collective-permute-start(bf16[4,64,256]{2,1,0:T(8,128)(2,1)S(1)} %get-tuple-element.43), channel_id=1, source_target_pairs={{0,1},{1,0},{2,3},{3,2},{4,5},{5,4},{6,7},{7,6},{8,9},{9,8},{10,11... | collective-permute-start | bytes 393224 | tf_op jit(solution)/shard_map/ppermute | solution.py:37
  71.2 15.2 %all-to-all-start.3 = ((bf16[8,64,256]{2,1,0:T(8,128)(2,1)}), bf16[8,64,256]{2,1,0:T(8,128)(2,1)S(1)}, u32[]{:S(2)}, u32[]{:S(2)}) async-start(bf16[8,64,256]{2,1,0:T(8,128)(2,1)} %get-tuple-element.41), calls=%async_computation.3 | async-start | bytes 524288 | tf_op jit(solution)/shard_map/all_to_all | solution.py:60
  87.8 16.7 %all-to-all-start.4 = ((bf16[8,48,256]{2,1,0:T(8,128)(2,1)}), bf16[8,48,256]{2,1,0:T(8,128)(2,1)S(1)}, u32[]{:S(2)}, u32[]{:S(2)}) async-start(bf16[8,48,256]{2,1,0:T(8,128)(2,1)} %get-tuple-element.46), calls=%async_computation.4 | async-start | bytes 393216 | tf_op jit(solution)/shard_map/all_to_all | solution.py:52
  105.4 10.9 %all-to-all-start.5 = ((bf16[8,64,256]{2,1,0:T(8,128)(2,1)}), bf16[8,64,256]{2,1,0:T(8,128)(2,1)S(1)}, u32[]{:S(2)}, u32[]{:S(2)}) async-start(bf16[8,64,256]{2,1,0:T(8,128)(2,1)} %get-tuple-element.47), calls=%async_computation.5 | async-start | bytes 524288 | tf_op jit(solution)/shard_map/all_to_all | solution.py:60
  117.7 14.7 %all-to-all-start.6 = ((bf16[8,16,256]{2,1,0:T(8,128)(2,1)}), bf16[8,16,256]{2,1,0:T(8,128)(2,1)S(1)}, u32[]{:S(2)}, u32[]{:S(2)}) async-start(bf16[8,16,256]{2,1,0:T(8,128)(2,1)} %next_state_1.1), calls=%async_computation.6 | async-start | bytes 131072 | tf_op jit(solution)/shard_map/all_to_all | solution.py:52
  134.9 10.8 %all-to-all-start.7 = ((bf16[8,16,256]{2,1,0:T(8,128)(2,1)}), bf16[8,16,256]{2,1,0:T(8,128)(2,1)S(1)}, u32[]{:S(2)}, u32[]{:S(2)}) async-start(bf16[8,16,256]{2,1,0:T(8,128)(2,1)} %get-tuple-element.52), calls=%async_computation.7 | async-start | bytes 131072 | tf_op jit(solution)/shard_map/all_to_all | solution.py:60
  148.1 10.5 %all-to-all-start.8 = ((bf16[8,16,256]{2,1,0:T(8,128)(2,1)}), bf16[8,16,256]{2,1,0:T(8,128)(2,1)S(1)}, u32[]{:S(2)}, u32[]{:S(2)}) async-start(bf16[8,16,256]{2,1,0:T(8,128)(2,1)} %share_last.1), calls=%async_computation.8 | async-start | bytes 131072 | tf_op jit(solution)/shard_map/all_to_all | solution.py:52
  160.6 12.7 %all-to-all-start.9 = ((bf16[8,80,256]{2,1,0:T(8,128)(2,1)}), bf16[8,80,256]{2,1,0:T(8,128)(2,1)S(1)}, u32[]{:S(2)}, u32[]{:S(2)}) async-start(bf16[8,80,256]{2,1,0:T(8,128)(2,1)} %get-tuple-element.63), calls=%async_computation.9 | async-start | bytes 655360 | tf_op jit(solution)/shard_map/all_to_all | solution.py:60
  176.1 8.6 %all-to-all-start.10 = ((bf16[8,16,256]{2,1,0:T(8,128)(2,1)}), bf16[8,16,256]{2,1,0:T(8,128)(2,1)S(1)}, u32[]{:S(2)}, u32[]{:S(2)}) async-start(bf16[8,16,256]{2,1,0:T(8,128)(2,1)} %copy-done), calls=%async_computation.10 | async-start | bytes 131072 | tf_op jit(solution)/shard_map/all_to_all | solution.py:60
  179.9 11.1 %collective-permute-start.12 = (bf16[2,64,256]{2,1,0:T(8,128)(2,1)S(1)}, bf16[2,64,256]{2,1,0:T(8,128)(2,1)S(1)}, u32[]{:S(2)}, u32[]{:S(2)}) collective-permute-start(bf16[2,64,256]{2,1,0:T(8,128)(2,1)S(1)} %pad_maximum_fusion.8), channel_id=1, source_target_pairs={{0,64},{32,96},{64,0},{96,32},{128,192},{160,224},{192,128},{224,1... | collective-permute-start | bytes 196616 | tf_op jit(solution)/shard_map/ppermute | solution.py:41
  181.4 9.7 %collective-permute-start.13 = (bf16[2,64,256]{2,1,0:T(8,128)(2,1)S(1)}, bf16[2,64,256]{2,1,0:T(8,128)(2,1)S(1)}, u32[]{:S(2)}, u32[]{:S(2)}) collective-permute-start(bf16[2,64,256]{2,1,0:T(8,128)(2,1)S(1)} %pad_maximum_fusion.8), channel_id=1, source_target_pairs={{0,128},{32,160},{64,192},{96,224},{128,0},{160,32},{192,64},{224,... | collective-permute-start | bytes 196616 | tf_op jit(solution)/shard_map/ppermute | solution.py:41
  185.6 14.1 %all-to-all-start.11 = ((bf16[32,2,256]{2,1,0:T(2,128)(2,1)}), bf16[32,2,256]{2,1,0:T(2,128)(2,1)S(1)}, u32[]{:S(2)}, u32[]{:S(2)}) async-start(bf16[32,2,256]{2,1,0:T(2,128)(2,1)} %reshape.209), calls=%async_computation.11 | async-start | bytes 65536 | tf_op jit(solution)/shard_map/all_to_all | solution.py:56
  (11 other events, 178.4 us)
Sparse Core Ops, SparseCore 0:
  11.2 124.3 all-gather.2

commit v9 on v8

--- a/solution.py
+++ b/solution.py
@@ -384,8 +384,6 @@
                 [SMEM] + [VMEM] * 5,
                 (tile_of, back, tiles, parts, outer_last, outer_rest),
             )
-            message, rhs_now = lax.optimization_barrier((message, rhs))
-            state0 = jnp.take(rhs_now, local_pivots, axis=1)
         else:
             (message,) = call(
                 lambda *refs: state_kernel(1, *refs),
@@ -394,7 +392,6 @@
                 [SMEM] + [VMEM] * 3,
                 (tile_of, back, tiles, parts),
             )
-            message, state0 = lax.optimization_barrier((message, state0))
 
     order = jnp.arange(ROWS)
     pick_own = (
@@ -444,11 +441,14 @@
     weights = fetch_call(0, pos_now, pack_all)
     back = swap_prow(message)
     middle, message, bulk = lower_call(0, back, bases[0], weights, [last])
+    message, rhs_now = lax.optimization_barrier((message, rhs))
+    state0 = jnp.take(rhs_now, local_pivots, axis=1)
     first = total(swap_prow(message)).astype(BF)
 
     window = jnp.concatenate([first, middle, last], axis=0)
     window = window.reshape(STEPS, rows_own, PER, TILE).transpose(0, 2, 1, 3)
     window = choose(window.reshape(STEPS * PER, rows_own, TILE), first_tiles)
+    window, bulk = lax.optimization_barrier((window, bulk))
     window = swap_pcol(window)
     pair = jnp.stack([bulk, pass_prow(bulk, 1)])
     pairs = [pair] + [pass_prow(pair, step) for step in range(2, NP, 2)]

time: 209 us -> 208 us (level)
  waiting for transfers between devices: 54.8 us -> 60.9 us
  local copies, waits for them, and re-layouts: 19.6 us -> 16.2 us
  other arithmetic: 7.17 us -> 4.52 us
    all_to_all x1, waiting for transfers between devices: 5.59 us -> 0.01 us  [swap_pcol(): return lax.all_to_all(x, 'pcol', 0, 0, tiled=True)]
    all_to_all x1, waiting for transfers between devices: 0.78 us -> 5.87 us  [swap_y(): lax.all_to_all(x, 'pcol', 0, 0, axis_index_groups=Y_GROUPS, tiled=True)]
    ppermute x4, waiting for transfers between devices: 0.01 us -> 4.66 us  [pass_prow(): return lax.ppermute(x, 'prow', [(at, at ^ step) for at in range(NP)])]
    gather x2, local copies, waits for them, and re-layouts: 10.4 us -> 5.78 us  [body(): state0 = jnp.take(rhs_now, local_pivots, axis=1)]
    all_to_all x5, starting transfers between devices: 25.6 us -> 22.1 us  [swap_z(): lax.all_to_all(x, 'pcol', 0, 0, axis_index_groups=Z_GROUPS, tiled=True)]
    all_to_all x5, waiting for transfers between devices: 26.3 us -> 29.1 us  [swap_z(): lax.all_to_all(x, 'pcol', 0, 0, axis_index_groups=Z_GROUPS, tiled=True)]
  transfers between devices with their start and end apart: 28 -> 28, of which waited for: 11 -> 13; matrix products, arithmetic and copies ran while one was open for 14% -> 11% of each run, Pallas kernels for 7% -> 7%
where the time goes in v9:
time: 208 us; the launch traced here: 206 us
  starting transfers between devices  81.7 us (39%)
  waiting for transfers between devices  60.9 us (29%)
  Pallas kernels  18.8 us (9%)
  between operations  17.6 us (8%)
  local copies, waits for them, and re-layouts  16.2 us (8%)
  matrix products  6.1 us (3%)
  other arithmetic  4.52 us (2%)
    all_to_all x5, starting transfers between devices, swap_prow(): return lax.all_to_all(x, 'prow', 0, 0, tiled=True)  29.6 us
    all_to_all x5, waiting for transfers between devices, swap_z(): lax.all_to_all(x, 'pcol', 0, 0, axis_index_groups=Z_GROUPS, tiled=True)  29.1 us
    all_to_all x5, starting transfers between devices, swap_z(): lax.all_to_all(x, 'pcol', 0, 0, axis_index_groups=Z_GROUPS, tiled=True)  22.1 us
    all_to_all x5, waiting for transfers between devices, swap_prow(): return lax.all_to_all(x, 'prow', 0, 0, tiled=True)  20.4 us
    pallas_call x13, Pallas kernels, call(): pl.pallas_call(kernel, out_shape=tuple((jax.ShapeDtypeStruct(shape, dtype...  18.8 us
    ppermute x11, starting transfers between devices, pass_y(): return lax.ppermute(x, 'pcol', [(at, at ^ step) for at in range(NC)])  13.4 us
    all_to_all x1, starting transfers between devices, swap_pcol(): return lax.all_to_all(x, 'pcol', 0, 0, tiled=True)  7.33 us
    all_to_all x1, waiting for transfers between devices, swap_y(): lax.all_to_all(x, 'pcol', 0, 0, axis_index_groups=Y_GROUPS, tiled=True)  5.87 us
  transfers between devices with their start and end apart: 28, of which 13 were waited for; matrix products, arithmetic and copies ran while one was open for 11% of the time, Pallas kernels for 7%

profile of v9, /device:TPU:1, one launch (start us, length us, event | category | flops | bytes accessed | tf_op | source)
XLA Modules:
  0.0 205.9 jit_solution(16507858006988747614)
XLA Ops:
  14.1 5.0 %all-to-all-start = ((bf16[4,160,256]{2,1,0:T(8,128)(2,1)}), bf16[4,160,256]{2,1,0:T(8,128)(2,1)S(1)}, u32[]{:S(2)}, u32[]{:S(2)}) async-start(bf16[4,160,256]{2,1,0:T(8,128)(2,1)} %pad_maximum_fusion.3), calls=%async_computation | async-start | bytes 655360 | tf_op jit(solution)/shard_map/all_to_all | solution.py:33
  19.1 5.9 %all-to-all-done.got = bf16[4,160,256]{2,1,0:T(8,128)(2,1)S(1)} async-done(((bf16[4,160,256]{2,1,0:T(8,128)(2,1)}), bf16[4,160,256]{2,1,0:T(8,128)(2,1)S(1)}, u32[]{:S(2)}, u32[]{:S(2)}) %all-to-all-start) | async-done | bytes 327712 | tf_op jit(solution)/shard_map/all_to_all | solution.py:33
  26.5 8.5 %all-to-all-start.1 = ((bf16[8,144,256]{2,1,0:T(8,128)(2,1)}), bf16[8,144,256]{2,1,0:T(8,128)(2,1)S(1)}, u32[]{:S(2)}, u32[]{:S(2)}) async-start(bf16[8,144,256]{2,1,0:T(8,128)(2,1)} %get-tuple-element.39), calls=%async_computation.1 | async-start | bytes 1179648 | tf_op jit(solution)/shard_map/all_to_all | solution.py:52
  51.1 7.1 %all-to-all-done.1.back = bf16[8,144,256]{2,1,0:T(8,128)(2,1)S(1)} async-done(((bf16[8,144,256]{2,1,0:T(8,128)(2,1)}), bf16[8,144,256]{2,1,0:T(8,128)(2,1)S(1)}, u32[]{:S(2)}, u32[]{:S(2)}) %all-to-all-start.1) | async-done | bytes 589856 | tf_op jit(solution)/shard_map/all_to_all | solution.py:52
  59.5 3.4 %all-to-all-start.2 = ((bf16[8,16,256]{2,1,0:T(8,128)(2,1)}), bf16[8,16,256]{2,1,0:T(8,128)(2,1)S(1)}, u32[]{:S(2)}, u32[]{:S(2)}) async-start(bf16[8,16,256]{2,1,0:T(8,128)(2,1)} %get-tuple-element.40), calls=%async_computation.2 | async-start | bytes 131072 | tf_op jit(solution)/shard_map/all_to_all | solution.py:52
  63.0 3.3 %collective-permute-start.5 = (bf16[4,64,256]{2,1,0:T(8,128)(2,1)S(1)}, bf16[4,64,256]{2,1,0:T(8,128)(2,1)S(1)}, u32[]{:S(2)}, u32[]{:S(2)}) collective-permute-start(bf16[4,64,256]{2,1,0:T(8,128)(2,1)S(1)} %get-tuple-element.43), channel_id=1, source_target_pairs={{0,3},{1,2},{2,1},{3,0},{4,7},{5,6},{6,5},{7,4},{8,11},{9,10},{10,... | collective-permute-start | bytes 393224 | tf_op jit(solution)/shard_map/ppermute | solution.py:37
  66.4 3.6 %all-to-all-done.2.refs_0_ = bf16[8,16,256]{2,1,0:T(8,128)(2,1)S(1)} async-done(((bf16[8,16,256]{2,1,0:T(8,128)(2,1)}), bf16[8,16,256]{2,1,0:T(8,128)(2,1)S(1)}, u32[]{:S(2)}, u32[]{:S(2)}) %all-to-all-start.2) | async-done | bytes 65568 | tf_op jit(solution)/shard_map/all_to_all | solution.py:52
  70.9 7.6 %all-to-all-start.3 = ((bf16[8,64,256]{2,1,0:T(8,128)(2,1)}), bf16[8,64,256]{2,1,0:T(8,128)(2,1)S(1)}, u32[]{:S(2)}, u32[]{:S(2)}) async-start(bf16[8,64,256]{2,1,0:T(8,128)(2,1)} %get-tuple-element.41), calls=%async_computation.3 | async-start | bytes 524288 | tf_op jit(solution)/shard_map/all_to_all | solution.py:60
  78.7 6.3 %all-to-all-done.3.refs_1_ = bf16[8,64,256]{2,1,0:T(8,128)(2,1)S(1)} async-done(((bf16[8,64,256]{2,1,0:T(8,128)(2,1)}), bf16[8,64,256]{2,1,0:T(8,128)(2,1)S(1)}, u32[]{:S(2)}, u32[]{:S(2)}) %all-to-all-start.3) | async-done | bytes 262176 | tf_op jit(solution)/shard_map/all_to_all | solution.py:60
  86.5 3.4 %all-to-all-start.4 = ((bf16[8,48,256]{2,1,0:T(8,128)(2,1)}), bf16[8,48,256]{2,1,0:T(8,128)(2,1)S(1)}, u32[]{:S(2)}, u32[]{:S(2)}) async-start(bf16[8,48,256]{2,1,0:T(8,128)(2,1)} %get-tuple-element.45), calls=%async_computation.4 | async-start | bytes 393216 | tf_op jit(solution)/shard_map/all_to_all | solution.py:52
  90.0 10.0 %all-to-all-done.4.refs_0_ = bf16[8,48,256]{2,1,0:T(8,128)(2,1)S(1)} async-done(((bf16[8,48,256]{2,1,0:T(8,128)(2,1)}), bf16[8,48,256]{2,1,0:T(8,128)(2,1)S(1)}, u32[]{:S(2)}, u32[]{:S(2)}) %all-to-all-start.4) | async-done | bytes 196640 | tf_op jit(solution)/shard_map/all_to_all | solution.py:52
  100.9 6.7 %all-to-all-start.5 = ((bf16[8,64,256]{2,1,0:T(8,128)(2,1)}), bf16[8,64,256]{2,1,0:T(8,128)(2,1)S(1)}, u32[]{:S(2)}, u32[]{:S(2)}) async-start(bf16[8,64,256]{2,1,0:T(8,128)(2,1)} %get-tuple-element.46), calls=%async_computation.5 | async-start | bytes 524288 | tf_op jit(solution)/shard_map/all_to_all | solution.py:60
  109.1 5.0 %all-to-all-done.5.refs_1_ = bf16[8,64,256]{2,1,0:T(8,128)(2,1)S(1)} async-done(((bf16[8,64,256]{2,1,0:T(8,128)(2,1)}), bf16[8,64,256]{2,1,0:T(8,128)(2,1)S(1)}, u32[]{:S(2)}, u32[]{:S(2)}) %all-to-all-start.5) | async-done | bytes 262176 | tf_op jit(solution)/shard_map/all_to_all | solution.py:60
  115.5 3.4 %all-to-all-start.6 = ((bf16[8,16,256]{2,1,0:T(8,128)(2,1)}), bf16[8,16,256]{2,1,0:T(8,128)(2,1)S(1)}, u32[]{:S(2)}, u32[]{:S(2)}) async-start(bf16[8,16,256]{2,1,0:T(8,128)(2,1)} %next_state_1.1), calls=%async_computation.6 | async-start | bytes 131072 | tf_op jit(solution)/shard_map/all_to_all | solution.py:52
  118.9 7.8 %all-to-all-done.6.back = bf16[8,16,256]{2,1,0:T(8,128)(2,1)S(1)} async-done(((bf16[8,16,256]{2,1,0:T(8,128)(2,1)}), bf16[8,16,256]{2,1,0:T(8,128)(2,1)S(1)}, u32[]{:S(2)}, u32[]{:S(2)}) %all-to-all-start.6) | async-done | bytes 65568 | tf_op jit(solution)/shard_map/all_to_all | solution.py:52
  129.6 5.7 %all-to-all-start.7 = ((bf16[8,16,256]{2,1,0:T(8,128)(2,1)}), bf16[8,16,256]{2,1,0:T(8,128)(2,1)S(1)}, u32[]{:S(2)}, u32[]{:S(2)}) async-start(bf16[8,16,256]{2,1,0:T(8,128)(2,1)} %get-tuple-element.49), calls=%async_computation.7 | async-start | bytes 131072 | tf_op jit(solution)/shard_map/all_to_all | solution.py:60
  135.3 4.8 %all-to-all-done.7.back = bf16[8,16,256]{2,1,0:T(8,128)(2,1)S(1)} async-done(((bf16[8,16,256]{2,1,0:T(8,128)(2,1)}), bf16[8,16,256]{2,1,0:T(8,128)(2,1)S(1)}, u32[]{:S(2)}, u32[]{:S(2)}) %all-to-all-start.7) | async-done | bytes 65568 | tf_op jit(solution)/shard_map/all_to_all | solution.py:60
  140.8 3.5 %all-to-all-start.8 = ((bf16[8,16,256]{2,1,0:T(8,128)(2,1)}), bf16[8,16,256]{2,1,0:T(8,128)(2,1)S(1)}, u32[]{:S(2)}, u32[]{:S(2)}) async-start(bf16[8,16,256]{2,1,0:T(8,128)(2,1)} %share_last.1), calls=%async_computation.8 | async-start | bytes 131072 | tf_op jit(solution)/shard_map/all_to_all | solution.py:52
  153.5 5.3 %all-to-all-start.9 = ((bf16[8,80,256]{2,1,0:T(8,128)(2,1)}), bf16[8,80,256]{2,1,0:T(8,128)(2,1)S(1)}, u32[]{:S(2)}, u32[]{:S(2)}) async-start(bf16[8,80,256]{2,1,0:T(8,128)(2,1)} %get-tuple-element.60), calls=%async_computation.9 | async-start | bytes 655360 | tf_op jit(solution)/shard_map/all_to_all | solution.py:60
  161.7 4.2 %all-to-all-done.9.refs_0_ = bf16[8,80,256]{2,1,0:T(8,128)(2,1)S(1)} async-done(((bf16[8,80,256]{2,1,0:T(8,128)(2,1)}), bf16[8,80,256]{2,1,0:T(8,128)(2,1)S(1)}, u32[]{:S(2)}, u32[]{:S(2)}) %all-to-all-start.9) | async-done | bytes 327712 | tf_op jit(solution)/shard_map/all_to_all | solution.py:60
  168.1 4.4 %all-to-all-start.10 = ((bf16[8,16,256]{2,1,0:T(8,128)(2,1)}), bf16[8,16,256]{2,1,0:T(8,128)(2,1)S(1)}, u32[]{:S(2)}, u32[]{:S(2)}) async-start(bf16[8,16,256]{2,1,0:T(8,128)(2,1)} %copy-done), calls=%async_computation.10 | async-start | bytes 131072 | tf_op jit(solution)/shard_map/all_to_all | solution.py:60
  173.8 5.5 %gather_fusion.1 = f32[2048,64]{1,0:T(8,128)S(1)} fusion(f32[64,2048]{0,1:T(8,128)S(1)} %copy.27, s32[2048]{0:T(1024)S(1)} %fusion.14), kind=kCustom, calls=%fused_computation.1 | custom fusion | bytes 1056768 | tf_op jit(solution)/shard_map/jit(_take)/gather | solution.py:445
  180.7 7.3 %all-to-all-start.11 = ((bf16[32,2,256]{2,1,0:T(2,128)(2,1)}), bf16[32,2,256]{2,1,0:T(2,128)(2,1)S(1)}, u32[]{:S(2)}, u32[]{:S(2)}) async-start(bf16[32,2,256]{2,1,0:T(2,128)(2,1)} %reshape.209), calls=%async_computation.11 | async-start | bytes 65536 | tf_op jit(solution)/shard_map/all_to_all | solution.py:56
  192.3 3.1 %collective-permute-done.13 = bf16[2,64,256]{2,1,0:T(8,128)(2,1)S(1)} collective-permute-done((bf16[2,64,256]{2,1,0:T(8,128)(2,1)S(1)}, bf16[2,64,256]{2,1,0:T(8,128)(2,1)S(1)}, u32[]{:S(2)}, u32[]{:S(2)}) %collective-permute-start.13) | collective-permute-done | bytes 65568 | tf_op jit(solution)/shard_map/ppermute | solution.py:41
  (171 shorter events, 57.8 us)
Async XLA Ops:
  7.2 141.3 %all-gather.3.cloned.1.call-start = ((), (), s32[]{:S(2)}) async-start(), calls=%async_computation.12 | async-start | bytes 10813440 | tf_op jit(solution)/shard_map/all_gather | solution.py:318
  14.1 10.9 %all-to-all-start = ((bf16[4,160,256]{2,1,0:T(8,128)(2,1)}), bf16[4,160,256]{2,1,0:T(8,128)(2,1)S(1)}, u32[]{:S(2)}, u32[]{:S(2)}) async-start(bf16[4,160,256]{2,1,0:T(8,128)(2,1)} %pad_maximum_fusion.3), calls=%async_computation | async-start | bytes 655360 | tf_op jit(solution)/shard_map/all_to_all | solution.py:33
  26.5 31.7 %all-to-all-start.1 = ((bf16[8,144,256]{2,1,0:T(8,128)(2,1)}), bf16[8,144,256]{2,1,0:T(8,128)(2,1)S(1)}, u32[]{:S(2)}, u32[]{:S(2)}) async-start(bf16[8,144,256]{2,1,0:T(8,128)(2,1)} %get-tuple-element.39), calls=%async_computation.1 | async-start | bytes 1179648 | tf_op jit(solution)/shard_map/all_to_all | solution.py:52
  35.9 13.4 %collective-permute-start = (bf16[512,256]{1,0:T(8,128)(2,1)S(1)}, bf16[512,256]{1,0:T(8,128)(2,1)S(1)}, u32[]{:S(2)}, u32[]{:S(2)}) collective-permute-start(bf16[512,256]{1,0:T(8,128)(2,1)S(1)} %bitcast.79), channel_id=1, source_target_pairs={{0,1},{1,0},{2,3},{3,2},{4,5},{5,4},{6,7},{7,6},{8,9},{9,8},{10,11... | collective-permute-start | bytes 786440 | tf_op jit(solution)/shard_map/ppermute | solution.py:37
  36.3 30.1 %collective-permute-start.1 = (bf16[512,256]{1,0:T(8,128)(2,1)S(1)}, bf16[512,256]{1,0:T(8,128)(2,1)S(1)}, u32[]{:S(2)}, u32[]{:S(2)}) collective-permute-start(bf16[512,256]{1,0:T(8,128)(2,1)S(1)} %bitcast.80), channel_id=1, source_target_pairs={{0,2},{1,3},{2,0},{3,1},{4,6},{5,7},{6,4},{7,5},{8,10},{9,11},{10,... | collective-permute-start | bytes 786440 | tf_op jit(solution)/shard_map/ppermute | solution.py:37
  38.1 28.4 %collective-permute-start.2 = (bf16[512,256]{1,0:T(8,128)(2,1)S(1)}, bf16[512,256]{1,0:T(8,128)(2,1)S(1)}, u32[]{:S(2)}, u32[]{:S(2)}) collective-permute-start(bf16[512,256]{1,0:T(8,128)(2,1)S(1)} %bitcast.81), channel_id=1, source_target_pairs={{0,3},{1,2},{2,1},{3,0},{4,7},{5,6},{6,5},{7,4},{8,11},{9,10},{10,... | collective-permute-start | bytes 786440 | tf_op jit(solution)/shard_map/ppermute | solution.py:37
  47.1 15.8 %collective-permute-start.6 = (bf16[48,256]{1,0:T(8,128)(2,1)S(1)}, bf16[48,256]{1,0:T(8,128)(2,1)S(1)}, u32[]{:S(2)}, u32[]{:S(2)}) collective-permute-start(bf16[48,256]{1,0:T(8,128)(2,1)S(1)} %bitcast.106), channel_id=1, source_target_pairs={{0,1},{1,0},{2,3},{3,2},{4,5},{5,4},{6,7},{7,6},{8,9},{9,8},{10,11... | collective-permute-start | bytes 73736 | tf_op jit(solution)/shard_map/ppermute | solution.py:37
  47.2 15.8 %collective-permute-start.7 = (bf16[48,256]{1,0:T(8,128)(2,1)S(1)}, bf16[48,256]{1,0:T(8,128)(2,1)S(1)}, u32[]{:S(2)}, u32[]{:S(2)}) collective-permute-start(bf16[48,256]{1,0:T(8,128)(2,1)S(1)} %bitcast.105), channel_id=1, source_target_pairs={{0,2},{1,3},{2,0},{3,1},{4,6},{5,7},{6,4},{7,5},{8,10},{9,11},{10,... | collective-permute-start | bytes 73736 | tf_op jit(solution)/shard_map/ppermute | solution.py:37
  49.3 17.0 %collective-permute-start.8 = (bf16[48,256]{1,0:T(8,128)(2,1)S(1)}, bf16[48,256]{1,0:T(8,128)(2,1)S(1)}, u32[]{:S(2)}, u32[]{:S(2)}) collective-permute-start(bf16[48,256]{1,0:T(8,128)(2,1)S(1)} %bitcast.104), channel_id=1, source_target_pairs={{0,3},{1,2},{2,1},{3,0},{4,7},{5,6},{6,5},{7,4},{8,11},{9,10},{10,... | collective-permute-start | bytes 73736 | tf_op jit(solution)/shard_map/ppermute | solution.py:37
  59.5 10.5 %all-to-all-start.2 = ((bf16[8,16,256]{2,1,0:T(8,128)(2,1)}), bf16[8,16,256]{2,1,0:T(8,128)(2,1)S(1)}, u32[]{:S(2)}, u32[]{:S(2)}) async-start(bf16[8,16,256]{2,1,0:T(8,128)(2,1)} %get-tuple-element.40), calls=%async_computation.2 | async-start | bytes 131072 | tf_op jit(solution)/shard_map/all_to_all | solution.py:52
  62.9 15.7 %collective-permute-start.4 = (bf16[4,64,256]{2,1,0:T(8,128)(2,1)S(1)}, bf16[4,64,256]{2,1,0:T(8,128)(2,1)S(1)}, u32[]{:S(2)}, u32[]{:S(2)}) collective-permute-start(bf16[4,64,256]{2,1,0:T(8,128)(2,1)S(1)} %get-tuple-element.43), channel_id=1, source_target_pairs={{0,2},{1,3},{2,0},{3,1},{4,6},{5,7},{6,4},{7,5},{8,10},{9,11},{10,... | collective-permute-start | bytes 393224 | tf_op jit(solution)/shard_map/ppermute | solution.py:37
  63.0 15.6 %collective-permute-start.5 = (bf16[4,64,256]{2,1,0:T(8,128)(2,1)S(1)}, bf16[4,64,256]{2,1,0:T(8,128)(2,1)S(1)}, u32[]{:S(2)}, u32[]{:S(2)}) collective-permute-start(bf16[4,64,256]{2,1,0:T(8,128)(2,1)S(1)} %get-tuple-element.43), channel_id=1, source_target_pairs={{0,3},{1,2},{2,1},{3,0},{4,7},{5,6},{6,5},{7,4},{8,11},{9,10},{10,... | collective-permute-start | bytes 393224 | tf_op jit(solution)/shard_map/ppermute | solution.py:37
  66.3 12.3 %collective-permute-start.3 = (bf16[4,64,256]{2,1,0:T(8,128)(2,1)S(1)}, bf16[4,64,256]{2,1,0:T(8,128)(2,1)S(1)}, u32[]{:S(2)}, u32[]{:S(2)}) collective-permute-start(bf16[4,64,256]{2,1,0:T(8,128)(2,1)S(1)} %get-tuple-element.43), channel_id=1, source_target_pairs={{0,1},{1,0},{2,3},{3,2},{4,5},{5,4},{6,7},{7,6},{8,9},{9,8},{10,11... | collective-permute-start | bytes 393224 | tf_op jit(solution)/shard_map/ppermute | solution.py:37
  70.9 14.1 %all-to-all-start.3 = ((bf16[8,64,256]{2,1,0:T(8,128)(2,1)}), bf16[8,64,256]{2,1,0:T(8,128)(2,1)S(1)}, u32[]{:S(2)}, u32[]{:S(2)}) async-start(bf16[8,64,256]{2,1,0:T(8,128)(2,1)} %get-tuple-element.41), calls=%async_computation.3 | async-start | bytes 524288 | tf_op jit(solution)/shard_map/all_to_all | solution.py:60
  86.5 13.5 %all-to-all-start.4 = ((bf16[8,48,256]{2,1,0:T(8,128)(2,1)}), bf16[8,48,256]{2,1,0:T(8,128)(2,1)S(1)}, u32[]{:S(2)}, u32[]{:S(2)}) async-start(bf16[8,48,256]{2,1,0:T(8,128)(2,1)} %get-tuple-element.45), calls=%async_computation.4 | async-start | bytes 393216 | tf_op jit(solution)/shard_map/all_to_all | solution.py:52
  100.9 13.2 %all-to-all-start.5 = ((bf16[8,64,256]{2,1,0:T(8,128)(2,1)}), bf16[8,64,256]{2,1,0:T(8,128)(2,1)S(1)}, u32[]{:S(2)}, u32[]{:S(2)}) async-start(bf16[8,64,256]{2,1,0:T(8,128)(2,1)} %get-tuple-element.46), calls=%async_computation.5 | async-start | bytes 524288 | tf_op jit(solution)/shard_map/all_to_all | solution.py:60
  115.5 11.2 %all-to-all-start.6 = ((bf16[8,16,256]{2,1,0:T(8,128)(2,1)}), bf16[8,16,256]{2,1,0:T(8,128)(2,1)S(1)}, u32[]{:S(2)}, u32[]{:S(2)}) async-start(bf16[8,16,256]{2,1,0:T(8,128)(2,1)} %next_state_1.1), calls=%async_computation.6 | async-start | bytes 131072 | tf_op jit(solution)/shard_map/all_to_all | solution.py:52
  127.4 7.9 %collective-permute-start.9 = (bf16[48,256]{1,0:T(8,128)(2,1)S(1)}, bf16[48,256]{1,0:T(8,128)(2,1)S(1)}, u32[]{:S(2)}, u32[]{:S(2)}) collective-permute-start(bf16[48,256]{1,0:T(8,128)(2,1)S(1)} %constant_dynamic-update-slice_fusion), channel_id=1, source_target_pairs={{0,1},{1,0},{2,3},{3,2},{4,5},{5,4},{6,7},{7,6},{8,9},{9,8},{10,11... | collective-permute-start | bytes 73736 | tf_op jit(solution)/shard_map/ppermute | solution.py:37
  129.6 10.6 %all-to-all-start.7 = ((bf16[8,16,256]{2,1,0:T(8,128)(2,1)}), bf16[8,16,256]{2,1,0:T(8,128)(2,1)S(1)}, u32[]{:S(2)}, u32[]{:S(2)}) async-start(bf16[8,16,256]{2,1,0:T(8,128)(2,1)} %get-tuple-element.49), calls=%async_computation.7 | async-start | bytes 131072 | tf_op jit(solution)/shard_map/all_to_all | solution.py:60
  140.8 10.6 %all-to-all-start.8 = ((bf16[8,16,256]{2,1,0:T(8,128)(2,1)}), bf16[8,16,256]{2,1,0:T(8,128)(2,1)S(1)}, u32[]{:S(2)}, u32[]{:S(2)}) async-start(bf16[8,16,256]{2,1,0:T(8,128)(2,1)} %share_last.1), calls=%async_computation.8 | async-start | bytes 131072 | tf_op jit(solution)/shard_map/all_to_all | solution.py:52
  153.5 12.4 %all-to-all-start.9 = ((bf16[8,80,256]{2,1,0:T(8,128)(2,1)}), bf16[8,80,256]{2,1,0:T(8,128)(2,1)S(1)}, u32[]{:S(2)}, u32[]{:S(2)}) async-start(bf16[8,80,256]{2,1,0:T(8,128)(2,1)} %get-tuple-element.60), calls=%async_computation.9 | async-start | bytes 655360 | tf_op jit(solution)/shard_map/all_to_all | solution.py:60
  168.1 11.6 %all-to-all-start.10 = ((bf16[8,16,256]{2,1,0:T(8,128)(2,1)}), bf16[8,16,256]{2,1,0:T(8,128)(2,1)S(1)}, u32[]{:S(2)}, u32[]{:S(2)}) async-start(bf16[8,16,256]{2,1,0:T(8,128)(2,1)} %copy-done), calls=%async_computation.10 | async-start | bytes 131072 | tf_op jit(solution)/shard_map/all_to_all | solution.py:60
  180.6 7.5 %collective-permute-start.11 = (bf16[64,256]{1,0:T(8,128)(2,1)S(1)}, bf16[64,256]{1,0:T(8,128)(2,1)S(1)}, u32[]{:S(2)}, u32[]{:S(2)}) collective-permute-start(bf16[64,256]{1,0:T(8,128)(2,1)S(1)} %get-tuple-element.69), channel_id=1, source_target_pairs={{0,32},{32,0},{64,96},{96,64},{128,160},{160,128},{192,224},{224,1... | collective-permute-start | bytes 98312 | tf_op jit(solution)/shard_map/ppermute | solution.py:41
  180.7 17.4 %all-to-all-start.11 = ((bf16[32,2,256]{2,1,0:T(2,128)(2,1)}), bf16[32,2,256]{2,1,0:T(2,128)(2,1)S(1)}, u32[]{:S(2)}, u32[]{:S(2)}) async-start(bf16[32,2,256]{2,1,0:T(2,128)(2,1)} %reshape.209), calls=%async_computation.11 | async-start | bytes 65536 | tf_op jit(solution)/shard_map/all_to_all | solution.py:56
  (15 other events, 226.6 us)
Sparse Core Ops, SparseCore 0:
  11.2 124.2 all-gather.2
